TPU v7x, 256 devices: a whole 4x4x8 slice. The times are simulated.
256 devices in a mesh: row: 8 (over z), col: 32 (over x, y, core).
Axes of the slice: x: 4, y: 4, z: 8, core: 2. Of those that a mesh axis runs over, the one named last changes fastest.
Arguments:
- image_embeds: bfloat16 [16384, 1280], P(('row', 'col')), as said below
- text_embeds: bfloat16 [16384, 1280], P(('row', 'col'))
- labels: int32 [16384], P('row'), may hold values from 0 to 16383, as said below
Outputs:
- image_grad: bfloat16 [16384, 1280], P(('row', 'col'))
- text_grad: bfloat16 [16384, 1280], P(('row', 'col'))
Inputs may be any that keep to these rules, and one draw needn't show every extreme that they name: `image_embeds`: entries of both embedding arrays lie within -18 to 18. labels is a permutation: each text is the match of exactly one image.
All inputs are finite; a program needn't handle non-finite values.
Results may differ from a plain program's by a relative error of at most 0.0045.
Values may be sent and summed in bfloat16 or wider, within the bound.
No kernel may reach another device: no remote copies, remote signals or barrier semaphores. Data moves between devices by JAX's collectives and lax.ppermute only.
A program may use at most 64 MiB of HBM per device.

v0:
```python
import jax
import jax.numpy as jnp
from jax import lax
from jax.sharding import PartitionSpec as P

score_scale = 0.1


def shards(image_embeds, text_embeds, labels):
    own_rows = text_embeds.shape[0]
    images = lax.all_gather(image_embeds, "col", axis=0, tiled=True)
    texts = lax.all_gather(text_embeds, "row", axis=0, tiled=True)
    col_count = texts.shape[0]
    scores = score_scale * jnp.dot(images, texts.T, preferred_element_type=jnp.float32)
    row_top = jnp.max(scores, axis=1)
    col_top = jnp.max(scores, axis=0)
    row_top = lax.pmax(row_top, "col")
    row_total = lax.psum(jnp.sum(jnp.exp(scores - row_top[:, None]), axis=1), "col")
    col_top = lax.pmax(col_top, "row")
    col_total = lax.psum(jnp.sum(jnp.exp(scores - col_top[None, :]), axis=0), "row")
    row_lse = row_top + jnp.log(row_total)
    col_lse = col_top + jnp.log(col_total)
    local_index = jnp.arange(col_count, dtype=jnp.int32)
    positions = (
        local_index // own_rows * (own_rows * lax.axis_size("col"))
        + lax.axis_index("col") * own_rows
        + local_index % own_rows
    )
    match = (labels[:, None] == positions[None, :]).astype(jnp.float32)
    dscores = (
        jnp.exp(scores - row_lse[:, None]) + jnp.exp(scores - col_lse[None, :]) - 2.0 * match
    ).astype(jnp.bfloat16)
    image_term = jnp.dot(dscores, texts, preferred_element_type=jnp.float32)
    image_total = lax.psum_scatter(image_term, "col", scatter_dimension=0, tiled=True)
    image_grad = (score_scale * image_total).astype(jnp.bfloat16)
    text_term = lax.dot_general(
        dscores, images, (((0,), (0,)), ((), ())), preferred_element_type=jnp.float32
    )
    text_total = lax.psum_scatter(text_term, "row", scatter_dimension=0, tiled=True)
    text_grad = (score_scale * text_total).astype(jnp.bfloat16)
    return (image_grad, text_grad)


def solution(mesh):
    in_specs = (P(("row", "col"), None), P(("row", "col"), None), P("row"))
    out_specs = (P(("row", "col"), None), P(("row", "col"), None))
    return jax.shard_map(shards, mesh=mesh, in_specs=in_specs, out_specs=out_specs, check_vma=False)
```

profile of v0, /device:TPU:32, one launch (start us, length us, event | category | flops | bytes accessed | tf_op | source)
XLA Modules:
  0.0 443.3 jit_solution(16102203768252579979)
XLA Ops:
  7.2 0.0 all-gather.5.cloned.1.call-start
  7.2 0.7 all-gather.5.cloned.1.call-update
  7.9 0.0 all-gather.3.cloned.1.call-start
  7.9 0.7 all-gather.3.cloned.1.call-update
  8.6 0.0 reduce-scatter.5.cloned.1.call-start
  8.7 42.5 %all-gather.5.cloned.1.call-done = bf16[512,1280]{1,0:T(8,128)(2,1)} async-done(((bf16[64,1280]{1,0:T(8,128)(2,1)}), bf16[512,1280]{1,0:T(8,128)(2,1)}) %all-gather.5.cloned.1.call-update) | async-done | bytes 1310736 | tf_op jit(solution)/shard_map/all_gather | solution.py:12
  51.2 54.2 %all-gather.3.cloned.1.call-done = bf16[2048,1280]{1,0:T(8,128)(2,1)} async-done(((bf16[64,1280]{1,0:T(8,128)(2,1)}), bf16[2048,1280]{1,0:T(8,128)(2,1)}) %all-gather.3.cloned.1.call-update) | async-done | bytes 5242896 | tf_op jit(solution)/shard_map/all_gather | solution.py:11
  105.4 7.9 %fusion.12 = (f32[2048]{0:T(1024)S(1)}, f32[512]{0:T(512)S(1)}, f32[2048,512]{1,0:T(8,128)}) fusion(bf16[2048,1280]{1,0:T(8,128)(2,1)} %all-gather.3.cloned.1.call-done, bf16[512,1280]{1,0:T(8,128)(2,1)} %all-gather.5.cloned.1.call-done), kind=kOutput, calls=%fused_computation.24 | convolution fusion | flops 2687497728 | bytes 10758144 | tf_op jit(solution)/shard_map/dot_general | solution.py:14
  113.3 66.2 %pmax.14 = f32[2048]{0:T(1024)S(1)} all-reduce(f32[2048]{0:T(1024)S(1)} %get-tuple-element.4), channel_id=1, replica_groups=mesh['row'=8,'col'=32] {'col'}, use_global_device_ids=true, to_apply=%region_1.0 | all-reduce | flops 2048 | bytes 16384 | tf_op jit(solution)/shard_map/pmax | solution.py:17
  179.5 16.1 %pmax.15 = f32[512]{0:T(512)S(1)} all-reduce(f32[512]{0:T(512)S(1)} %get-tuple-element.5), channel_id=1, replica_groups=mesh['row'=8,'col'=32] {'row'}, use_global_device_ids=true, to_apply=%region_5.0 | all-reduce | flops 512 | bytes 4096 | tf_op jit(solution)/shard_map/pmax | solution.py:19
  195.6 3.1 exponential_reduce_fusion.1
  198.7 63.7 %psum.14 = f32[2048]{0:T(1024)S(1)} all-reduce(f32[2048]{0:T(1024)S(1)} %get-tuple-element.2), channel_id=1, replica_groups=mesh['row'=8,'col'=32] {'col'}, use_global_device_ids=true, to_apply=%region_3.0 | all-reduce | flops 2048 | bytes 16384 | tf_op jit(solution)/shard_map/psum | solution.py:18
  262.5 16.0 %psum.15 = f32[512]{0:T(512)S(1)} all-reduce(f32[512]{0:T(512)S(1)} %get-tuple-element.3), channel_id=1, replica_groups=mesh['row'=8,'col'=32] {'row'}, use_global_device_ids=true, to_apply=%region_7.0 | all-reduce | flops 512 | bytes 4096 | tf_op jit(solution)/shard_map/psum | solution.py:20
  278.5 0.0 copy-done.1
  278.5 8.7 %fusion.10 = f32[512,1280]{1,0:T(8,128)} fusion(bf16[2048,1280]{1,0:T(8,128)(2,1)} %all-gather.3.cloned.1.call-done, f32[2048,512]{1,0:T(8,128)} %get-tuple-element.6, s32[512]{0:T(512)S(1)} %fusion.6, f32[512]{0:T(512)S(1)} %log_add_fusion.1, f32[2048]{0:T(1024)S(1)} %log_add_fusion, s32[2048]{0:T(1024)S(1)} %copy-done.1), kind=kOutput, calls=%fused_computation.22 | convolution fusion | flops 2691694592 | bytes 12079104 | tf_op jit(solution)/shard_map/dot_general | solution.py:36
  287.2 0.0 reduce-scatter.5.cloned.1.call-update
  287.2 0.0 reduce-scatter.3.cloned.1.call-start
  287.3 0.0 copy-done
  287.3 8.0 %fusion.11 = f32[2048,1280]{1,0:T(8,128)} fusion(bf16[512,1280]{1,0:T(8,128)(2,1)S(1)} %copy-done, f32[2048,512]{1,0:T(8,128)} %get-tuple-element.6, s32[512]{0:T(512)S(1)} %fusion.6, f32[512]{0:T(512)S(1)} %log_add_fusion.1, f32[2048]{0:T(1024)S(1)} %log_add_fusion, s32[2048]{0:T(1024)S(1)} %copy-done.1), kind=kOutput, calls=%fused_computation.23 | convolution fusion | flops 2691694592 | bytes 16011264 | tf_op jit(solution)/shard_map/dot_general | solution.py:33
  295.3 0.0 reduce-scatter.3.cloned.1.call-update
  295.3 30.0 %reduce-scatter.5.cloned.1.call-done = f32[64,1280]{1,0:T(8,128)} async-done(((f32[512,1280]{1,0:T(8,128)}), f32[64,1280]{1,0:T(8,128)}) %reduce-scatter.5.cloned.1.call-update) | async-done | bytes 327696 | tf_op jit(solution)/shard_map/reduce_scatter | solution.py:39
  325.4 1.7 multiply_convert_fusion
  327.0 108.1 %reduce-scatter.3.cloned.1.call-done = f32[64,1280]{1,0:T(8,128)} async-done(((f32[2048,1280]{1,0:T(8,128)}), f32[64,1280]{1,0:T(8,128)}) %reduce-scatter.3.cloned.1.call-update) | async-done | bytes 327696 | tf_op jit(solution)/shard_map/reduce_scatter | solution.py:34
  435.1 1.7 multiply_convert_fusion.1
  (5 shorter events, 0.0 us)
Async XLA Ops:
  7.2 44.0 %all-gather.5.cloned.1.call-start = ((), (), s32[]{:S(2)}) async-start(), calls=%async_computation.3 | async-start | bytes 1474560 | tf_op jit(solution)/shard_map/all_gather | solution.py:12
  7.9 97.5 %all-gather.3.cloned.1.call-start = ((), (), s32[]{:S(2)}) async-start(), calls=%async_computation.2 | async-start | bytes 5406720 | tf_op jit(solution)/shard_map/all_gather | solution.py:11
  8.6 316.7 %reduce-scatter.5.cloned.1.call-start = ((), (), s32[]{:S(2)}) async-start(), calls=%async_computation.5 | async-start | bytes 2949120 | tf_op jit(solution)/shard_map/reduce_scatter | solution.py:39
  113.3 165.2 %copy-start.1 = (s32[2048]{0:T(1024)S(1)}, s32[2048]{0:T(1024)}, u32[]{:S(2)}) copy-start(s32[2048]{0:T(1024)} %param.5) | copy-start | bytes 24580
  278.5 8.8 %copy-start = (bf16[512,1280]{1,0:T(8,128)(2,1)S(1)}, bf16[512,1280]{1,0:T(8,128)(2,1)}, u32[]{:S(2)}) copy-start(bf16[512,1280]{1,0:T(8,128)(2,1)} %all-gather.5.cloned.1.call-done) | copy-start | bytes 3932164
  287.2 147.9 %reduce-scatter.3.cloned.1.call-start = ((), (), s32[]{:S(2)}) async-start(), calls=%async_computation.4 | async-start | bytes 10813440 | tf_op jit(solution)/shard_map/reduce_scatter | solution.py:34
Sparse Core Ops, SparseCore 0:
  9.8 41.3 all-gather.4
  53.8 51.5 all-gather.2
  287.4 37.9 reduce-scatter.4
  329.3 105.8 reduce-scatter.2
where the time goes:
time: 444 us; the launch traced here: 443 us
  waiting for transfers between devices  236 us (53%)
  blocking collectives  162 us (36%)
  matrix products  24.6 us (6%)
  between operations  13.8 us (3%)
  other arithmetic  6.5 us (1%)
    reduce_scatter x1, waiting for transfers between devices, shards(): lax.psum_scatter(image_term, 'col', scatter_dimension=0, tiled=True)  108 us
    pmax x1, blocking collectives, shards(): row_top = lax.pmax(row_top, 'col')  66.2 us
    psum x1, blocking collectives, shards(): lax.psum(jnp.sum(jnp.exp(scores - row_top[:, None]), axis=1), 'col')  63.7 us
    all_gather x1, waiting for transfers between devices, shards(): images = lax.all_gather(image_embeds, 'col', axis=0, tiled=True)  54.2 us
    all_gather x1, waiting for transfers between devices, shards(): texts = lax.all_gather(text_embeds, 'row', axis=0, tiled=True)  42.5 us
    reduce_scatter x1, waiting for transfers between devices, shards(): lax.psum_scatter(text_term, 'row', scatter_dimension=0, tiled=True)  30 us
    pmax x1, blocking collectives, shards(): col_top = lax.pmax(col_top, 'row')  16.1 us
    psum x1, blocking collectives, shards(): lax.psum(jnp.sum(jnp.exp(scores - col_top[None, :]), axis=0), 'row')  16 us
  transfers between devices with their start and end apart: 4, of which 4 were waited for; matrix products, arithmetic and copies ran while one was open for 2% of the time, Pallas kernels for 0%

commit v1 on v0

v1 whole, which is shorter than its diff:
```python
import functools

import jax
import jax.numpy as jnp
from jax import lax
from jax.experimental import pallas as pl
from jax.experimental.pallas import tpu as pltpu
from jax.sharding import Mesh, PartitionSpec as P

score_scale = 0.1
lanes = 128
row_block = 256
vmem_bytes = 32 * 1024 * 1024
every = ("z", "x", "y", "core")
swap = [(0, 1), (1, 0)]


def statistics_groups():
    def device(z, x, y, core):
        return ((z * 4 + x) * 4 + y) * 2 + core

    columns = [
        [device(z, x + odd, y, 0) for odd in range(2) for z in range(8)] for x in (0, 2) for y in range(4)
    ]
    rows = [[device(z, x, y, 1) for x in range(4) for y in range(4)] for z in range(8)]
    return columns + rows


def scores_kernel(core, images, texts, scores, kept, sent, col_top, col_sum, rows_out):
    step = pl.program_id(0)
    s = score_scale * lax.dot_general(
        images[...], texts[...], (((1,), (1,)), ((), ())), preferred_element_type=jnp.float32
    )
    scores[...] = s
    top = jnp.max(s, axis=1, keepdims=True)
    row = top + jnp.log(jnp.sum(jnp.exp(s - top), axis=1, keepdims=True))
    row = jnp.broadcast_to(row, (s.shape[0], lanes)).T
    per_step = s.shape[0] // lanes
    for i in range(per_step):
        rows_out[pl.ds(step * per_step + i, 1), :] = row[:1, i * lanes : (i + 1) * lanes]

    @pl.when(step == 0)
    def _():
        col_top[...] = jnp.full(col_top.shape, -jnp.inf, jnp.float32)
        col_sum[...] = jnp.zeros(col_sum.shape, jnp.float32)

    old = col_top[...]
    new = jnp.maximum(old, jnp.max(s, axis=0, keepdims=True))
    total = col_sum[...] * jnp.exp(old - new) + jnp.sum(jnp.exp(s - new), axis=0, keepdims=True)
    col_top[...] = new
    col_sum[...] = total

    @pl.when(step == pl.num_programs(0) - 1)
    def _():
        col = new + jnp.log(total)
        first = core[0] == 0
        for i in range(kept.shape[0]):
            col_here = col[:, i * lanes : (i + 1) * lanes]
            row_here = rows_out[i : i + 1, :]
            kept[i : i + 1, :] = jnp.where(first, col_here, row_here)
            sent[i : i + 1, :] = jnp.where(first, row_here, col_here)


def local_scores(core, images, texts):
    rows, width = images.shape
    cols = texts.shape[0]
    steps = rows // row_block
    tile = (rows // lanes, lanes)
    return pl.pallas_call(
        scores_kernel,
        grid_spec=pltpu.PrefetchScalarGridSpec(
            num_scalar_prefetch=1,
            grid=(steps,),
            in_specs=[
                pl.BlockSpec((row_block, width), lambda i, c: (i, 0)),
                pl.BlockSpec((cols, width), lambda i, c: (0, 0)),
            ],
            out_specs=[
                pl.BlockSpec((row_block, cols), lambda i, c: (i, 0)),
                pl.BlockSpec(tile, lambda i, c: (0, 0)),
                pl.BlockSpec(tile, lambda i, c: (0, 0)),
            ],
            scratch_shapes=[
                pltpu.VMEM((1, cols), jnp.float32),
                pltpu.VMEM((1, cols), jnp.float32),
                pltpu.VMEM(tile, jnp.float32),
            ],
        ),
        out_shape=[
            jax.ShapeDtypeStruct((rows, cols), jnp.float32),
            jax.ShapeDtypeStruct(tile, jnp.float32),
            jax.ShapeDtypeStruct(tile, jnp.float32),
        ],
        compiler_params=pltpu.CompilerParams(vmem_limit_bytes=vmem_bytes),
        cost_estimate=pl.CostEstimate(
            flops=2 * rows * cols * width, bytes_accessed=10_000_000, transcendentals=2 * rows * cols
        ),
        name="scores",
    )(core, images, texts)


def merge_kernel(place, parts, kept, sent):
    def total(pieces):
        top = pieces[0]
        for piece in pieces[1:]:
            top = jnp.maximum(top, piece)
        sums = jnp.exp(pieces[0] - top)
        for piece in pieces[1:]:
            sums = sums + jnp.exp(piece - top)
        return top + jnp.log(sums)

    @pl.when(place[0] == 0)
    def _():
        first = place[1] * 8
        col = total([parts[first + z, core] for z in range(8) for core in range(2)])
        kept[...] = col
        sent[...] = col

    @pl.when(place[0] == 1)
    def _():
        sent[...] = total([parts[i, 0] for i in range(16)])
        kept[...] = total([parts[i, 1] for i in range(16)])


def merge(place, parts):
    tile = parts.shape[2:]
    return pl.pallas_call(
        merge_kernel,
        grid_spec=pltpu.PrefetchScalarGridSpec(
            num_scalar_prefetch=1,
            grid=(1,),
            in_specs=[pl.BlockSpec(parts.shape, lambda i, p: (0, 0, 0, 0))],
            out_specs=[pl.BlockSpec(tile, lambda i, p: (0, 0))] * 2,
        ),
        out_shape=[jax.ShapeDtypeStruct(tile, jnp.float32)] * 2,
        compiler_params=pltpu.CompilerParams(vmem_limit_bytes=vmem_bytes),
        name="merge",
    )(place, parts)


def dscores_kernel(core, scores, kept, received, targets, images, dscores, own, other, total):
    step = pl.program_id(0)
    rows, cols = scores.shape
    first = core[0] == 0
    per_step = rows // lanes
    col_lse = jnp.where(first, kept[...], received[...])
    here = pl.ds(step * per_step, per_step)
    row_here = jnp.where(first, received[here, :], kept[here, :])
    row_lse = jnp.concatenate(
        [jnp.broadcast_to(row_here[i : i + 1], (lanes, lanes)).T for i in range(per_step)], axis=0
    )
    target = targets[...]
    lane = lax.broadcasted_iota(jnp.int32, (rows, lanes), 1)
    for chunk in range(cols // lanes):
        part = slice(chunk * lanes, (chunk + 1) * lanes)
        s = scores[:, part]
        match = jnp.where(target == lane + chunk * lanes, 2.0, 0.0)
        dscores[:, part] = (
            jnp.exp(s - row_lse) + jnp.exp(s - col_lse[chunk : chunk + 1]) - match
        ).astype(jnp.bfloat16)

    @pl.when(step == 0)
    def _():
        total[...] = jnp.zeros(total.shape, jnp.float32)

    total[...] += lax.dot_general(
        dscores[...], images[...], (((0,), (0,)), ((), ())), preferred_element_type=jnp.float32
    )

    @pl.when(step == pl.num_programs(0) - 1)
    def _():
        piece = own.shape[0] // 8
        for z in range(8):
            rows_here = slice(z * piece, (z + 1) * piece)
            mine = pl.multiple_of((2 * z + core[0]) * piece, piece)
            theirs = pl.multiple_of((2 * z + 1 - core[0]) * piece, piece)
            own[rows_here] = total[pl.ds(mine, piece), :]
            other[rows_here] = total[pl.ds(theirs, piece), :].astype(jnp.bfloat16)


def local_dscores(core, scores, kept, received, targets, images):
    rows, cols = scores.shape
    width = images.shape[1]
    steps = rows // row_block
    return pl.pallas_call(
        dscores_kernel,
        grid_spec=pltpu.PrefetchScalarGridSpec(
            num_scalar_prefetch=1,
            grid=(steps,),
            in_specs=[
                pl.BlockSpec((row_block, cols), lambda i, c: (i, 0)),
                pl.BlockSpec(kept.shape, lambda i, c: (0, 0)),
                pl.BlockSpec(kept.shape, lambda i, c: (0, 0)),
                pl.BlockSpec((row_block, lanes), lambda i, c: (i, 0)),
                pl.BlockSpec((row_block, width), lambda i, c: (i, 0)),
            ],
            out_specs=[
                pl.BlockSpec((row_block, cols), lambda i, c: (i, 0)),
                pl.BlockSpec((cols // 2, width), lambda i, c: (0, 0)),
                pl.BlockSpec((cols // 2, width), lambda i, c: (0, 0)),
            ],
            scratch_shapes=[pltpu.VMEM((cols, width), jnp.float32)],
        ),
        out_shape=[
            jax.ShapeDtypeStruct((rows, cols), jnp.bfloat16),
            jax.ShapeDtypeStruct((cols // 2, width), jnp.float32),
            jax.ShapeDtypeStruct((cols // 2, width), jnp.bfloat16),
        ],
        compiler_params=pltpu.CompilerParams(vmem_limit_bytes=vmem_bytes),
        cost_estimate=pl.CostEstimate(
            flops=2 * rows * cols * width, bytes_accessed=12_000_000, transcendentals=2 * rows * cols
        ),
        name="dscores",
    )(core, scores, kept, received, targets, images)


def product_kernel(left, right, out):
    out[...] = jnp.dot(left[...], right[...], preferred_element_type=jnp.float32).astype(out.dtype)


def product(left, right):
    rows, depth = left.shape
    width = right.shape[1]
    return pl.pallas_call(
        product_kernel,
        grid=(rows // row_block,),
        in_specs=[
            pl.BlockSpec((row_block, depth), lambda i: (i, 0)),
            pl.BlockSpec((depth, width), lambda i: (0, 0)),
        ],
        out_specs=pl.BlockSpec((row_block, width), lambda i: (i, 0)),
        out_shape=jax.ShapeDtypeStruct((rows, width), jnp.bfloat16),
        compiler_params=pltpu.CompilerParams(vmem_limit_bytes=vmem_bytes),
        cost_estimate=pl.CostEstimate(
            flops=2 * rows * depth * width, bytes_accessed=8_000_000, transcendentals=0
        ),
        name="image_product",
    )(left, right)


def shards(image_embeds, text_embeds, labels):
    block, width = image_embeds.shape
    x, y, core = lax.axis_index("x"), lax.axis_index("y"), lax.axis_index("core")
    texts = lax.all_gather(text_embeds, ("z", "core"), axis=0, tiled=True)
    images = lax.all_to_all(
        jnp.broadcast_to(image_embeds, (16, block, width)), ("x", "y"), 0, 0, tiled=True
    ).reshape(16 * block, width)

    mine = lax.dynamic_index_in_dim(labels.reshape(16, 2, block), core, 1, keepdims=False).reshape(-1)
    pair = 2 * block
    plane = 16 * pair
    here = mine % plane // pair == x * 4 + y
    target = jnp.where(here, mine // plane * pair + mine % pair, -1)
    targets = jnp.broadcast_to(target[:, None], (16 * block, lanes))

    scores, kept, sent = local_scores(core.reshape(1), images, texts)
    received = lax.ppermute(sent, "core", swap)
    parts = jnp.stack([jnp.where(core == 0, kept, received), jnp.where(core == 0, received, kept)])
    parts = jnp.broadcast_to(parts, (16, *parts.shape))
    parts = lax.all_to_all(
        parts.reshape(256, lanes), every, 0, 0, axis_index_groups=statistics_groups(), tiled=True
    ).reshape(parts.shape)
    kept, sent = merge(jnp.stack([core, x % 2]), parts)
    received = lax.ppermute(sent, "core", swap)
    dscores, own, other = local_dscores(core.reshape(1), scores, kept, received, targets, images)
    theirs = lax.ppermute(other, "core", swap)
    image_term = product(dscores, texts)
    both = own + theirs.astype(jnp.float32)
    image_term, both = lax.optimization_barrier((image_term, both))
    text_total = lax.psum_scatter(both, "z", scatter_dimension=0, tiled=True)
    image_terms = lax.all_to_all(
        image_term.reshape(16, block, width), ("x", "y"), 0, 0, tiled=True
    )
    image_total = jnp.sum(image_terms.astype(jnp.float32), axis=0)
    image_grad = (score_scale * image_total).astype(jnp.bfloat16)
    text_grad = (score_scale * text_total).astype(jnp.bfloat16)
    return (image_grad, text_grad)


def solution(mesh):
    grid = Mesh(mesh.devices.reshape(8, 4, 4, 2), every)
    split = P(every, None)
    return jax.shard_map(
        shards, mesh=grid, in_specs=(split, split, P("z")), out_specs=(split, split), check_vma=False
    )
```

time: 444 us -> 147 us (0.33)
  waiting for transfers between devices: 236 us -> 47.8 us
  blocking collectives: 162 us -> 38.5 us
  matrix products: 24.6 us -> 0 us
  Pallas kernels: 0 us -> 16 us
  starting transfers between devices: 0.16 us -> 16 us
  local copies, waits for them, and re-layouts: 0.01 us -> 9.59 us
    reduce_scatter x2 -> x1, waiting for transfers between devices: 138 us -> 0.01 us  [shards(): text_total = lax.psum_scatter(both, 'z', scatter_dimension=0, tiled=True)]
    all_gather x2 -> x1, waiting for transfers between devices: 96.7 us -> 0.01 us  [shards(): texts = lax.all_gather(text_embeds, ('z', 'core'), axis=0, tiled=True)]
    pmax x2 -> x0, blocking collectives: 82.3 us -> none  [the longest x1 66.2 us: shards(): row_top = lax.pmax(row_top, 'col')]
    psum x2 -> x0, blocking collectives: 79.7 us -> none  [the longest x1 63.7 us: shards(): lax.psum(jnp.sum(jnp.exp(scores - row_top[:, None]), axis=1), 'col')]
    all_to_all x0 -> x2, waiting for transfers between devices: none -> 44.8 us  [the longest x1 37.1 us: shards(): lax.all_to_all(jnp.broadcast_to(image_embeds, (16, block, width)), ('x',...]
    all_to_all x0 -> x1, blocking collectives: none -> 38.5 us  [shards(): lax.all_to_all(image_term.reshape(16, block, width), ('x', 'y'), 0, 0, ti...]
    dot_general x3 -> x0, matrix products: 24.6 us -> none  [the longest x1 8.73 us: shards(): lax.dot_general(dscores, images, (((0,), (0,)), ((), ())), preferred_elem...]
    pallas_call x0 -> x4, Pallas kernels: none -> 16 us  [the longest x1 6.03 us: local_dscores(): pl.pallas_call(dscores_kernel, grid_spec=pltpu.PrefetchScalarGridSpec(num...]
  transfers between devices with their start and end apart: 4 -> 7, of which waited for: 4 -> 4; matrix products, arithmetic and copies ran while one was open for 2% -> 3% of each run, Pallas kernels for 0% -> 2%
where the time goes in v1:
time: 147 us
  waiting for transfers between devices  47.8 us (33%)
  blocking collectives  38.5 us (26%)
  starting transfers between devices  16 us (11%)
  Pallas kernels  16 us (11%)
  between operations  14.2 us (10%)
  local copies, waits for them, and re-layouts  9.59 us (7%)
  other arithmetic  4.64 us (3%)
    all_to_all x1, blocking collectives, shards(): lax.all_to_all(image_term.reshape(16, block, width), ('x', 'y'), 0, 0, ti...  38.5 us
    all_to_all x1, waiting for transfers between devices, shards(): lax.all_to_all(jnp.broadcast_to(image_embeds, (16, block, width)), ('x',...  37.1 us
    all_to_all x1, starting transfers between devices, shards(): lax.all_to_all(parts.reshape(256, lanes), every, 0, 0, axis_index_groups=...  8.59 us
    all_to_all x1, waiting for transfers between devices, shards(): lax.all_to_all(parts.reshape(256, lanes), every, 0, 0, axis_index_groups=...  7.69 us
    all_to_all x1, starting transfers between devices, shards(): lax.all_to_all(jnp.broadcast_to(image_embeds, (16, block, width)), ('x',...  7.03 us
    pallas_call x1, Pallas kernels, local_dscores(): pl.pallas_call(dscores_kernel, grid_spec=pltpu.PrefetchScalarGridSpec(num...  6.03 us
    pallas_call x1, Pallas kernels, local_scores(): pl.pallas_call(scores_kernel, grid_spec=pltpu.PrefetchScalarGridSpec(num_...  5.89 us
    unnamed x10, local copies, waits for them, and re-layouts  5.87 us
  transfers between devices with their start and end apart: 7, of which 4 were waited for; matrix products, arithmetic and copies ran while one was open for 3% of the time, Pallas kernels for 2%

profile of v1, /device:TPU:32, one launch (start us, length us, event | category | flops | bytes accessed | tf_op | source)
XLA Modules:
  0.0 146.7 jit_solution(10116295956274542772)
XLA Ops:
  7.2 0.7 all-gather.2.cloned.1.call-update
  7.9 2.7 %broadcast_in_dim.16 = bf16[16,64,1280]{2,1,0:T(8,128)(2,1)} broadcast(bf16[64,1280]{1,0:T(8,128)(2,1)} %param.3), dimensions={1,2} | broadcast | bytes 2785280 | tf_op jit(solution)/shard_map/broadcast_in_dim | solution.py:246
  10.6 7.0 %all-to-all-start = ((bf16[16,64,1280]{2,1,0:T(8,128)(2,1)}), bf16[16,64,1280]{2,1,0:T(8,128)(2,1)S(1)}, u32[]{:S(2)}, u32[]{:S(2)}) async-start(bf16[16,64,1280]{2,1,0:T(8,128)(2,1)} %broadcast_in_dim.16), calls=%async_computation | async-start | bytes 5242880 | tf_op jit(solution)/shard_map/all_to_all | solution.py:245
  17.6 37.1 %all-to-all-done = bf16[16,64,1280]{2,1,0:T(8,128)(2,1)S(1)} async-done(((bf16[16,64,1280]{2,1,0:T(8,128)(2,1)}), bf16[16,64,1280]{2,1,0:T(8,128)(2,1)S(1)}, u32[]{:S(2)}, u32[]{:S(2)}) %all-to-all-start) | async-done | bytes 2621472 | tf_op jit(solution)/shard_map/all_to_all | solution.py:245
  54.7 1.7 %copy-done = bf16[1024,1280]{1,0:T(8,128)(2,1)S(1)} copy-done((bf16[1024,1280]{1,0:T(8,128)(2,1)S(1)}, bf16[1024,1280]{1,0:T(8,128)(2,1)}, u32[]{:S(2)}) %copy-start) | copy-done | bytes 2621464
  56.4 5.9 %scores.1 = (f32[1024,1024]{1,0:T(8,128)S(1)}, f32[8,128]{1,0:T(8,128)S(1)}, f32[8,128]{1,0:T(8,128)S(1)}) custom-call(s32[1]{0:T(128)} %bitcast.core, bf16[1024,1280]{1,0:T(8,128)(2,1)S(1)} %bitcast.11, bf16[1024,1280]{1,0:T(8,128)(2,1)S(1)} %copy-done), custom_call_target="tpu_custom_call" | custom-call | flops 2684354560 | bytes 10000000 | tf_op jit(solution)/shard_map/scores/pallas_call | solution.py:69
  62.3 1.9 %copy-done.2 = f32[1024,1024]{1,0:T(8,128)} copy-done((f32[1024,1024]{1,0:T(8,128)}, f32[1024,1024]{1,0:T(8,128)S(1)}, u32[]{:S(2)}) %copy-start.2) | copy-done | bytes 4194328
  64.3 1.2 collective-permute-done
  65.5 0.7 broadcast_in_dim.18
  66.1 8.6 %all-to-all-start.1 = ((f32[16,16,128]{2,1,0:T(8,128)}), f32[16,16,128]{2,1,0:T(8,128)S(1)}, u32[]{:S(2)}, u32[]{:S(2)}) async-start(f32[16,16,128]{2,1,0:T(8,128)} %broadcast_in_dim.18), calls=%async_computation.1 | async-start | bytes 262144 | tf_op jit(solution)/shard_map/all_to_all | solution.py:260
  75.0 7.7 %all-to-all-done.1 = f32[16,16,128]{2,1,0:T(8,128)S(1)} async-done(((f32[16,16,128]{2,1,0:T(8,128)}), f32[16,16,128]{2,1,0:T(8,128)S(1)}, u32[]{:S(2)}, u32[]{:S(2)}) %all-to-all-start.1) | async-done | bytes 131104 | tf_op jit(solution)/shard_map/all_to_all | solution.py:260
  82.7 0.6 merge.1
  83.3 0.1 collective-permute-start.1
  83.4 1.1 collective-permute-done.1.received
  84.6 0.2 broadcast_in_dim.19.targets
  84.8 2.2 %copy-done.3 = f32[1024,1024]{1,0:T(8,128)S(1)} copy-done((f32[1024,1024]{1,0:T(8,128)S(1)}, f32[1024,1024]{1,0:T(8,128)}, u32[]{:S(2)}) %copy-start.3) | copy-done | bytes 4194328
  87.0 6.0 %dscores.1 = (bf16[1024,1024]{1,0:T(8,128)(2,1)S(1)}, f32[512,1280]{1,0:T(8,128)S(1)}, bf16[512,1280]{1,0:T(8,128)(2,1)S(1)}) custom-call(s32[1]{0:T(128)} %bitcast.core, f32[1024,1024]{1,0:T(8,128)S(1)} %copy-done.3, f32[8,128]{1,0:T(8,128)S(1)} %get-tuple-element.15.kept, f32[8,128]{1,0:T(8,128)S(1)} %collective-permute-done.1.received, ...), custom_call_target="tpu_custom_call" | custom-call | flops 2684354560 | bytes 12000000 | tf_op jit(solution)/shard_map/dscores/pallas_call | solution.py:185
  93.0 0.2 collective-permute-start.2
  93.3 3.5 %image_product.1 = bf16[1024,1280]{1,0:T(8,128)(2,1)S(1)} custom-call(bf16[1024,1024]{1,0:T(8,128)(2,1)S(1)} %get-tuple-element.17.left, bf16[1024,1280]{1,0:T(8,128)(2,1)S(1)} %copy-done.1), custom_call_target="tpu_custom_call" | custom-call | flops 2684354560 | bytes 8000000 | tf_op jit(solution)/shard_map/image_product/pallas_call | solution.py:224
  96.7 1.8 %convert_add_fusion = f32[512,1280]{1,0:T(8,128)} fusion(f32[512,1280]{1,0:T(8,128)S(1)} %get-tuple-element.18, bf16[512,1280]{1,0:T(8,128)(2,1)S(1)} %collective-permute-done.2), kind=kLoop, calls=%fused_computation.1 | loop fusion | flops 1310720 | bytes 6553600 | tf_op jit(solution)/shard_map/add | solution.py:268
  98.6 38.5 %all_to_all.16 = bf16[16,64,1280]{2,1,0:T(8,128)(2,1)S(1)} all-to-all(bf16[16,64,1280]{2,1,0:T(8,128)(2,1)S(1)} %bitcast.13), channel_id=1, replica_groups=mesh['z'=8,'x'=4,'y'=4,'core'=2] {'x','y'}, dimensions={0} | all-to-all | bytes 5242880 | tf_op jit(solution)/shard_map/all_to_all | solution.py:271
  137.1 0.4 convert_reduce_fusion
  137.5 0.7 multiply_convert_fusion.1
  138.2 1.7 %multiply_convert_fusion = bf16[64,1280]{1,0:T(8,128)(2,1)} fusion(f32[64,1280]{1,0:T(8,128)} %reduce-scatter.2.cloned.1.call-done), kind=kLoop, calls=%fused_computation.2 | loop fusion | flops 163840 | bytes 491520 | tf_op jit(solution)/shard_map/convert_element_type | solution.py:276
  (21 shorter events, 0.4 us)
Async XLA Ops:
  7.2 47.5 %all-gather.2.cloned.1.call-start = ((), (), s32[]{:S(2)}) async-start(), calls=%async_computation.4 | async-start | bytes 2785280 | tf_op jit(solution)/shard_map/all_gather | solution.py:244
  10.6 44.1 %all-to-all-start = ((bf16[16,64,1280]{2,1,0:T(8,128)(2,1)}), bf16[16,64,1280]{2,1,0:T(8,128)(2,1)S(1)}, u32[]{:S(2)}, u32[]{:S(2)}) async-start(bf16[16,64,1280]{2,1,0:T(8,128)(2,1)} %broadcast_in_dim.16), calls=%async_computation | async-start | bytes 5242880 | tf_op jit(solution)/shard_map/all_to_all | solution.py:245
  54.7 1.7 %copy-start = (bf16[1024,1280]{1,0:T(8,128)(2,1)S(1)}, bf16[1024,1280]{1,0:T(8,128)(2,1)}, u32[]{:S(2)}) copy-start(bf16[1024,1280]{1,0:T(8,128)(2,1)} %all-gather.2.cloned.1.call-done.texts.right) | copy-start | bytes 7864324
  56.4 18.3 %copy-start.4 = (s32[2048]{0:T(1024)S(1)}, s32[2048]{0:T(1024)}, u32[]{:S(2)}) copy-start(s32[2048]{0:T(1024)} %param.5) | copy-start | bytes 24580
  62.3 1.9 %copy-start.2 = (f32[1024,1024]{1,0:T(8,128)}, f32[1024,1024]{1,0:T(8,128)S(1)}, u32[]{:S(2)}) copy-start(f32[1024,1024]{1,0:T(8,128)S(1)} %get-tuple-element.12.scores) | copy-start | bytes 12582916
  64.3 1.2 collective-permute-start
  66.1 16.6 %all-to-all-start.1 = ((f32[16,16,128]{2,1,0:T(8,128)}), f32[16,16,128]{2,1,0:T(8,128)S(1)}, u32[]{:S(2)}, u32[]{:S(2)}) async-start(f32[16,16,128]{2,1,0:T(8,128)} %broadcast_in_dim.18), calls=%async_computation.1 | async-start | bytes 262144 | tf_op jit(solution)/shard_map/all_to_all | solution.py:260
  74.7 63.4 %reduce-scatter.2.cloned.1.call-start = ((), (), s32[]{:S(2)}) async-start(), calls=%async_computation.5 | async-start | bytes 2949120 | tf_op jit(solution)/shard_map/reduce_scatter | solution.py:270
  83.3 1.3 collective-permute-start.1
  84.8 2.2 %copy-start.3 = (f32[1024,1024]{1,0:T(8,128)S(1)}, f32[1024,1024]{1,0:T(8,128)}, u32[]{:S(2)}) copy-start(f32[1024,1024]{1,0:T(8,128)} %copy-done.2) | copy-start | bytes 12582916
  87.0 6.3 %copy-start.1 = (bf16[1024,1280]{1,0:T(8,128)(2,1)S(1)}, bf16[1024,1280]{1,0:T(8,128)(2,1)}, u32[]{:S(2)}) copy-start(bf16[1024,1280]{1,0:T(8,128)(2,1)} %all-gather.2.cloned.1.call-done.texts.right) | copy-start | bytes 7864324
  93.0 3.7 %collective-permute-start.2 = (bf16[512,1280]{1,0:T(8,128)(2,1)S(1)}, bf16[512,1280]{1,0:T(8,128)(2,1)S(1)}, u32[]{:S(2)}, u32[]{:S(2)}) collective-permute-start(bf16[512,1280]{1,0:T(8,128)(2,1)S(1)} %get-tuple-element.19), channel_id=1, source_target_pairs={{0,1},{1,0},{2,3},{3,2},{4,5},{5,4},{6,7},{7,6},{8,9},{9,8},{10,11... | collective-permute-start | bytes 3932168 | tf_op jit(solution)/shard_map/ppermute | solution.py:266
Sparse Core Ops, SparseCore 0:
  9.8 42.3 all-gather.1
  98.7 38.0 reduce-scatter.1

commit v2 on v0

v2 whole, which is shorter than its diff:
```python
import jax
import jax.numpy as jnp
from jax import lax
from jax.experimental import pallas as pl
from jax.experimental.pallas import tpu as pltpu
from jax.sharding import Mesh, PartitionSpec as P

score_scale = 0.1
lanes = 128
sizes = {"z": 8, "x": 4, "y": 4, "core": 2}
every = tuple(sizes)
offsets = (0, -1, 1, 2)
vmem_bytes = 24 * 1024 * 1024
in_vmem = pl.BlockSpec(memory_space=pltpu.VMEM)
in_smem = pl.BlockSpec(memory_space=pltpu.SMEM)
in_hbm = pl.BlockSpec(memory_space=pltpu.MemorySpace.HBM)
f32 = jnp.float32
bf16 = jnp.bfloat16


def device(z, x, y, core):
    return ((z % 8 * 4 + x % 4) * 4 + y % 4) * 2 + core


def send(value, move):
    pairs = [
        (device(z, x, y, core), device(*move(z, x, y, core)))
        for z in range(8)
        for x in range(4)
        for y in range(4)
        for core in range(2)
    ]
    return lax.ppermute(value, every, pairs)


def send_first(value, k):
    return send(value, lambda z, x, y, core: (z, x, y + k, 0) if core == 0 else (z, x + k, y, 1))


def send_second(value, k):
    return send(value, lambda z, x, y, core: (z, x + k, y, 0) if core == 0 else (z, x, y + k, 1))


def send_z(value, k):
    return send(value, lambda z, x, y, core: (z + k, x, y, 0) if core == 0 else (z - k, x, y, 1))


def swap_cores(value):
    return send(value, lambda z, x, y, core: (z, x, y, 1 - core))


def statistics_groups():
    columns = [
        [device(z, x + odd, y, 0) for odd in range(2) for z in range(8)] for x in (0, 2) for y in range(4)
    ]
    rows = [[device(z, x, y, 1) for x in range(4) for y in range(4)] for z in range(8)]
    return columns + rows


def row_tile(place, i, j):
    first = (place[1] + offsets[j]) & 3
    second = (place[2] + offsets[i]) & 3
    return jnp.where(place[0] == 0, second * 4 + first, first * 4 + second)


def scores_kernel(place, *refs):
    groups, pieces = refs[:4], refs[4:10]
    scores_out, texts_out, kept, sent, scores, texts, rows_out, sems = refs[10:]
    core, z = place[0], place[3]
    own, other = pieces[0], pieces[1]
    half = own.shape[0]
    pair = 2 * half
    side = 2 * core - 1

    def put(value, step, whose):
        start = pl.multiple_of(((z + step) & 7) * pair + whose * half, half)
        texts[pl.ds(start, half), :] = value

    put(own[...], 0, core)
    put(other[...], 0, 1 - core)
    for near, far, steps, whose in (
        (pieces[2], pieces[3], side, core),
        (pieces[4], pieces[5], -side, 1 - core),
    ):
        for k, piece in ((1, near[:pair]), (2, near[pair:]), (3, far[:pair])):
            put(piece[:half], steps * k, whose)
            put(piece[half:], steps * k, 1 - whose)
        put(far[pair:], 4, whose)

    rows_here = groups[0].shape[0]
    copies = [pltpu.make_async_copy(texts, texts_out, sems.at[4])]
    copies[0].start()
    for i in range(4):
        here = pl.ds(i * rows_here, rows_here)
        s = score_scale * lax.dot_general(
            groups[i][...], texts[...], (((1,), (1,)), ((), ())), preferred_element_type=f32
        )
        scores[here, :] = s
        copies.append(pltpu.make_async_copy(scores.at[here], scores_out.at[here], sems.at[i]))
        copies[-1].start()
        top = jnp.max(s, axis=1, keepdims=True)
        row = top + jnp.log(jnp.sum(jnp.exp(s - top), axis=1, keepdims=True))
        row = jnp.broadcast_to(row, (rows_here, lanes)).T
        for j in range(4):
            tile = row[:8, j // 2 * lanes : (j // 2 + 1) * lanes]
            if j % 2:
                tile = pltpu.roll(tile, half, 1)
            rows_out[pl.ds(row_tile(place, i, j), 1), :] = tile[:1]
        new = jnp.max(s, axis=0, keepdims=True)
        if i:
            new = jnp.maximum(col_top, new)
        total = jnp.sum(jnp.exp(s - new), axis=0, keepdims=True)
        if i:
            total = total + col_sum * jnp.exp(col_top - new)
        col_top, col_sum = new, total

    col = col_top + jnp.log(col_sum)
    first = core == 0
    for i in range(kept.shape[0]):
        row_here = rows_out[i : i + 1, :]
        k = i % (col.shape[1] // lanes)
        col_here = col[:, k * lanes : (k + 1) * lanes]
        kept[i : i + 1, :] = jnp.where(first, col_here, row_here)
        sent[i : i + 1, :] = jnp.where(first, row_here, col_here)
    for copy in copies:
        copy.wait()


def local_scores(place, groups, pieces):
    width = groups[0].shape[1]
    rows = 4 * groups[0].shape[0]
    cols = 16 * pieces[0].shape[0]
    tile = (16, lanes)
    return pl.pallas_call(
        scores_kernel,
        in_specs=[in_smem] + [in_vmem] * 10,
        out_specs=[in_hbm, in_hbm, in_vmem, in_vmem],
        out_shape=[
            pltpu.MemorySpace.HBM((rows, cols), f32),
            pltpu.MemorySpace.HBM((cols, width), bf16),
            jax.ShapeDtypeStruct(tile, f32),
            jax.ShapeDtypeStruct(tile, f32),
        ],
        scratch_shapes=[
            pltpu.VMEM((rows, cols), f32),
            pltpu.VMEM((cols, width), bf16),
            pltpu.VMEM(tile, f32),
            pltpu.SemaphoreType.DMA((5,)),
        ],
        compiler_params=pltpu.CompilerParams(vmem_limit_bytes=vmem_bytes),
        cost_estimate=pl.CostEstimate(
            flops=2 * rows * cols * width, bytes_accessed=6_000_000, transcendentals=2 * rows * cols
        ),
        name="scores",
    )(place, *groups, *pieces)


def spread_kernel(place, kept, received, out):
    first = place[0] == 0
    low = jnp.where(first, kept[...], received[...])
    high = jnp.where(first, received[...], kept[...])
    for i in range(out.shape[0]):
        out[i, 0] = low
        out[i, 1] = high


def spread(place, kept, received):
    return pl.pallas_call(
        spread_kernel,
        in_specs=[in_smem] + [in_vmem] * 2,
        out_specs=in_vmem,
        out_shape=jax.ShapeDtypeStruct((16, 2, *kept.shape), f32),
        compiler_params=pltpu.CompilerParams(vmem_limit_bytes=vmem_bytes),
        name="spread",
    )(place, kept, received)


def merge_kernel(place, parts, kept, sent):
    def total(pieces):
        top = pieces[0]
        for piece in pieces[1:]:
            top = jnp.maximum(top, piece)
        sums = jnp.exp(pieces[0] - top)
        for piece in pieces[1:]:
            sums = sums + jnp.exp(piece - top)
        return top + jnp.log(sums)

    @pl.when(place[0] == 0)
    def _():
        first = place[4] * 8
        col = total([parts[first + z, core] for z in range(8) for core in range(2)])
        kept[...] = col
        sent[...] = col

    @pl.when(place[0] == 1)
    def _():
        sent[...] = total([parts[i, 0] for i in range(16)])
        kept[...] = total([parts[i, 1] for i in range(16)])


def merge(place, parts):
    tile = parts.shape[2:]
    return pl.pallas_call(
        merge_kernel,
        in_specs=[in_smem, in_vmem],
        out_specs=[in_vmem] * 2,
        out_shape=[jax.ShapeDtypeStruct(tile, f32)] * 2,
        compiler_params=pltpu.CompilerParams(vmem_limit_bytes=vmem_bytes),
        name="merge",
    )(place, parts)


def dscores_kernel(
    place, scores_in, kept, received, labels, g0, g1, g2, g3, dscores, mine, theirs, scores, total, targets, sems
):
    core, z = place[0], place[3]
    first = core == 0
    half = lanes // 2
    rows_here = g0.shape[0]
    cols = scores.shape[1]
    copies = []
    for i in range(4):
        here = pl.ds(i * rows_here, rows_here)
        copies.append(pltpu.make_async_copy(scores_in.at[here], scores.at[here], sems.at[i]))
        copies[-1].start()
    label = labels[...]
    spot = place[5]
    target = jnp.where((label >> 7) & 15 == spot, (label >> 11) * lanes + (label & 127), -1).astype(f32)
    target = jnp.where(first, target, pltpu.roll(target, half, 1))
    lane_row = lax.broadcasted_iota(jnp.int32, (8, lanes), 1)
    lane = lax.broadcasted_iota(jnp.int32, (lanes, lanes), 1).astype(f32)

    def column(read, i, j):
        low = jnp.broadcast_to(read(row_tile(place, i, j)), (8, lanes))
        high = pltpu.roll(jnp.broadcast_to(read(row_tile(place, i, j + 1)), (8, lanes)), half, 1)
        both = jnp.where(lane_row < half, low, high)
        return jnp.broadcast_to(both[:1], (lanes, lanes)).T

    def row_lse(k):
        return jnp.where(first, received[pl.ds(k, 1), :], kept[pl.ds(k, 1), :])

    targets[...] = target

    def target_of(k):
        return targets[pl.ds(k, 1), :]

    col_lse = jnp.where(first, kept[...], received[...])
    for i in range(4):
        copies[i].wait()
        for j in (0, 2):
            row = column(row_lse, i, j)
            wanted = column(target_of, i, j)
            here = slice(i * rows_here + j * half, i * rows_here + j * half + lanes)
            for chunk in range(cols // lanes):
                part = slice(chunk * lanes, (chunk + 1) * lanes)
                s = scores[here, part]
                match = jnp.where(wanted == lane + float(chunk * lanes), 2.0, 0.0)
                dscores[here, part] = (
                    jnp.exp(s - row) + jnp.exp(s - col_lse[chunk : chunk + 1]) - match
                ).astype(bf16)

    images = jnp.concatenate([g0[...], g1[...], g2[...], g3[...]], axis=0)
    total[...] = lax.dot_general(
        dscores[...], images, (((0,), (0,)), ((), ())), preferred_element_type=f32
    )
    side = 1 - 2 * core

    def take(step, offset, size):
        return total[pl.ds(pl.multiple_of(((z + step) & 7) * lanes + offset, half), size), :]

    for k in range(1, 4):
        here = slice((k - 1) * lanes, k * lanes)
        mine[here, :] = take(side * k, 0, lanes)
        theirs[here, :] = take(-side * k, 0, lanes).astype(bf16)
    for k, step in ((6, 4), (7, 0)):
        here = slice(k * half, (k + 1) * half)
        mine[here, :] = take(step, core * half, half)
        theirs[here, :] = take(step, (1 - core) * half, half).astype(bf16)


def local_dscores(place, scores, kept, received, labels, groups):
    rows, cols = scores.shape
    width = groups[0].shape[1]
    return pl.pallas_call(
        dscores_kernel,
        in_specs=[in_smem, in_hbm] + [in_vmem] * 7,
        out_specs=[in_vmem] * 3,
        out_shape=[
            pltpu.VMEM((rows, cols), bf16),
            pltpu.VMEM((cols // 2, width), f32),
            pltpu.VMEM((cols // 2, width), bf16),
        ],
        scratch_shapes=[
            pltpu.VMEM((rows, cols), f32),
            pltpu.VMEM((cols, width), f32),
            pltpu.VMEM(labels.shape, f32),
            pltpu.SemaphoreType.DMA((4,)),
        ],
        compiler_params=pltpu.CompilerParams(vmem_limit_bytes=vmem_bytes),
        cost_estimate=pl.CostEstimate(
            flops=2 * rows * cols * width, bytes_accessed=6_000_000, transcendentals=2 * rows * cols
        ),
        name="dscores",
    )(place, scores, kept, received, labels, *groups)


def product_kernel(dscores, texts, *outs):
    rows_here = outs[0].shape[0]
    for i in (3, 1, 2, 0):
        outs[i][...] = jnp.dot(
            dscores[i * rows_here : (i + 1) * rows_here, :], texts[...], preferred_element_type=f32
        ).astype(outs[i].dtype)


def product(dscores, texts):
    rows, depth = dscores.shape
    width = texts.shape[1]
    return pl.pallas_call(
        product_kernel,
        in_specs=[in_vmem] * 2,
        out_specs=[in_vmem] * 4,
        out_shape=[pltpu.VMEM((rows // 4, width), f32 if i == 0 else bf16) for i in range(4)],
        compiler_params=pltpu.CompilerParams(vmem_limit_bytes=vmem_bytes),
        cost_estimate=pl.CostEstimate(
            flops=2 * rows * depth * width, bytes_accessed=6_000_000, transcendentals=0
        ),
        name="image_product",
    )(dscores, texts)


def add_text_kernel(mine, received, near, far, own):
    start = 0
    for out in (near, far, own):
        here = slice(start, start + out.shape[0])
        out[...] = (mine[here, :] + received[here, :].astype(f32)).astype(out.dtype)
        start += out.shape[0]


def add_text(mine, received):
    rows, width = mine.shape
    shapes = [(rows // 2, f32), (rows // 8 * 3, bf16), (rows // 8, f32)]
    return pl.pallas_call(
        add_text_kernel,
        in_specs=[in_vmem] * 2,
        out_specs=[in_vmem] * 3,
        out_shape=[pltpu.VMEM((n, width), kind) for n, kind in shapes],
        compiler_params=pltpu.CompilerParams(vmem_limit_bytes=vmem_bytes),
        cost_estimate=pl.CostEstimate(flops=rows * width, bytes_accessed=6 * rows * width, transcendentals=0),
        name="text_add",
    )(mine, received)


def relay_text_kernel(place, near, received, one, two):
    pair, half = one.shape[0], one.shape[0] // 2
    one[...] = (near[:pair] + received[:pair].astype(f32)).astype(bf16)
    two[...] = near[pair:].astype(bf16)
    here = pl.multiple_of(place[0] * half, half)
    two[pl.ds(here, half), :] = (
        near[pl.ds(pair + here, half), :] + received[pair:].astype(f32)
    ).astype(bf16)


def relay_text(place, near, received):
    rows, width = near.shape
    return pl.pallas_call(
        relay_text_kernel,
        in_specs=[in_smem] + [in_vmem] * 2,
        out_specs=[in_vmem] * 2,
        out_shape=[pltpu.VMEM((rows // 2, width), bf16)] * 2,
        compiler_params=pltpu.CompilerParams(vmem_limit_bytes=vmem_bytes),
        cost_estimate=pl.CostEstimate(flops=rows * width, bytes_accessed=6 * rows * width, transcendentals=0),
        name="text_relay",
    )(place, near, received)


def split_text_kernel(place, one, two, own, here, there):
    half = own.shape[0]
    core = place[0]

    def total(which):
        rows = pl.ds(pl.multiple_of(which * half, half), half)
        return one[rows, :].astype(f32) + two[rows, :].astype(f32)

    here[...] = total(core) + own[...]
    there[...] = total(1 - core)


def split_text(place, one, two, own):
    return pl.pallas_call(
        split_text_kernel,
        in_specs=[in_smem] + [in_vmem] * 3,
        out_specs=[in_vmem] * 2,
        out_shape=[pltpu.VMEM(own.shape, f32)] * 2,
        compiler_params=pltpu.CompilerParams(vmem_limit_bytes=vmem_bytes),
        cost_estimate=pl.CostEstimate(flops=4 * own.size, bytes_accessed=20 * own.size, transcendentals=0),
        name="text_split",
    )(place, one, two, own)


def join_kernel(*refs):
    out = refs[-1]
    start = 0
    for ref in refs[:-1]:
        size = min(ref.shape[0], out.shape[0] - start)
        out[start : start + size, :] = ref[:size, :]
        start += size


def join(rows, *parts):
    width = parts[0].shape[1]
    return pl.pallas_call(
        join_kernel,
        in_specs=[in_vmem] * len(parts),
        out_specs=in_vmem,
        out_shape=pltpu.VMEM((rows, width), bf16),
        compiler_params=pltpu.CompilerParams(vmem_limit_bytes=vmem_bytes),
        cost_estimate=pl.CostEstimate(flops=0, bytes_accessed=4 * rows * width, transcendentals=0),
        name="join",
    )(*parts)


def add_image_kernel(p0, p1, p2, p3, *outs):
    size = outs[0].shape[0]
    for j in range(4):
        here = slice(j * size, (j + 1) * size)
        outs[j][...] = (
            p0[here, :] + p1[here, :].astype(f32) + p2[here, :].astype(f32) + p3[here, :].astype(f32)
        )


def add_image(parts):
    rows, width = parts[0].shape
    return pl.pallas_call(
        add_image_kernel,
        in_specs=[in_vmem] * 4,
        out_specs=[in_vmem] * 4,
        out_shape=[pltpu.VMEM((rows // 4, width), f32)] * 4,
        compiler_params=pltpu.CompilerParams(vmem_limit_bytes=vmem_bytes),
        cost_estimate=pl.CostEstimate(
            flops=4 * rows * width, bytes_accessed=14 * rows * width, transcendentals=0
        ),
        name="image_add",
    )(*parts)


def gather(image_embeds, text_embeds):
    block = image_embeds.shape[0]
    line = [send_first(image_embeds, -k) for k in offsets[1:]]
    other = swap_cores(text_embeds)
    pair = join(2 * block, text_embeds, other)
    near = [send_z(pair, 2), send_z(pair, 1)]
    line, near = lax.optimization_barrier((line, near))
    line = join(4 * block, image_embeds, *line)
    ahead = join(3 * block, near[1], near[0])
    groups = [line] + [send_second(line, -k) for k in offsets[1:]]
    far = send_z(ahead, 2)
    near = join(4 * block, near[1], near[0])
    pieces = [text_embeds, other, near, far, swap_cores(near), swap_cores(far)]
    return groups, pieces


def shards(image_embeds, text_embeds, labels):
    z, x, y, core = (lax.axis_index(name) for name in every)
    along = [core, jnp.where(core == 0, y, x), jnp.where(core == 0, x, y), z, x & 1, x * 4 + y]
    place = jnp.stack(along).astype(jnp.int32)
    image_embeds, text_embeds, labels, place = lax.optimization_barrier(
        (image_embeds, text_embeds, labels, place)
    )
    groups, pieces = gather(image_embeds, text_embeds)
    scores, texts, kept, sent = local_scores(place, groups, pieces)
    parts = spread(place, kept, swap_cores(sent))
    parts = lax.all_to_all(
        parts.reshape(-1, lanes), every, 0, 0, axis_index_groups=statistics_groups(), tiled=True
    ).reshape(parts.shape)
    kept, sent = merge(place, parts)
    received = swap_cores(sent)

    dscores, mine, theirs = local_dscores(
        place, scores, kept, received, labels.reshape(-1, lanes), groups
    )
    theirs = swap_cores(theirs)
    terms = product(dscores, texts)
    near, far, own = add_text(mine, theirs)
    far = send_z(far, 2)
    parts = [send_second(t, k) for t, k in zip(terms[1:], offsets[1:])]
    far, parts = lax.optimization_barrier((far, parts))
    one, two = relay_text(place, near, far)
    terms = add_image([terms[0]] + parts)
    two, one = send_z(two, 2), send_z(one, 1)
    image_parts = [terms[0]] + [send_first(t, k) for t, k in zip(terms[1:], offsets[1:])]
    here, there = split_text(place, one, two, own)
    text_grad = (score_scale * (here + swap_cores(there))).astype(bf16)
    image_total = image_parts[0] + image_parts[1] + image_parts[2] + image_parts[3]
    image_grad = (score_scale * image_total).astype(bf16)
    return (image_grad, text_grad)


def solution(mesh):
    grid = Mesh(mesh.devices.reshape(tuple(sizes.values())), every)
    split = P(every, None)
    return jax.shard_map(
        shards, mesh=grid, in_specs=(split, split, P("z")), out_specs=(split, split), check_vma=False
    )
```

time: 444 us -> 120 us (0.27)
  waiting for transfers between devices: 236 us -> 48.2 us
  blocking collectives: 162 us -> 16.2 us
  starting transfers between devices: 0.16 us -> 31.8 us
  matrix products: 24.6 us -> 0 us
  Pallas kernels: 0 us -> 17.5 us
  between operations: 13.8 us -> 0.82 us
  other arithmetic: 6.5 us -> 1.45 us
    reduce_scatter x2 -> x0, waiting for transfers between devices: 138 us -> none  [the longest x1 108 us: shards(): lax.psum_scatter(image_term, 'col', scatter_dimension=0, tiled=True)]
    all_gather x2 -> x0, waiting for transfers between devices: 96.7 us -> none  [the longest x1 54.2 us: shards(): images = lax.all_gather(image_embeds, 'col', axis=0, tiled=True)]
    pmax x2 -> x0, blocking collectives: 82.3 us -> none  [the longest x1 66.2 us: shards(): row_top = lax.pmax(row_top, 'col')]
    psum x2 -> x0, blocking collectives: 79.7 us -> none  [the longest x1 63.7 us: shards(): lax.psum(jnp.sum(jnp.exp(scores - row_top[:, None]), axis=1), 'col')]
    ppermute x0 -> x25, waiting for transfers between devices: none -> 48.2 us  [send(): return lax.ppermute(value, every, pairs)]
    ppermute x0 -> x25, starting transfers between devices: none -> 31.8 us  [send(): return lax.ppermute(value, every, pairs)]
    dot_general x3 -> x0, matrix products: 24.6 us -> none  [the longest x1 8.73 us: shards(): lax.dot_general(dscores, images, (((0,), (0,)), ((), ())), preferred_elem...]
    pallas_call x0 -> x13, Pallas kernels: none -> 17.5 us  [the longest x1 6.44 us: local_dscores(): pl.pallas_call(dscores_kernel, in_specs=[in_smem, in_hbm] + [in_vmem] * 7...]
  transfers between devices with their start and end apart: 4 -> 25, of which waited for: 4 -> 13; matrix products, arithmetic and copies ran while one was open for 2% -> 1% of each run, Pallas kernels for 0% -> 3%
where the time goes in v2:
time: 120 us; the launch traced here: 119 us
  waiting for transfers between devices  48.2 us (40%)
  starting transfers between devices  31.8 us (26%)
  Pallas kernels  17.5 us (15%)
  blocking collectives  16.2 us (14%)
  local copies, waits for them, and re-layouts  3.21 us (3%)
  other arithmetic  1.45 us (1%)
    ppermute x25, waiting for transfers between devices, send(): return lax.ppermute(value, every, pairs)  48.2 us
    ppermute x25, starting transfers between devices, send(): return lax.ppermute(value, every, pairs)  31.8 us
    all_to_all x1, blocking collectives, shards(): lax.all_to_all(parts.reshape(-1, lanes), every, 0, 0, axis_index_groups=s...  16.2 us
    pallas_call x1, Pallas kernels, local_dscores(): pl.pallas_call(dscores_kernel, in_specs=[in_smem, in_hbm] + [in_vmem] * 7...  6.44 us
    pallas_call x1, Pallas kernels, local_scores(): pl.pallas_call(scores_kernel, in_specs=[in_smem] + [in_vmem] * 10, out_sp...  5.01 us
    unnamed x12, local copies, waits for them, and re-layouts  3.12 us
    pallas_call x1, Pallas kernels, product(): pl.pallas_call(product_kernel, in_specs=[in_vmem] * 2, out_specs=[in_vmem...  2.89 us
  transfers between devices with their start and end apart: 25, of which 13 were waited for; matrix products, arithmetic and copies ran while one was open for 1% of the time, Pallas kernels for 3%

profile of v2, /device:TPU:32, one launch (start us, length us, event | category | flops | bytes accessed | tf_op | source)
XLA Modules:
  0.0 119.1 jit_solution(8915917920610554408)
XLA Ops:
  0.8 1.6 %collective-permute-done.3.refs_1_.refs_5_ = bf16[64,1280]{1,0:T(8,128)(2,1)S(1)} collective-permute-done((bf16[64,1280]{1,0:T(8,128)(2,1)}, bf16[64,1280]{1,0:T(8,128)(2,1)S(1)}, u32[]{:S(2)}, u32[]{:S(2)}) %collective-permute-start.3) | collective-permute-done | bytes 163872 | tf_op jit(solution)/shard_map/ppermute | solution.py:33
  3.3 2.0 %collective-permute-start.5 = (bf16[128,1280]{1,0:T(8,128)(2,1)S(1)}, bf16[128,1280]{1,0:T(8,128)(2,1)S(1)}, u32[]{:S(2)}, u32[]{:S(2)}) collective-permute-start(bf16[128,1280]{1,0:T(8,128)(2,1)S(1)} %join.4), channel_id=1, source_target_pairs={{0,32},{1,225},{2,34},{3,227},{4,36},{5,229},{6,38},{7,231},{8,40}... | collective-permute-start | bytes 983048 | tf_op jit(solution)/shard_map/ppermute | solution.py:33
  5.3 4.5 %collective-permute-start.4 = (bf16[128,1280]{1,0:T(8,128)(2,1)S(1)}, bf16[128,1280]{1,0:T(8,128)(2,1)S(1)}, u32[]{:S(2)}, u32[]{:S(2)}) collective-permute-start(bf16[128,1280]{1,0:T(8,128)(2,1)S(1)} %join.4), channel_id=1, source_target_pairs={{0,64},{1,193},{2,66},{3,195},{4,68},{5,197},{6,70},{7,199},{8,72}... | collective-permute-start | bytes 983048 | tf_op jit(solution)/shard_map/ppermute | solution.py:33
  9.8 3.2 %collective-permute-start.2 = (bf16[64,1280]{1,0:T(8,128)(2,1)}, bf16[64,1280]{1,0:T(8,128)(2,1)S(1)}, u32[]{:S(2)}, u32[]{:S(2)}) collective-permute-start(bf16[64,1280]{1,0:T(8,128)(2,1)} %refs_0_.1), channel_id=1, source_target_pairs={{0,4},{1,17},{2,6},{3,19},{4,0},{5,21},{6,2},{7,23},{8,12},{9,25},... | collective-permute-start | bytes 491528 | tf_op jit(solution)/shard_map/ppermute | solution.py:33
  15.0 1.8 %collective-permute-done.2.refs_3_ = bf16[64,1280]{1,0:T(8,128)(2,1)S(1)} collective-permute-done((bf16[64,1280]{1,0:T(8,128)(2,1)}, bf16[64,1280]{1,0:T(8,128)(2,1)S(1)}, u32[]{:S(2)}, u32[]{:S(2)}) %collective-permute-start.2) | collective-permute-done | bytes 163872 | tf_op jit(solution)/shard_map/ppermute | solution.py:33
  16.8 2.1 %collective-permute-done.1.refs_2_ = bf16[64,1280]{1,0:T(8,128)(2,1)S(1)} collective-permute-done((bf16[64,1280]{1,0:T(8,128)(2,1)}, bf16[64,1280]{1,0:T(8,128)(2,1)S(1)}, u32[]{:S(2)}, u32[]{:S(2)}) %collective-permute-start.1) | collective-permute-done | bytes 163872 | tf_op jit(solution)/shard_map/ppermute | solution.py:33
  18.9 1.9 %collective-permute-done.refs_1_ = bf16[64,1280]{1,0:T(8,128)(2,1)S(1)} collective-permute-done((bf16[64,1280]{1,0:T(8,128)(2,1)}, bf16[64,1280]{1,0:T(8,128)(2,1)S(1)}, u32[]{:S(2)}, u32[]{:S(2)}) %collective-permute-start) | collective-permute-done | bytes 163872 | tf_op jit(solution)/shard_map/ppermute | solution.py:33
  20.9 1.5 %collective-permute-start.9 = (bf16[192,1280]{1,0:T(8,128)(2,1)S(1)}, bf16[192,1280]{1,0:T(8,128)(2,1)S(1)}, u32[]{:S(2)}, u32[]{:S(2)}) collective-permute-start(bf16[192,1280]{1,0:T(8,128)(2,1)S(1)} %join.7), channel_id=1, source_target_pairs={{0,64},{1,193},{2,66},{3,195},{4,68},{5,197},{6,70},{7,199},{8,72}... | collective-permute-start | bytes 1474568 | tf_op jit(solution)/shard_map/ppermute | solution.py:33
  22.6 3.1 %collective-permute-start.8 = (bf16[256,1280]{1,0:T(8,128)(2,1)S(1)}, bf16[256,1280]{1,0:T(8,128)(2,1)S(1)}, u32[]{:S(2)}, u32[]{:S(2)}) collective-permute-start(bf16[256,1280]{1,0:T(8,128)(2,1)S(1)} %join.5.refs_0_.g0), channel_id=1, source_target_pairs={{0,16},{1,5},{2,18},{3,7},{4,20},{5,1},{6,22},{7,3},{8,24},{9,13},... | collective-permute-start | bytes 1966088 | tf_op jit(solution)/shard_map/ppermute | solution.py:33
  27.7 7.9 %collective-permute-done.9.refs_7_ = bf16[192,1280]{1,0:T(8,128)(2,1)S(1)} collective-permute-done((bf16[192,1280]{1,0:T(8,128)(2,1)S(1)}, bf16[192,1280]{1,0:T(8,128)(2,1)S(1)}, u32[]{:S(2)}, u32[]{:S(2)}) %collective-permute-start.9) | collective-permute-done | bytes 491552 | tf_op jit(solution)/shard_map/ppermute | solution.py:33
  35.7 6.2 %collective-permute-done.7.refs_2_.g2 = bf16[256,1280]{1,0:T(8,128)(2,1)S(1)} collective-permute-done((bf16[256,1280]{1,0:T(8,128)(2,1)S(1)}, bf16[256,1280]{1,0:T(8,128)(2,1)S(1)}, u32[]{:S(2)}, u32[]{:S(2)}) %collective-permute-start.7) | collective-permute-done | bytes 655392 | tf_op jit(solution)/shard_map/ppermute | solution.py:33
  41.9 5.0 %scores.1 = (f32[1024,1024]{1,0:T(8,128)}, bf16[1024,1280]{1,0:T(8,128)(2,1)}, f32[16,128]{1,0:T(8,128)S(1)}, f32[16,128]{1,0:T(8,128)S(1)}) custom-call(s32[6]{0:T(128)S(1)} %stack.27.place, bf16[256,1280]{1,0:T(8,128)(2,1)S(1)} %join.5.refs_0_.g0, bf16[256,1280]{1,0:T(8,128)(2,1)S(1)} %collective-permute-done.6.refs_1_.g1, ...), custom_call_target="tpu_custom_call" | custom-call | flops 2684354560 | bytes 6000000 | tf_op jit(solution)/shard_map/scores/pallas_call | solution.py:134
  49.0 16.2 %all_to_all.9 = f32[16,32,128]{2,1,0:T(8,128)S(1)} all-to-all(f32[16,32,128]{2,1,0:T(8,128)S(1)} %bitcast.10), channel_id=1, replica_groups={{0,32,64,96,128,160,192,224,8,40,72,104,136,168,200,232},{2,34,66,98,13..., dimensions={0} | all-to-all | bytes 524288 | tf_op jit(solution)/shard_map/all_to_all | solution.py:472
  67.0 2.2 %copy-done.4 = f32[1024,1024]{1,0:T(8,128)S(1)} copy-done((f32[1024,1024]{1,0:T(8,128)S(1)}, f32[1024,1024]{1,0:T(8,128)}, u32[]{:S(2)}) %copy-start.4) | copy-done | bytes 4194328
  69.2 6.4 %dscores.1 = (bf16[1024,1024]{1,0:T(8,128)(2,1)S(1)}, f32[512,1280]{1,0:T(8,128)S(1)}, bf16[512,1280]{1,0:T(8,128)(2,1)S(1)}) custom-call(s32[6]{0:T(128)S(1)} %stack.27.place, f32[1024,1024]{1,0:T(8,128)S(1)} %copy-done.4, f32[16,128]{1,0:T(8,128)S(1)} %get-tuple-element.50.kept, f32[16,128]{1,0:T(8,128)S(1)} %collective-permute-done.13.received, ...), custom_call_target="tpu_custom_call" | custom-call | flops 2684354560 | bytes 6000000 | tf_op jit(solution)/shard_map/dscores/pallas_call | solution.py:284
  75.9 2.9 %image_product.1 = (f32[256,1280]{1,0:T(8,128)S(1)}, bf16[256,1280]{1,0:T(8,128)(2,1)S(1)}, bf16[256,1280]{1,0:T(8,128)(2,1)S(1)}, bf16[256,1280]{1,0:T(8,128)(2,1)S(1)}) custom-call(bf16[1024,1024]{1,0:T(8,128)(2,1)S(1)} %get-tuple-element.53.dscores, bf16[1024,1280]{1,0:T(8,128)(2,1)S(1)} %copy-done.5), custom_call_target="tpu_custom_call" | custom-call | flops 2684354560 | bytes 6000000 | tf_op jit(solution)/shard_map/image_product/pallas_call | solution.py:318
  78.8 2.4 %collective-permute-start.16 = (bf16[256,1280]{1,0:T(8,128)(2,1)S(1)}, bf16[256,1280]{1,0:T(8,128)(2,1)S(1)}, u32[]{:S(2)}, u32[]{:S(2)}) collective-permute-start(bf16[256,1280]{1,0:T(8,128)(2,1)S(1)} %get-tuple-element.59), channel_id=1, source_target_pairs={{0,24},{1,7},{2,26},{3,1},{4,28},{5,3},{6,30},{7,5},{8,0},{9,15},{... | collective-permute-start | bytes 1966088 | tf_op jit(solution)/shard_map/ppermute | solution.py:33
  81.2 2.4 %collective-permute-start.18 = (bf16[256,1280]{1,0:T(8,128)(2,1)S(1)}, bf16[256,1280]{1,0:T(8,128)(2,1)S(1)}, u32[]{:S(2)}, u32[]{:S(2)}) collective-permute-start(bf16[256,1280]{1,0:T(8,128)(2,1)S(1)} %get-tuple-element.61), channel_id=1, source_target_pairs={{0,16},{1,5},{2,18},{3,7},{4,20},{5,1},{6,22},{7,3},{8,24},{9,13},... | collective-permute-start | bytes 1966088 | tf_op jit(solution)/shard_map/ppermute | solution.py:33
  84.7 11.7 %collective-permute-done.16.p1 = bf16[256,1280]{1,0:T(8,128)(2,1)S(1)} collective-permute-done((bf16[256,1280]{1,0:T(8,128)(2,1)S(1)}, bf16[256,1280]{1,0:T(8,128)(2,1)S(1)}, u32[]{:S(2)}, u32[]{:S(2)}) %collective-permute-start.16) | collective-permute-done | bytes 655392 | tf_op jit(solution)/shard_map/ppermute | solution.py:33
  96.4 3.7 %collective-permute-done.17.p2 = bf16[256,1280]{1,0:T(8,128)(2,1)S(1)} collective-permute-done((bf16[256,1280]{1,0:T(8,128)(2,1)S(1)}, bf16[256,1280]{1,0:T(8,128)(2,1)S(1)}, u32[]{:S(2)}, u32[]{:S(2)}) %collective-permute-start.17) | collective-permute-done | bytes 655392 | tf_op jit(solution)/shard_map/ppermute | solution.py:33
  102.8 3.1 %collective-permute-start.19 = (f32[64,1280]{1,0:T(8,128)S(1)}, f32[64,1280]{1,0:T(8,128)S(1)}, u32[]{:S(2)}, u32[]{:S(2)}) collective-permute-start(f32[64,1280]{1,0:T(8,128)S(1)} %get-tuple-element.66), channel_id=1, source_target_pairs={{0,6},{1,25},{2,0},{3,27},{4,2},{5,29},{6,4},{7,31},{8,14},{9,1},{... | collective-permute-start | bytes 983048 | tf_op jit(solution)/shard_map/ppermute | solution.py:33
  105.9 2.2 %collective-permute-start.21 = (f32[64,1280]{1,0:T(8,128)S(1)}, f32[64,1280]{1,0:T(8,128)S(1)}, u32[]{:S(2)}, u32[]{:S(2)}) collective-permute-start(f32[64,1280]{1,0:T(8,128)S(1)} %get-tuple-element.68), channel_id=1, source_target_pairs={{0,4},{1,17},{2,6},{3,19},{4,0},{5,21},{6,2},{7,23},{8,12},{9,25},... | collective-permute-start | bytes 983048 | tf_op jit(solution)/shard_map/ppermute | solution.py:33
  108.1 7.5 %collective-permute-done.23.two = bf16[128,1280]{1,0:T(8,128)(2,1)S(1)} collective-permute-done((bf16[128,1280]{1,0:T(8,128)(2,1)S(1)}, bf16[128,1280]{1,0:T(8,128)(2,1)S(1)}, u32[]{:S(2)}, u32[]{:S(2)}) %collective-permute-start.23) | collective-permute-done | bytes 327712 | tf_op jit(solution)/shard_map/ppermute | solution.py:33
  116.4 1.3 %collective-permute-done.20 = f32[64,1280]{1,0:T(8,128)S(1)} collective-permute-done((f32[64,1280]{1,0:T(8,128)S(1)}, f32[64,1280]{1,0:T(8,128)S(1)}, u32[]{:S(2)}, u32[]{:S(2)}) %collective-permute-start.20) | collective-permute-done | bytes 327712 | tf_op jit(solution)/shard_map/ppermute | solution.py:33
  (55 shorter events, 15.5 us)
Async XLA Ops:
  0.7 1.6 %collective-permute-start.3 = (bf16[64,1280]{1,0:T(8,128)(2,1)}, bf16[64,1280]{1,0:T(8,128)(2,1)S(1)}, u32[]{:S(2)}, u32[]{:S(2)}) collective-permute-start(bf16[64,1280]{1,0:T(8,128)(2,1)} %refs_4_), channel_id=1, source_target_pairs={{0,1},{1,0},{2,3},{3,2},{4,5},{5,4},{6,7},{7,6},{8,9},{9,8},{10,11... | collective-permute-start | bytes 491528 | tf_op jit(solution)/shard_map/ppermute | solution.py:33
  3.3 17.5 %collective-permute-start.5 = (bf16[128,1280]{1,0:T(8,128)(2,1)S(1)}, bf16[128,1280]{1,0:T(8,128)(2,1)S(1)}, u32[]{:S(2)}, u32[]{:S(2)}) collective-permute-start(bf16[128,1280]{1,0:T(8,128)(2,1)S(1)} %join.4), channel_id=1, source_target_pairs={{0,32},{1,225},{2,34},{3,227},{4,36},{5,229},{6,38},{7,231},{8,40}... | collective-permute-start | bytes 983048 | tf_op jit(solution)/shard_map/ppermute | solution.py:33
  5.3 15.6 %collective-permute-start.4 = (bf16[128,1280]{1,0:T(8,128)(2,1)S(1)}, bf16[128,1280]{1,0:T(8,128)(2,1)S(1)}, u32[]{:S(2)}, u32[]{:S(2)}) collective-permute-start(bf16[128,1280]{1,0:T(8,128)(2,1)S(1)} %join.4), channel_id=1, source_target_pairs={{0,64},{1,193},{2,66},{3,195},{4,68},{5,197},{6,70},{7,199},{8,72}... | collective-permute-start | bytes 983048 | tf_op jit(solution)/shard_map/ppermute | solution.py:33
  9.8 7.0 %collective-permute-start.2 = (bf16[64,1280]{1,0:T(8,128)(2,1)}, bf16[64,1280]{1,0:T(8,128)(2,1)S(1)}, u32[]{:S(2)}, u32[]{:S(2)}) collective-permute-start(bf16[64,1280]{1,0:T(8,128)(2,1)} %refs_0_.1), channel_id=1, source_target_pairs={{0,4},{1,17},{2,6},{3,19},{4,0},{5,21},{6,2},{7,23},{8,12},{9,25},... | collective-permute-start | bytes 491528 | tf_op jit(solution)/shard_map/ppermute | solution.py:33
  13.0 5.9 %collective-permute-start.1 = (bf16[64,1280]{1,0:T(8,128)(2,1)}, bf16[64,1280]{1,0:T(8,128)(2,1)S(1)}, u32[]{:S(2)}, u32[]{:S(2)}) collective-permute-start(bf16[64,1280]{1,0:T(8,128)(2,1)} %refs_0_.1), channel_id=1, source_target_pairs={{0,6},{1,25},{2,0},{3,27},{4,2},{5,29},{6,4},{7,31},{8,14},{9,1},{... | collective-permute-start | bytes 491528 | tf_op jit(solution)/shard_map/ppermute | solution.py:33
  14.0 6.7 %collective-permute-start = (bf16[64,1280]{1,0:T(8,128)(2,1)}, bf16[64,1280]{1,0:T(8,128)(2,1)S(1)}, u32[]{:S(2)}, u32[]{:S(2)}) collective-permute-start(bf16[64,1280]{1,0:T(8,128)(2,1)} %refs_0_.1), channel_id=1, source_target_pairs={{0,2},{1,9},{2,4},{3,11},{4,6},{5,13},{6,0},{7,15},{8,10},{9,17},{... | collective-permute-start | bytes 491528 | tf_op jit(solution)/shard_map/ppermute | solution.py:33
  20.9 14.8 %collective-permute-start.9 = (bf16[192,1280]{1,0:T(8,128)(2,1)S(1)}, bf16[192,1280]{1,0:T(8,128)(2,1)S(1)}, u32[]{:S(2)}, u32[]{:S(2)}) collective-permute-start(bf16[192,1280]{1,0:T(8,128)(2,1)S(1)} %join.7), channel_id=1, source_target_pairs={{0,64},{1,193},{2,66},{3,195},{4,68},{5,197},{6,70},{7,199},{8,72}... | collective-permute-start | bytes 1474568 | tf_op jit(solution)/shard_map/ppermute | solution.py:33
  22.4 13.3 %collective-permute-start.10 = (bf16[256,1280]{1,0:T(8,128)(2,1)S(1)}, bf16[256,1280]{1,0:T(8,128)(2,1)S(1)}, u32[]{:S(2)}, u32[]{:S(2)}) collective-permute-start(bf16[256,1280]{1,0:T(8,128)(2,1)S(1)} %join.6.refs_6_), channel_id=1, source_target_pairs={{0,1},{1,0},{2,3},{3,2},{4,5},{5,4},{6,7},{7,6},{8,9},{9,8},{10,11... | collective-permute-start | bytes 1966088 | tf_op jit(solution)/shard_map/ppermute | solution.py:33
  22.6 13.1 %collective-permute-start.8 = (bf16[256,1280]{1,0:T(8,128)(2,1)S(1)}, bf16[256,1280]{1,0:T(8,128)(2,1)S(1)}, u32[]{:S(2)}, u32[]{:S(2)}) collective-permute-start(bf16[256,1280]{1,0:T(8,128)(2,1)S(1)} %join.5.refs_0_.g0), channel_id=1, source_target_pairs={{0,16},{1,5},{2,18},{3,7},{4,20},{5,1},{6,22},{7,3},{8,24},{9,13},... | collective-permute-start | bytes 1966088 | tf_op jit(solution)/shard_map/ppermute | solution.py:33
  25.7 16.2 %collective-permute-start.7 = (bf16[256,1280]{1,0:T(8,128)(2,1)S(1)}, bf16[256,1280]{1,0:T(8,128)(2,1)S(1)}, u32[]{:S(2)}, u32[]{:S(2)}) collective-permute-start(bf16[256,1280]{1,0:T(8,128)(2,1)S(1)} %join.5.refs_0_.g0), channel_id=1, source_target_pairs={{0,24},{1,7},{2,26},{3,1},{4,28},{5,3},{6,30},{7,5},{8,0},{9,15},{... | collective-permute-start | bytes 1966088 | tf_op jit(solution)/shard_map/ppermute | solution.py:33
  26.9 15.1 %collective-permute-start.6 = (bf16[256,1280]{1,0:T(8,128)(2,1)S(1)}, bf16[256,1280]{1,0:T(8,128)(2,1)S(1)}, u32[]{:S(2)}, u32[]{:S(2)}) collective-permute-start(bf16[256,1280]{1,0:T(8,128)(2,1)S(1)} %join.5.refs_0_.g0), channel_id=1, source_target_pairs={{0,8},{1,3},{2,10},{3,5},{4,12},{5,7},{6,14},{7,1},{8,16},{9,11},{... | collective-permute-start | bytes 1966088 | tf_op jit(solution)/shard_map/ppermute | solution.py:33
  35.7 6.3 %collective-permute-start.11 = (bf16[192,1280]{1,0:T(8,128)(2,1)S(1)}, bf16[192,1280]{1,0:T(8,128)(2,1)S(1)}, u32[]{:S(2)}, u32[]{:S(2)}) collective-permute-start(bf16[192,1280]{1,0:T(8,128)(2,1)S(1)} %collective-permute-done.9.refs_7_), channel_id=1, source_target_pairs={{0,1},{1,0},{2,3},{3,2},{4,5},{5,4},{6,7},{7,6},{8,9},{9,8},{10,11... | collective-permute-start | bytes 1474568 | tf_op jit(solution)/shard_map/ppermute | solution.py:33
  47.0 1.4 %collective-permute-start.12 = (f32[16,128]{1,0:T(8,128)S(1)}, f32[16,128]{1,0:T(8,128)S(1)}, u32[]{:S(2)}, u32[]{:S(2)}) collective-permute-start(f32[16,128]{1,0:T(8,128)S(1)} %get-tuple-element.49), channel_id=1, source_target_pairs={{0,1},{1,0},{2,3},{3,2},{4,5},{5,4},{6,7},{7,6},{8,9},{9,8},{10,11... | collective-permute-start | bytes 24584 | tf_op jit(solution)/shard_map/ppermute | solution.py:33
  75.7 7.9 %collective-permute-start.14 = (bf16[512,1280]{1,0:T(8,128)(2,1)S(1)}, bf16[512,1280]{1,0:T(8,128)(2,1)S(1)}, u32[]{:S(2)}, u32[]{:S(2)}) collective-permute-start(bf16[512,1280]{1,0:T(8,128)(2,1)S(1)} %get-tuple-element.57), channel_id=1, source_target_pairs={{0,1},{1,0},{2,3},{3,2},{4,5},{5,4},{6,7},{7,6},{8,9},{9,8},{10,11... | collective-permute-start | bytes 3932168 | tf_op jit(solution)/shard_map/ppermute | solution.py:33
  78.8 17.6 %collective-permute-start.16 = (bf16[256,1280]{1,0:T(8,128)(2,1)S(1)}, bf16[256,1280]{1,0:T(8,128)(2,1)S(1)}, u32[]{:S(2)}, u32[]{:S(2)}) collective-permute-start(bf16[256,1280]{1,0:T(8,128)(2,1)S(1)} %get-tuple-element.59), channel_id=1, source_target_pairs={{0,24},{1,7},{2,26},{3,1},{4,28},{5,3},{6,30},{7,5},{8,0},{9,15},{... | collective-permute-start | bytes 1966088 | tf_op jit(solution)/shard_map/ppermute | solution.py:33
  81.2 18.8 %collective-permute-start.17 = (bf16[256,1280]{1,0:T(8,128)(2,1)S(1)}, bf16[256,1280]{1,0:T(8,128)(2,1)S(1)}, u32[]{:S(2)}, u32[]{:S(2)}) collective-permute-start(bf16[256,1280]{1,0:T(8,128)(2,1)S(1)} %get-tuple-element.60), channel_id=1, source_target_pairs={{0,8},{1,3},{2,10},{3,5},{4,12},{5,7},{6,14},{7,1},{8,16},{9,11},{... | collective-permute-start | bytes 1966088 | tf_op jit(solution)/shard_map/ppermute | solution.py:33
  81.2 18.8 %collective-permute-start.18 = (bf16[256,1280]{1,0:T(8,128)(2,1)S(1)}, bf16[256,1280]{1,0:T(8,128)(2,1)S(1)}, u32[]{:S(2)}, u32[]{:S(2)}) collective-permute-start(bf16[256,1280]{1,0:T(8,128)(2,1)S(1)} %get-tuple-element.61), channel_id=1, source_target_pairs={{0,16},{1,5},{2,18},{3,7},{4,20},{5,1},{6,22},{7,3},{8,24},{9,13},... | collective-permute-start | bytes 1966088 | tf_op jit(solution)/shard_map/ppermute | solution.py:33
  83.8 16.2 %collective-permute-start.15 = (bf16[192,1280]{1,0:T(8,128)(2,1)S(1)}, bf16[192,1280]{1,0:T(8,128)(2,1)S(1)}, u32[]{:S(2)}, u32[]{:S(2)}) collective-permute-start(bf16[192,1280]{1,0:T(8,128)(2,1)S(1)} %get-tuple-element.58), channel_id=1, source_target_pairs={{0,64},{1,193},{2,66},{3,195},{4,68},{5,197},{6,70},{7,199},{8,72}... | collective-permute-start | bytes 1474568 | tf_op jit(solution)/shard_map/ppermute | solution.py:33
  100.8 7.4 %collective-permute-start.22 = (bf16[128,1280]{1,0:T(8,128)(2,1)S(1)}, bf16[128,1280]{1,0:T(8,128)(2,1)S(1)}, u32[]{:S(2)}, u32[]{:S(2)}) collective-permute-start(bf16[128,1280]{1,0:T(8,128)(2,1)S(1)} %get-tuple-element.71), channel_id=1, source_target_pairs={{0,32},{1,225},{2,34},{3,227},{4,36},{5,229},{6,38},{7,231},{8,40}... | collective-permute-start | bytes 983048 | tf_op jit(solution)/shard_map/ppermute | solution.py:33
  101.4 14.2 %collective-permute-start.23 = (bf16[128,1280]{1,0:T(8,128)(2,1)S(1)}, bf16[128,1280]{1,0:T(8,128)(2,1)S(1)}, u32[]{:S(2)}, u32[]{:S(2)}) collective-permute-start(bf16[128,1280]{1,0:T(8,128)(2,1)S(1)} %get-tuple-element.72), channel_id=1, source_target_pairs={{0,64},{1,193},{2,66},{3,195},{4,68},{5,197},{6,70},{7,199},{8,72}... | collective-permute-start | bytes 983048 | tf_op jit(solution)/shard_map/ppermute | solution.py:33
  102.8 13.6 %collective-permute-start.19 = (f32[64,1280]{1,0:T(8,128)S(1)}, f32[64,1280]{1,0:T(8,128)S(1)}, u32[]{:S(2)}, u32[]{:S(2)}) collective-permute-start(f32[64,1280]{1,0:T(8,128)S(1)} %get-tuple-element.66), channel_id=1, source_target_pairs={{0,6},{1,25},{2,0},{3,27},{4,2},{5,29},{6,4},{7,31},{8,14},{9,1},{... | collective-permute-start | bytes 983048 | tf_op jit(solution)/shard_map/ppermute | solution.py:33
  105.9 11.8 %collective-permute-start.20 = (f32[64,1280]{1,0:T(8,128)S(1)}, f32[64,1280]{1,0:T(8,128)S(1)}, u32[]{:S(2)}, u32[]{:S(2)}) collective-permute-start(f32[64,1280]{1,0:T(8,128)S(1)} %get-tuple-element.67), channel_id=1, source_target_pairs={{0,2},{1,9},{2,4},{3,11},{4,6},{5,13},{6,0},{7,15},{8,10},{9,17},{... | collective-permute-start | bytes 983048 | tf_op jit(solution)/shard_map/ppermute | solution.py:33
  105.9 11.8 %collective-permute-start.21 = (f32[64,1280]{1,0:T(8,128)S(1)}, f32[64,1280]{1,0:T(8,128)S(1)}, u32[]{:S(2)}, u32[]{:S(2)}) collective-permute-start(f32[64,1280]{1,0:T(8,128)S(1)} %get-tuple-element.68), channel_id=1, source_target_pairs={{0,4},{1,17},{2,6},{3,19},{4,0},{5,21},{6,2},{7,23},{8,12},{9,25},... | collective-permute-start | bytes 983048 | tf_op jit(solution)/shard_map/ppermute | solution.py:33
  116.3 2.2 %collective-permute-start.24 = (f32[64,1280]{1,0:T(8,128)S(1)}, f32[64,1280]{1,0:T(8,128)S(1)}, u32[]{:S(2)}, u32[]{:S(2)}) collective-permute-start(f32[64,1280]{1,0:T(8,128)S(1)} %get-tuple-element.75), channel_id=1, source_target_pairs={{0,1},{1,0},{2,3},{3,2},{4,5},{5,4},{6,7},{7,6},{8,9},{9,8},{10,11... | collective-permute-start | bytes 983048 | tf_op jit(solution)/shard_map/ppermute | solution.py:33
  (7 other events, 116.1 us)

commit v3 on v2

--- a/solution.py
+++ b/solution.py
@@ -1,3 +1,5 @@
+import functools
+
 import jax
 import jax.numpy as jnp
 from jax import lax
@@ -10,6 +12,7 @@
 sizes = {"z": 8, "x": 4, "y": 4, "core": 2}
 every = tuple(sizes)
 offsets = (0, -1, 1, 2)
+steps = (-3, 3, 4, -1, -2, 1, 2, 0)
 vmem_bytes = 24 * 1024 * 1024
 in_vmem = pl.BlockSpec(memory_space=pltpu.VMEM)
 in_smem = pl.BlockSpec(memory_space=pltpu.SMEM)
@@ -63,29 +66,24 @@
     return jnp.where(place[0] == 0, second * 4 + first, first * 4 + second)
 
 
+def chunk_place(place, chunk):
+    core = place[0]
+    z = (place[3] + (2 * core - 1) * steps[chunk]) & 7
+    return z, (1 - core if steps[chunk] < 0 else core) == 1
+
+
 def scores_kernel(place, *refs):
     groups, pieces = refs[:4], refs[4:10]
-    scores_out, texts_out, kept, sent, scores, texts, rows_out, sems = refs[10:]
-    core, z = place[0], place[3]
-    own, other = pieces[0], pieces[1]
+    scores_out, texts_out, kept, sent, scores, texts, rows_out, cols_out, sems = refs[10:]
+    own, other, near, far, other_near, other_far = pieces
     half = own.shape[0]
     pair = 2 * half
-    side = 2 * core - 1
-
-    def put(value, step, whose):
-        start = pl.multiple_of(((z + step) & 7) * pair + whose * half, half)
-        texts[pl.ds(start, half), :] = value
-
-    put(own[...], 0, core)
-    put(other[...], 0, 1 - core)
-    for near, far, steps, whose in (
-        (pieces[2], pieces[3], side, core),
-        (pieces[4], pieces[5], -side, 1 - core),
+    start = 0
+    for piece in (
+        other_far[:pair], far[:pair], far[pair:], other_far[pair:], other_near[...], near[...], own[...], other[...]
     ):
-        for k, piece in ((1, near[:pair]), (2, near[pair:]), (3, far[:pair])):
-            put(piece[:half], steps * k, whose)
-            put(piece[half:], steps * k, 1 - whose)
-        put(far[pair:], 4, whose)
+        texts[start : start + piece.shape[0], :] = piece
+        start += piece.shape[0]
 
     rows_here = groups[0].shape[0]
     copies = [pltpu.make_async_copy(texts, texts_out, sems.at[4])]
@@ -115,13 +113,15 @@
         col_top, col_sum = new, total
 
     col = col_top + jnp.log(col_sum)
-    first = core == 0
-    for i in range(kept.shape[0]):
-        row_here = rows_out[i : i + 1, :]
-        k = i % (col.shape[1] // lanes)
-        col_here = col[:, k * lanes : (k + 1) * lanes]
-        kept[i : i + 1, :] = jnp.where(first, col_here, row_here)
-        sent[i : i + 1, :] = jnp.where(first, row_here, col_here)
+    cols_out[...] = jnp.zeros(cols_out.shape, f32)
+    for chunk in range(len(steps)):
+        z, turned = chunk_place(place, chunk)
+        tile = jnp.broadcast_to(col[:, chunk * lanes : (chunk + 1) * lanes], (8, lanes))
+        tile = jnp.where(turned, pltpu.roll(tile, half, 1), tile)
+        cols_out[pl.ds(z, 1), :] = tile[:1]
+    first = place[0] == 0
+    kept[...] = jnp.where(first, cols_out[...], rows_out[...])
+    sent[...] = jnp.where(first, rows_out[...], cols_out[...])
     for copy in copies:
         copy.wait()
 
@@ -145,6 +145,7 @@
             pltpu.VMEM((rows, cols), f32),
             pltpu.VMEM((cols, width), bf16),
             pltpu.VMEM(tile, f32),
+            pltpu.VMEM(tile, f32),
             pltpu.SemaphoreType.DMA((5,)),
         ],
         compiler_params=pltpu.CompilerParams(vmem_limit_bytes=vmem_bytes),
@@ -210,23 +211,35 @@
     )(place, parts)
 
 
+def text_product(dscores, columns, images):
+    return lax.dot_general(
+        dscores[:, columns], images, (((0,), (0,)), ((), ())), preferred_element_type=f32
+    )
+
+
 def dscores_kernel(
-    place, scores_in, kept, received, labels, g0, g1, g2, g3, dscores, mine, theirs, scores, total, targets, sems
+    place, scores_in, kept, received, labels, g0, g1, g2, g3, dscores, mine, theirs, scores, targets, sems
 ):
-    core, z = place[0], place[3]
+    core, z, spot = place[0], place[3], place[5]
     first = core == 0
     half = lanes // 2
     rows_here = g0.shape[0]
-    cols = scores.shape[1]
     copies = []
     for i in range(4):
         here = pl.ds(i * rows_here, rows_here)
         copies.append(pltpu.make_async_copy(scores_in.at[here], scores.at[here], sems.at[i]))
         copies[-1].start()
+
     label = labels[...]
-    spot = place[5]
-    target = jnp.where((label >> 7) & 15 == spot, (label >> 11) * lanes + (label & 127), -1).astype(f32)
-    target = jnp.where(first, target, pltpu.roll(target, half, 1))
+    step = ((2 * core - 1) * ((label >> 11) - z)) & 7
+    chunk = jnp.zeros(label.shape, jnp.int32)
+    for i in range(1, len(steps)):
+        chunk = jnp.where(step == (steps[i] & 7), i, chunk)
+    leading = jnp.where(step > 4, 1 - core, core)
+    target = chunk * lanes + jnp.where((label >> 6) & 1 == leading, 0, half) + (label & (half - 1))
+    target = jnp.where((label >> 7) & 15 == spot, target, -1).astype(f32)
+    targets[...] = jnp.where(first, target, pltpu.roll(target, half, 1))
+
     lane_row = lax.broadcasted_iota(jnp.int32, (8, lanes), 1)
     lane = lax.broadcasted_iota(jnp.int32, (lanes, lanes), 1).astype(f32)
 
@@ -239,69 +252,89 @@
     def row_lse(k):
         return jnp.where(first, received[pl.ds(k, 1), :], kept[pl.ds(k, 1), :])
 
-    targets[...] = target
-
     def target_of(k):
         return targets[pl.ds(k, 1), :]
 
-    col_lse = jnp.where(first, kept[...], received[...])
+    col_lse = []
+    for i in range(len(steps)):
+        k, turned = chunk_place(place, i)
+        tile = jnp.where(first, kept[pl.ds(k, 1), :], received[pl.ds(k, 1), :])
+        tile = jnp.broadcast_to(tile, (8, lanes))
+        col_lse.append(jnp.where(turned, pltpu.roll(tile, half, 1), tile)[:1])
     for i in range(4):
         copies[i].wait()
         for j in (0, 2):
             row = column(row_lse, i, j)
             wanted = column(target_of, i, j)
             here = slice(i * rows_here + j * half, i * rows_here + j * half + lanes)
-            for chunk in range(cols // lanes):
+            for chunk in range(len(steps)):
                 part = slice(chunk * lanes, (chunk + 1) * lanes)
                 s = scores[here, part]
                 match = jnp.where(wanted == lane + float(chunk * lanes), 2.0, 0.0)
-                dscores[here, part] = (
-                    jnp.exp(s - row) + jnp.exp(s - col_lse[chunk : chunk + 1]) - match
-                ).astype(bf16)
+                dscores[here, part] = (jnp.exp(s - row) + jnp.exp(s - col_lse[chunk]) - match).astype(bf16)
 
     images = jnp.concatenate([g0[...], g1[...], g2[...], g3[...]], axis=0)
-    total[...] = lax.dot_general(
-        dscores[...], images, (((0,), (0,)), ((), ())), preferred_element_type=f32
-    )
-    side = 1 - 2 * core
-
-    def take(step, offset, size):
-        return total[pl.ds(pl.multiple_of(((z + step) & 7) * lanes + offset, half), size), :]
-
-    for k in range(1, 4):
-        here = slice((k - 1) * lanes, k * lanes)
-        mine[here, :] = take(side * k, 0, lanes)
-        theirs[here, :] = take(-side * k, 0, lanes).astype(bf16)
-    for k, step in ((6, 4), (7, 0)):
-        here = slice(k * half, (k + 1) * half)
-        mine[here, :] = take(step, core * half, half)
-        theirs[here, :] = take(step, (1 - core) * half, half).astype(bf16)
+    far = text_product(dscores, slice(0, 3 * lanes), images)
+    mine[:lanes, :] = far[:lanes]
+    mine[lanes:, :] = far[2 * lanes : 2 * lanes + half]
+    theirs[:lanes, :] = far[lanes : 2 * lanes].astype(bf16)
+    theirs[lanes:, :] = far[2 * lanes + half :].astype(bf16)
 
 
 def local_dscores(place, scores, kept, received, labels, groups):
     rows, cols = scores.shape
     width = groups[0].shape[1]
+    part = cols // 16 * 3
+    scores = pltpu.with_memory_space_constraint(scores, pltpu.MemorySpace.HBM)
     return pl.pallas_call(
         dscores_kernel,
         in_specs=[in_smem, in_hbm] + [in_vmem] * 7,
         out_specs=[in_vmem] * 3,
         out_shape=[
             pltpu.VMEM((rows, cols), bf16),
-            pltpu.VMEM((cols // 2, width), f32),
-            pltpu.VMEM((cols // 2, width), bf16),
+            pltpu.VMEM((part, width), f32),
+            pltpu.VMEM((part, width), bf16),
         ],
         scratch_shapes=[
             pltpu.VMEM((rows, cols), f32),
-            pltpu.VMEM((cols, width), f32),
             pltpu.VMEM(labels.shape, f32),
             pltpu.SemaphoreType.DMA((4,)),
         ],
         compiler_params=pltpu.CompilerParams(vmem_limit_bytes=vmem_bytes),
         cost_estimate=pl.CostEstimate(
-            flops=2 * rows * cols * width, bytes_accessed=6_000_000, transcendentals=2 * rows * cols
+            flops=rows * cols * width, bytes_accessed=6_000_000, transcendentals=2 * rows * cols
         ),
         name="dscores",
     )(place, scores, kept, received, labels, *groups)
+
+
+def near_kernel(dscores, g0, g1, g2, g3, after, mine, t1, t2, t3):
+    half = lanes // 2
+    images = jnp.concatenate([g0[...], g1[...], g2[...], g3[...]], axis=0)
+    near = text_product(dscores, slice(3 * lanes, dscores.shape[1]), images)
+    mine[: 2 * lanes, :] = near[: 2 * lanes]
+    mine[2 * lanes :, :] = near[4 * lanes : 4 * lanes + half]
+    t1[...] = near[2 * lanes : 3 * lanes].astype(bf16)
+    t2[...] = near[3 * lanes : 4 * lanes].astype(bf16)
+    t3[...] = near[4 * lanes + half :].astype(bf16)
+
+
+def near_texts(dscores, groups, after):
+    rows, cols = dscores.shape
+    width = groups[0].shape[1]
+    part = cols // 16 * 5
+    return pl.pallas_call(
+        near_kernel,
+        in_specs=[in_vmem] * 6,
+        out_specs=[in_vmem] * 4,
+        out_shape=[pltpu.VMEM((part, width), f32)]
+        + [pltpu.VMEM((n, width), bf16) for n in (lanes, lanes, lanes // 2)],
+        compiler_params=pltpu.CompilerParams(vmem_limit_bytes=vmem_bytes),
+        cost_estimate=pl.CostEstimate(
+            flops=2 * rows * cols * width, bytes_accessed=6_000_000, transcendentals=0
+        ),
+        name="near_texts",
+    )(dscores, *groups, after)
 
 
 def product_kernel(dscores, texts, *outs):
@@ -328,104 +361,96 @@
     )(dscores, texts)
 
 
-def add_text_kernel(mine, received, near, far, own):
-    start = 0
-    for out in (near, far, own):
-        here = slice(start, start + out.shape[0])
-        out[...] = (mine[here, :] + received[here, :].astype(f32)).astype(out.dtype)
-        start += out.shape[0]
-
-
-def add_text(mine, received):
+def add_far_kernel(mine, received, out):
+    out[...] = (mine[...] + received[...].astype(f32)).astype(bf16)
+
+
+def add_far(mine, received):
+    return pl.pallas_call(
+        add_far_kernel,
+        in_specs=[in_vmem] * 2,
+        out_specs=in_vmem,
+        out_shape=pltpu.VMEM(mine.shape, bf16),
+        compiler_params=pltpu.CompilerParams(vmem_limit_bytes=vmem_bytes),
+        cost_estimate=pl.CostEstimate(flops=mine.size, bytes_accessed=8 * mine.size, transcendentals=0),
+        name="text_far",
+    )(mine, received)
+
+
+def relay_text_kernel(mine, t1, t2, t3, far, one, two, own):
+    pair, half = one.shape[0], own.shape[0]
+
+    one[...] = (mine[:pair, :] + t1[...].astype(f32) + far[:pair, :].astype(f32)).astype(bf16)
+    second = mine[pair : 2 * pair, :] + t2[...].astype(f32)
+    two[:half, :] = second[:half].astype(bf16)
+    two[half:, :] = (second[half:] + far[pair:, :].astype(f32)).astype(bf16)
+    own[...] = mine[2 * pair :, :] + t3[...].astype(f32)
+
+
+def relay_text(mine, received, far):
     rows, width = mine.shape
-    shapes = [(rows // 2, f32), (rows // 8 * 3, bf16), (rows // 8, f32)]
-    return pl.pallas_call(
-        add_text_kernel,
-        in_specs=[in_vmem] * 2,
+    pair = rows // 5 * 2
+    return pl.pallas_call(
+        relay_text_kernel,
+        in_specs=[in_vmem] * 5,
         out_specs=[in_vmem] * 3,
-        out_shape=[pltpu.VMEM((n, width), kind) for n, kind in shapes],
-        compiler_params=pltpu.CompilerParams(vmem_limit_bytes=vmem_bytes),
-        cost_estimate=pl.CostEstimate(flops=rows * width, bytes_accessed=6 * rows * width, transcendentals=0),
-        name="text_add",
-    )(mine, received)
-
-
-def relay_text_kernel(place, near, received, one, two):
-    pair, half = one.shape[0], one.shape[0] // 2
-    one[...] = (near[:pair] + received[:pair].astype(f32)).astype(bf16)
-    two[...] = near[pair:].astype(bf16)
-    here = pl.multiple_of(place[0] * half, half)
-    two[pl.ds(here, half), :] = (
-        near[pl.ds(pair + here, half), :] + received[pair:].astype(f32)
-    ).astype(bf16)
-
-
-def relay_text(place, near, received):
-    rows, width = near.shape
-    return pl.pallas_call(
-        relay_text_kernel,
-        in_specs=[in_smem] + [in_vmem] * 2,
-        out_specs=[in_vmem] * 2,
-        out_shape=[pltpu.VMEM((rows // 2, width), bf16)] * 2,
-        compiler_params=pltpu.CompilerParams(vmem_limit_bytes=vmem_bytes),
-        cost_estimate=pl.CostEstimate(flops=rows * width, bytes_accessed=6 * rows * width, transcendentals=0),
+        out_shape=[
+            pltpu.VMEM((pair, width), bf16),
+            pltpu.VMEM((pair, width), bf16),
+            pltpu.VMEM((pair // 2, width), f32),
+        ],
+        compiler_params=pltpu.CompilerParams(vmem_limit_bytes=vmem_bytes),
+        cost_estimate=pl.CostEstimate(flops=10_000_000_000, bytes_accessed=10 * mine.size, transcendentals=0),
         name="text_relay",
-    )(place, near, received)
-
-
-def split_text_kernel(place, one, two, own, here, there):
+    )(mine, *received, far)
+
+
+def split_text_kernel(one, two, own, here, there):
     half = own.shape[0]
-    core = place[0]
-
-    def total(which):
-        rows = pl.ds(pl.multiple_of(which * half, half), half)
-        return one[rows, :].astype(f32) + two[rows, :].astype(f32)
-
-    here[...] = total(core) + own[...]
-    there[...] = total(1 - core)
-
-
-def split_text(place, one, two, own):
+    here[...] = one[half:, :].astype(f32) + two[half:, :].astype(f32) + own[...]
+    there[...] = one[:half, :].astype(f32) + two[:half, :].astype(f32)
+
+
+def split_text(one, two, own):
     return pl.pallas_call(
         split_text_kernel,
-        in_specs=[in_smem] + [in_vmem] * 3,
+        in_specs=[in_vmem] * 3,
         out_specs=[in_vmem] * 2,
         out_shape=[pltpu.VMEM(own.shape, f32)] * 2,
         compiler_params=pltpu.CompilerParams(vmem_limit_bytes=vmem_bytes),
         cost_estimate=pl.CostEstimate(flops=4 * own.size, bytes_accessed=20 * own.size, transcendentals=0),
         name="text_split",
-    )(place, one, two, own)
-
-
-def join_kernel(*refs):
+    )(one, two, own)
+
+
+def join_kernel(count, *refs):
     out = refs[-1]
     start = 0
-    for ref in refs[:-1]:
+    for ref in refs[:count]:
         size = min(ref.shape[0], out.shape[0] - start)
         out[start : start + size, :] = ref[:size, :]
         start += size
 
 
-def join(rows, *parts):
+def join(rows, *parts, after=()):
     width = parts[0].shape[1]
     return pl.pallas_call(
-        join_kernel,
-        in_specs=[in_vmem] * len(parts),
+        functools.partial(join_kernel, len(parts)),
+        in_specs=[in_vmem] * (len(parts) + len(after)),
         out_specs=in_vmem,
         out_shape=pltpu.VMEM((rows, width), bf16),
         compiler_params=pltpu.CompilerParams(vmem_limit_bytes=vmem_bytes),
         cost_estimate=pl.CostEstimate(flops=0, bytes_accessed=4 * rows * width, transcendentals=0),
         name="join",
-    )(*parts)
+    )(*parts, *after)
 
 
 def add_image_kernel(p0, p1, p2, p3, *outs):
     size = outs[0].shape[0]
     for j in range(4):
         here = slice(j * size, (j + 1) * size)
-        outs[j][...] = (
-            p0[here, :] + p1[here, :].astype(f32) + p2[here, :].astype(f32) + p3[here, :].astype(f32)
-        )
+        total = p0[here, :] + p1[here, :].astype(f32) + p2[here, :].astype(f32) + p3[here, :].astype(f32)
+        outs[j][...] = total.astype(outs[j].dtype)
 
 
 def add_image(parts):
@@ -434,7 +459,7 @@
         add_image_kernel,
         in_specs=[in_vmem] * 4,
         out_specs=[in_vmem] * 4,
-        out_shape=[pltpu.VMEM((rows // 4, width), f32)] * 4,
+        out_shape=[pltpu.VMEM((rows // 4, width), bf16 if j else f32) for j in range(4)],
         compiler_params=pltpu.CompilerParams(vmem_limit_bytes=vmem_bytes),
         cost_estimate=pl.CostEstimate(
             flops=4 * rows * width, bytes_accessed=14 * rows * width, transcendentals=0
@@ -443,18 +468,42 @@
     )(*parts)
 
 
+def load_kernel(a, b, a_out, b_out, sems):
+    copies = [pltpu.make_async_copy(a, a_out, sems.at[0]), pltpu.make_async_copy(b, b_out, sems.at[1])]
+    for copy in copies:
+        copy.start()
+    for copy in copies:
+        copy.wait()
+
+
+def load(a, b):
+    return pl.pallas_call(
+        load_kernel,
+        in_specs=[in_hbm] * 2,
+        out_specs=[in_vmem] * 2,
+        out_shape=[pltpu.VMEM(a.shape, a.dtype), pltpu.VMEM(b.shape, b.dtype)],
+        scratch_shapes=[pltpu.SemaphoreType.DMA((2,))],
+        compiler_params=pltpu.CompilerParams(vmem_limit_bytes=vmem_bytes),
+        cost_estimate=pl.CostEstimate(flops=0, bytes_accessed=4 * a.size, transcendentals=0),
+        name="load",
+    )(
+        pltpu.with_memory_space_constraint(a, pltpu.MemorySpace.HBM),
+        pltpu.with_memory_space_constraint(b, pltpu.MemorySpace.HBM),
+    )
+
+
 def gather(image_embeds, text_embeds):
     block = image_embeds.shape[0]
     line = [send_first(image_embeds, -k) for k in offsets[1:]]
     other = swap_cores(text_embeds)
+    image_embeds, text_embeds = load(image_embeds, text_embeds)
     pair = join(2 * block, text_embeds, other)
     near = [send_z(pair, 2), send_z(pair, 1)]
-    line, near = lax.optimization_barrier((line, near))
     line = join(4 * block, image_embeds, *line)
-    ahead = join(3 * block, near[1], near[0])
+    ahead = join(3 * block, near[1], near[0], after=(line,))
     groups = [line] + [send_second(line, -k) for k in offsets[1:]]
     far = send_z(ahead, 2)
-    near = join(4 * block, near[1], near[0])
+    near = join(4 * block, near[1], near[0], after=(line,))
     pieces = [text_embeds, other, near, far, swap_cores(near), swap_cores(far)]
     return groups, pieces
 
@@ -480,17 +529,16 @@
     )
     theirs = swap_cores(theirs)
     terms = product(dscores, texts)
-    near, far, own = add_text(mine, theirs)
-    far = send_z(far, 2)
+    far = send_z(add_far(mine, theirs), 2)
     parts = [send_second(t, k) for t, k in zip(terms[1:], offsets[1:])]
-    far, parts = lax.optimization_barrier((far, parts))
-    one, two = relay_text(place, near, far)
+    mine, *theirs = near_texts(dscores, groups, terms[0])
+    one, two, own = relay_text(mine, [swap_cores(t) for t in theirs], far)
     terms = add_image([terms[0]] + parts)
     two, one = send_z(two, 2), send_z(one, 1)
     image_parts = [terms[0]] + [send_first(t, k) for t, k in zip(terms[1:], offsets[1:])]
-    here, there = split_text(place, one, two, own)
+    here, there = split_text(one, two, own)
     text_grad = (score_scale * (here + swap_cores(there))).astype(bf16)
-    image_total = image_parts[0] + image_parts[1] + image_parts[2] + image_parts[3]
+    image_total = sum(part.astype(f32) for part in image_parts)
     image_grad = (score_scale * image_total).astype(bf16)
     return (image_grad, text_grad)
 

time: 120 us -> 113 us (0.942)
  waiting for transfers between devices: 48.2 us -> 43.9 us
  local copies, waits for them, and re-layouts: 3.21 us -> 0.09 us
  blocking collectives: 16.2 us -> 14.7 us
  starting transfers between devices: 31.8 us -> 33.3 us
    ppermute x25 -> x28, waiting for transfers between devices: 48.2 us -> 43.9 us  [send(): return lax.ppermute(value, every, pairs)]
    unnamed x12 -> x4, local copies, waits for them, and re-layouts: 3.12 us -> 0.01 us
    pallas_call x7 -> x9, Pallas kernels: 1.67 us -> 3.44 us  [the longest x1 1.93 us: near_texts(): pl.pallas_call(near_kernel, in_specs=[in_vmem] * 6, out_specs=[in_vmem] *...]
    ppermute x25 -> x28, starting transfers between devices: 31.8 us -> 33.3 us  [send(): return lax.ppermute(value, every, pairs)]
    all_to_all x1, blocking collectives: 16.2 us -> 14.7 us  [shards(): lax.all_to_all(parts.reshape(-1, lanes), every, 0, 0, axis_index_groups=s...]
  transfers between devices with their start and end apart: 25 -> 28, of which waited for: 13 -> 13; matrix products, arithmetic and copies ran while one was open for 1% -> 1% of each run, Pallas kernels for 3% -> 6%
where the time goes in v3:
time: 113 us
  waiting for transfers between devices  43.9 us (39%)
  starting transfers between devices  33.3 us (29%)
  Pallas kernels  18.2 us (16%)
  blocking collectives  14.7 us (13%)
  other arithmetic  1.46 us (1%)
    ppermute x28, waiting for transfers between devices, send(): return lax.ppermute(value, every, pairs)  43.9 us
    ppermute x28, starting transfers between devices, send(): return lax.ppermute(value, every, pairs)  33.3 us
    all_to_all x1, blocking collectives, shards(): lax.all_to_all(parts.reshape(-1, lanes), every, 0, 0, axis_index_groups=s...  14.7 us
    pallas_call x1, Pallas kernels, local_dscores(): pl.pallas_call(dscores_kernel, in_specs=[in_smem, in_hbm] + [in_vmem] * 7...  5.3 us
    pallas_call x1, Pallas kernels, local_scores(): pl.pallas_call(scores_kernel, in_specs=[in_smem] + [in_vmem] * 10, out_sp...  5.14 us
    pallas_call x1, Pallas kernels, product(): pl.pallas_call(product_kernel, in_specs=[in_vmem] * 2, out_specs=[in_vmem...  2.87 us
  transfers between devices with their start and end apart: 28, of which 13 were waited for; matrix products, arithmetic and copies ran while one was open for 1% of the time, Pallas kernels for 6%

profile of v3, /device:TPU:32, one launch (start us, length us, event | category | flops | bytes accessed | tf_op | source)
XLA Modules:
  0.0 112.6 jit_solution(79313311213192533)
XLA Ops:
  2.4 3.3 %collective-permute-start.8 = (bf16[128,1280]{1,0:T(8,128)(2,1)S(1)}, bf16[128,1280]{1,0:T(8,128)(2,1)S(1)}, u32[]{:S(2)}, u32[]{:S(2)}) collective-permute-start(bf16[128,1280]{1,0:T(8,128)(2,1)S(1)} %join.5), channel_id=1, source_target_pairs={{0,64},{1,193},{2,66},{3,195},{4,68},{5,197},{6,70},{7,199},{8,72}... | collective-permute-start | bytes 983048 | tf_op jit(solution)/shard_map/ppermute | solution.py:36
  5.7 3.1 %collective-permute-start.7 = (bf16[128,1280]{1,0:T(8,128)(2,1)S(1)}, bf16[128,1280]{1,0:T(8,128)(2,1)S(1)}, u32[]{:S(2)}, u32[]{:S(2)}) collective-permute-start(bf16[128,1280]{1,0:T(8,128)(2,1)S(1)} %join.5), channel_id=1, source_target_pairs={{0,32},{1,225},{2,34},{3,227},{4,36},{5,229},{6,38},{7,231},{8,40}... | collective-permute-start | bytes 983048 | tf_op jit(solution)/shard_map/ppermute | solution.py:36
  8.9 3.2 %collective-permute-start.2 = (bf16[64,1280]{1,0:T(8,128)(2,1)}, bf16[64,1280]{1,0:T(8,128)(2,1)S(1)}, u32[]{:S(2)}, u32[]{:S(2)}) collective-permute-start(bf16[64,1280]{1,0:T(8,128)(2,1)} %a), channel_id=1, source_target_pairs={{0,4},{1,17},{2,6},{3,19},{4,0},{5,21},{6,2},{7,23},{8,12},{9,25},... | collective-permute-start | bytes 491528 | tf_op jit(solution)/shard_map/ppermute | solution.py:36
  14.1 1.8 %collective-permute-done.2.refs_3_ = bf16[64,1280]{1,0:T(8,128)(2,1)S(1)} collective-permute-done((bf16[64,1280]{1,0:T(8,128)(2,1)}, bf16[64,1280]{1,0:T(8,128)(2,1)S(1)}, u32[]{:S(2)}, u32[]{:S(2)}) %collective-permute-start.2) | collective-permute-done | bytes 163872 | tf_op jit(solution)/shard_map/ppermute | solution.py:36
  15.9 2.1 %collective-permute-done.1.refs_2_ = bf16[64,1280]{1,0:T(8,128)(2,1)S(1)} collective-permute-done((bf16[64,1280]{1,0:T(8,128)(2,1)}, bf16[64,1280]{1,0:T(8,128)(2,1)S(1)}, u32[]{:S(2)}, u32[]{:S(2)}) %collective-permute-start.1) | collective-permute-done | bytes 163872 | tf_op jit(solution)/shard_map/ppermute | solution.py:36
  18.0 1.9 %collective-permute-done.refs_1_ = bf16[64,1280]{1,0:T(8,128)(2,1)S(1)} collective-permute-done((bf16[64,1280]{1,0:T(8,128)(2,1)}, bf16[64,1280]{1,0:T(8,128)(2,1)S(1)}, u32[]{:S(2)}, u32[]{:S(2)}) %collective-permute-start) | collective-permute-done | bytes 163872 | tf_op jit(solution)/shard_map/ppermute | solution.py:36
  20.0 2.5 %collective-permute-start.9 = (bf16[192,1280]{1,0:T(8,128)(2,1)S(1)}, bf16[192,1280]{1,0:T(8,128)(2,1)S(1)}, u32[]{:S(2)}, u32[]{:S(2)}) collective-permute-start(bf16[192,1280]{1,0:T(8,128)(2,1)S(1)} %join.7), channel_id=1, source_target_pairs={{0,64},{1,193},{2,66},{3,195},{4,68},{5,197},{6,70},{7,199},{8,72}... | collective-permute-start | bytes 1474568 | tf_op jit(solution)/shard_map/ppermute | solution.py:36
  22.5 3.0 %collective-permute-start.5 = (bf16[256,1280]{1,0:T(8,128)(2,1)S(1)}, bf16[256,1280]{1,0:T(8,128)(2,1)S(1)}, u32[]{:S(2)}, u32[]{:S(2)}) collective-permute-start(bf16[256,1280]{1,0:T(8,128)(2,1)S(1)} %join.4.refs_2_.refs_0_.g0), channel_id=1, source_target_pairs={{0,16},{1,5},{2,18},{3,7},{4,20},{5,1},{6,22},{7,3},{8,24},{9,13},... | collective-permute-start | bytes 1966088 | tf_op jit(solution)/shard_map/ppermute | solution.py:36
  27.7 8.6 %collective-permute-done.9.refs_7_ = bf16[192,1280]{1,0:T(8,128)(2,1)S(1)} collective-permute-done((bf16[192,1280]{1,0:T(8,128)(2,1)S(1)}, bf16[192,1280]{1,0:T(8,128)(2,1)S(1)}, u32[]{:S(2)}, u32[]{:S(2)}) %collective-permute-start.9) | collective-permute-done | bytes 491552 | tf_op jit(solution)/shard_map/ppermute | solution.py:36
  36.3 5.4 %collective-permute-done.4.refs_2_.g2 = bf16[256,1280]{1,0:T(8,128)(2,1)S(1)} collective-permute-done((bf16[256,1280]{1,0:T(8,128)(2,1)S(1)}, bf16[256,1280]{1,0:T(8,128)(2,1)S(1)}, u32[]{:S(2)}, u32[]{:S(2)}) %collective-permute-start.4) | collective-permute-done | bytes 655392 | tf_op jit(solution)/shard_map/ppermute | solution.py:36
  41.7 5.1 %scores.1 = (f32[1024,1024]{1,0:T(8,128)}, bf16[1024,1280]{1,0:T(8,128)(2,1)}, f32[16,128]{1,0:T(8,128)S(1)}, f32[16,128]{1,0:T(8,128)S(1)}) custom-call(s32[6]{0:T(128)S(1)} %stack.27.place, bf16[256,1280]{1,0:T(8,128)(2,1)S(1)} %join.4.refs_2_.refs_0_.g0, bf16[256,1280]{1,0:T(8,128)(2,1)S(1)} %collective-permute-done.3.refs_1_.g1, ...), custom_call_target="tpu_custom_call" | custom-call | flops 2684354560 | bytes 6000000 | tf_op jit(solution)/shard_map/scores/pallas_call | solution.py:134
  47.1 1.2 %collective-permute-done.12.received = f32[16,128]{1,0:T(8,128)S(1)} collective-permute-done((f32[16,128]{1,0:T(8,128)S(1)}, f32[16,128]{1,0:T(8,128)S(1)}, u32[]{:S(2)}, u32[]{:S(2)}) %collective-permute-start.12) | collective-permute-done | bytes 8224 | tf_op jit(solution)/shard_map/ppermute | solution.py:36
  48.9 14.7 %all_to_all.9 = f32[16,32,128]{2,1,0:T(8,128)S(1)} all-to-all(f32[16,32,128]{2,1,0:T(8,128)S(1)} %bitcast.10), channel_id=1, replica_groups={{0,32,64,96,128,160,192,224,8,40,72,104,136,168,200,232},{2,34,66,98,13..., dimensions={0} | all-to-all | bytes 524288 | tf_op jit(solution)/shard_map/all_to_all | solution.py:521
  65.5 5.3 %dscores.1 = (bf16[1024,1024]{1,0:T(8,128)(2,1)S(1)}, f32[192,1280]{1,0:T(8,128)S(1)}, bf16[192,1280]{1,0:T(8,128)(2,1)S(1)}) custom-call(s32[6]{0:T(128)S(1)} %stack.27.place, f32[1024,1024]{1,0:T(8,128)} %get-tuple-element.39.scores_in, f32[16,128]{1,0:T(8,128)S(1)} %get-tuple-element.42.kept, f32[16,128]{1,0:T(8,128)S(1)} %collective-permute-done.13.received, ...), custom_call_target="tpu_custom_call" | custom-call | flops 1342177280 | bytes 6000000 | tf_op jit(solution)/shard_map/dscores/pallas_call | solution.py:289
  71.1 2.9 %image_product.1 = (f32[256,1280]{1,0:T(8,128)S(1)}, bf16[256,1280]{1,0:T(8,128)(2,1)S(1)}, bf16[256,1280]{1,0:T(8,128)(2,1)S(1)}, bf16[256,1280]{1,0:T(8,128)(2,1)S(1)}) custom-call(bf16[1024,1024]{1,0:T(8,128)(2,1)S(1)} %get-tuple-element.45.dscores, bf16[1024,1280]{1,0:T(8,128)(2,1)S(1)} %copy-done.1), custom_call_target="tpu_custom_call" | custom-call | flops 2684354560 | bytes 6000000 | tf_op jit(solution)/shard_map/image_product/pallas_call | solution.py:351
  75.1 1.9 %near_texts.1 = (f32[320,1280]{1,0:T(8,128)S(1)}, bf16[128,1280]{1,0:T(8,128)(2,1)S(1)}, bf16[128,1280]{1,0:T(8,128)(2,1)S(1)}, bf16[64,1280]{1,0:T(8,128)(2,1)S(1)}) custom-call(bf16[1024,1024]{1,0:T(8,128)(2,1)S(1)} %get-tuple-element.45.dscores, bf16[256,1280]{1,0:T(8,128)(2,1)S(1)} %join.4.refs_2_.refs_0_.g0, ...), custom_call_target="tpu_custom_call" | custom-call | flops 2684354560 | bytes 6000000 | tf_op jit(solution)/shard_map/near_texts/pallas_call | solution.py:326
  78.2 2.5 %collective-permute-start.14 = (bf16[256,1280]{1,0:T(8,128)(2,1)S(1)}, bf16[256,1280]{1,0:T(8,128)(2,1)S(1)}, u32[]{:S(2)}, u32[]{:S(2)}) collective-permute-start(bf16[256,1280]{1,0:T(8,128)(2,1)S(1)} %get-tuple-element.48), channel_id=1, source_target_pairs={{0,24},{1,7},{2,26},{3,1},{4,28},{5,3},{6,30},{7,5},{8,0},{9,15},{... | collective-permute-start | bytes 1966088 | tf_op jit(solution)/shard_map/ppermute | solution.py:36
  80.9 2.7 %collective-permute-start.16 = (bf16[256,1280]{1,0:T(8,128)(2,1)S(1)}, bf16[256,1280]{1,0:T(8,128)(2,1)S(1)}, u32[]{:S(2)}, u32[]{:S(2)}) collective-permute-start(bf16[256,1280]{1,0:T(8,128)(2,1)S(1)} %get-tuple-element.50), channel_id=1, source_target_pairs={{0,16},{1,5},{2,18},{3,7},{4,20},{5,1},{6,22},{7,3},{8,24},{9,13},... | collective-permute-start | bytes 1966088 | tf_op jit(solution)/shard_map/ppermute | solution.py:36
  83.5 6.4 %collective-permute-done.24.far = bf16[192,1280]{1,0:T(8,128)(2,1)S(1)} collective-permute-done((bf16[192,1280]{1,0:T(8,128)(2,1)S(1)}, bf16[192,1280]{1,0:T(8,128)(2,1)S(1)}, u32[]{:S(2)}, u32[]{:S(2)}) %collective-permute-start.24) | collective-permute-done | bytes 491552 | tf_op jit(solution)/shard_map/ppermute | solution.py:36
  90.5 5.3 %collective-permute-done.14.p1 = bf16[256,1280]{1,0:T(8,128)(2,1)S(1)} collective-permute-done((bf16[256,1280]{1,0:T(8,128)(2,1)S(1)}, bf16[256,1280]{1,0:T(8,128)(2,1)S(1)}, u32[]{:S(2)}, u32[]{:S(2)}) %collective-permute-start.14) | collective-permute-done | bytes 655392 | tf_op jit(solution)/shard_map/ppermute | solution.py:36
  95.8 3.7 %collective-permute-done.15.p2 = bf16[256,1280]{1,0:T(8,128)(2,1)S(1)} collective-permute-done((bf16[256,1280]{1,0:T(8,128)(2,1)S(1)}, bf16[256,1280]{1,0:T(8,128)(2,1)S(1)}, u32[]{:S(2)}, u32[]{:S(2)}) %collective-permute-start.15) | collective-permute-done | bytes 655392 | tf_op jit(solution)/shard_map/ppermute | solution.py:36
  99.7 3.1 %collective-permute-start.17 = (bf16[64,1280]{1,0:T(8,128)(2,1)S(1)}, bf16[64,1280]{1,0:T(8,128)(2,1)S(1)}, u32[]{:S(2)}, u32[]{:S(2)}) collective-permute-start(bf16[64,1280]{1,0:T(8,128)(2,1)S(1)} %get-tuple-element.52), channel_id=1, source_target_pairs={{0,6},{1,25},{2,0},{3,27},{4,2},{5,29},{6,4},{7,31},{8,14},{9,1},{... | collective-permute-start | bytes 491528 | tf_op jit(solution)/shard_map/ppermute | solution.py:36
  102.8 2.2 %collective-permute-start.19 = (bf16[64,1280]{1,0:T(8,128)(2,1)S(1)}, bf16[64,1280]{1,0:T(8,128)(2,1)S(1)}, u32[]{:S(2)}, u32[]{:S(2)}) collective-permute-start(bf16[64,1280]{1,0:T(8,128)(2,1)S(1)} %get-tuple-element.54), channel_id=1, source_target_pairs={{0,4},{1,17},{2,6},{3,19},{4,0},{5,21},{6,2},{7,23},{8,12},{9,25},... | collective-permute-start | bytes 491528 | tf_op jit(solution)/shard_map/ppermute | solution.py:36
  105.7 5.4 %collective-permute-done.18 = bf16[64,1280]{1,0:T(8,128)(2,1)S(1)} collective-permute-done((bf16[64,1280]{1,0:T(8,128)(2,1)S(1)}, bf16[64,1280]{1,0:T(8,128)(2,1)S(1)}, u32[]{:S(2)}, u32[]{:S(2)}) %collective-permute-start.18) | collective-permute-done | bytes 163872 | tf_op jit(solution)/shard_map/ppermute | solution.py:36
  (55 shorter events, 14.4 us)
Async XLA Ops:
  2.4 17.5 %collective-permute-start.8 = (bf16[128,1280]{1,0:T(8,128)(2,1)S(1)}, bf16[128,1280]{1,0:T(8,128)(2,1)S(1)}, u32[]{:S(2)}, u32[]{:S(2)}) collective-permute-start(bf16[128,1280]{1,0:T(8,128)(2,1)S(1)} %join.5), channel_id=1, source_target_pairs={{0,64},{1,193},{2,66},{3,195},{4,68},{5,197},{6,70},{7,199},{8,72}... | collective-permute-start | bytes 983048 | tf_op jit(solution)/shard_map/ppermute | solution.py:36
  5.7 14.2 %collective-permute-start.7 = (bf16[128,1280]{1,0:T(8,128)(2,1)S(1)}, bf16[128,1280]{1,0:T(8,128)(2,1)S(1)}, u32[]{:S(2)}, u32[]{:S(2)}) collective-permute-start(bf16[128,1280]{1,0:T(8,128)(2,1)S(1)} %join.5), channel_id=1, source_target_pairs={{0,32},{1,225},{2,34},{3,227},{4,36},{5,229},{6,38},{7,231},{8,40}... | collective-permute-start | bytes 983048 | tf_op jit(solution)/shard_map/ppermute | solution.py:36
  8.9 7.0 %collective-permute-start.2 = (bf16[64,1280]{1,0:T(8,128)(2,1)}, bf16[64,1280]{1,0:T(8,128)(2,1)S(1)}, u32[]{:S(2)}, u32[]{:S(2)}) collective-permute-start(bf16[64,1280]{1,0:T(8,128)(2,1)} %a), channel_id=1, source_target_pairs={{0,4},{1,17},{2,6},{3,19},{4,0},{5,21},{6,2},{7,23},{8,12},{9,25},... | collective-permute-start | bytes 491528 | tf_op jit(solution)/shard_map/ppermute | solution.py:36
  12.1 5.9 %collective-permute-start.1 = (bf16[64,1280]{1,0:T(8,128)(2,1)}, bf16[64,1280]{1,0:T(8,128)(2,1)S(1)}, u32[]{:S(2)}, u32[]{:S(2)}) collective-permute-start(bf16[64,1280]{1,0:T(8,128)(2,1)} %a), channel_id=1, source_target_pairs={{0,6},{1,25},{2,0},{3,27},{4,2},{5,29},{6,4},{7,31},{8,14},{9,1},{... | collective-permute-start | bytes 491528 | tf_op jit(solution)/shard_map/ppermute | solution.py:36
  13.1 6.7 %collective-permute-start = (bf16[64,1280]{1,0:T(8,128)(2,1)}, bf16[64,1280]{1,0:T(8,128)(2,1)S(1)}, u32[]{:S(2)}, u32[]{:S(2)}) collective-permute-start(bf16[64,1280]{1,0:T(8,128)(2,1)} %a), channel_id=1, source_target_pairs={{0,2},{1,9},{2,4},{3,11},{4,6},{5,13},{6,0},{7,15},{8,10},{9,17},{... | collective-permute-start | bytes 491528 | tf_op jit(solution)/shard_map/ppermute | solution.py:36
  20.0 16.3 %collective-permute-start.9 = (bf16[192,1280]{1,0:T(8,128)(2,1)S(1)}, bf16[192,1280]{1,0:T(8,128)(2,1)S(1)}, u32[]{:S(2)}, u32[]{:S(2)}) collective-permute-start(bf16[192,1280]{1,0:T(8,128)(2,1)S(1)} %join.7), channel_id=1, source_target_pairs={{0,64},{1,193},{2,66},{3,195},{4,68},{5,197},{6,70},{7,199},{8,72}... | collective-permute-start | bytes 1474568 | tf_op jit(solution)/shard_map/ppermute | solution.py:36
  22.5 13.8 %collective-permute-start.5 = (bf16[256,1280]{1,0:T(8,128)(2,1)S(1)}, bf16[256,1280]{1,0:T(8,128)(2,1)S(1)}, u32[]{:S(2)}, u32[]{:S(2)}) collective-permute-start(bf16[256,1280]{1,0:T(8,128)(2,1)S(1)} %join.4.refs_2_.refs_0_.g0), channel_id=1, source_target_pairs={{0,16},{1,5},{2,18},{3,7},{4,20},{5,1},{6,22},{7,3},{8,24},{9,13},... | collective-permute-start | bytes 1966088 | tf_op jit(solution)/shard_map/ppermute | solution.py:36
  25.5 16.2 %collective-permute-start.4 = (bf16[256,1280]{1,0:T(8,128)(2,1)S(1)}, bf16[256,1280]{1,0:T(8,128)(2,1)S(1)}, u32[]{:S(2)}, u32[]{:S(2)}) collective-permute-start(bf16[256,1280]{1,0:T(8,128)(2,1)S(1)} %join.4.refs_2_.refs_0_.g0), channel_id=1, source_target_pairs={{0,24},{1,7},{2,26},{3,1},{4,28},{5,3},{6,30},{7,5},{8,0},{9,15},{... | collective-permute-start | bytes 1966088 | tf_op jit(solution)/shard_map/ppermute | solution.py:36
  26.6 15.1 %collective-permute-start.3 = (bf16[256,1280]{1,0:T(8,128)(2,1)S(1)}, bf16[256,1280]{1,0:T(8,128)(2,1)S(1)}, u32[]{:S(2)}, u32[]{:S(2)}) collective-permute-start(bf16[256,1280]{1,0:T(8,128)(2,1)S(1)} %join.4.refs_2_.refs_0_.g0), channel_id=1, source_target_pairs={{0,8},{1,3},{2,10},{3,5},{4,12},{5,7},{6,14},{7,1},{8,16},{9,11},{... | collective-permute-start | bytes 1966088 | tf_op jit(solution)/shard_map/ppermute | solution.py:36
  27.6 14.1 %collective-permute-start.10 = (bf16[256,1280]{1,0:T(8,128)(2,1)S(1)}, bf16[256,1280]{1,0:T(8,128)(2,1)S(1)}, u32[]{:S(2)}, u32[]{:S(2)}) collective-permute-start(bf16[256,1280]{1,0:T(8,128)(2,1)S(1)} %join.6.refs_6_), channel_id=1, source_target_pairs={{0,1},{1,0},{2,3},{3,2},{4,5},{5,4},{6,7},{7,6},{8,9},{9,8},{10,11... | collective-permute-start | bytes 1966088 | tf_op jit(solution)/shard_map/ppermute | solution.py:36
  36.2 5.5 %collective-permute-start.11 = (bf16[192,1280]{1,0:T(8,128)(2,1)S(1)}, bf16[192,1280]{1,0:T(8,128)(2,1)S(1)}, u32[]{:S(2)}, u32[]{:S(2)}) collective-permute-start(bf16[192,1280]{1,0:T(8,128)(2,1)S(1)} %collective-permute-done.9.refs_7_), channel_id=1, source_target_pairs={{0,1},{1,0},{2,3},{3,2},{4,5},{5,4},{6,7},{7,6},{8,9},{9,8},{10,11... | collective-permute-start | bytes 1474568 | tf_op jit(solution)/shard_map/ppermute | solution.py:36
  70.8 3.1 %collective-permute-start.23 = (bf16[192,1280]{1,0:T(8,128)(2,1)S(1)}, bf16[192,1280]{1,0:T(8,128)(2,1)S(1)}, u32[]{:S(2)}, u32[]{:S(2)}) collective-permute-start(bf16[192,1280]{1,0:T(8,128)(2,1)S(1)} %get-tuple-element.60), channel_id=1, source_target_pairs={{0,1},{1,0},{2,3},{3,2},{4,5},{5,4},{6,7},{7,6},{8,9},{9,8},{10,11... | collective-permute-start | bytes 1474568 | tf_op jit(solution)/shard_map/ppermute | solution.py:36
  74.0 15.9 %collective-permute-start.24 = (bf16[192,1280]{1,0:T(8,128)(2,1)S(1)}, bf16[192,1280]{1,0:T(8,128)(2,1)S(1)}, u32[]{:S(2)}, u32[]{:S(2)}) collective-permute-start(bf16[192,1280]{1,0:T(8,128)(2,1)S(1)} %text_far.1), channel_id=1, source_target_pairs={{0,64},{1,193},{2,66},{3,195},{4,68},{5,197},{6,70},{7,199},{8,72}... | collective-permute-start | bytes 1474568 | tf_op jit(solution)/shard_map/ppermute | solution.py:36
  77.0 3.8 %collective-permute-start.20 = (bf16[128,1280]{1,0:T(8,128)(2,1)S(1)}, bf16[128,1280]{1,0:T(8,128)(2,1)S(1)}, u32[]{:S(2)}, u32[]{:S(2)}) collective-permute-start(bf16[128,1280]{1,0:T(8,128)(2,1)S(1)} %get-tuple-element.56), channel_id=1, source_target_pairs={{0,1},{1,0},{2,3},{3,2},{4,5},{5,4},{6,7},{7,6},{8,9},{9,8},{10,11... | collective-permute-start | bytes 983048 | tf_op jit(solution)/shard_map/ppermute | solution.py:36
  77.7 5.9 %collective-permute-start.21 = (bf16[128,1280]{1,0:T(8,128)(2,1)S(1)}, bf16[128,1280]{1,0:T(8,128)(2,1)S(1)}, u32[]{:S(2)}, u32[]{:S(2)}) collective-permute-start(bf16[128,1280]{1,0:T(8,128)(2,1)S(1)} %get-tuple-element.57), channel_id=1, source_target_pairs={{0,1},{1,0},{2,3},{3,2},{4,5},{5,4},{6,7},{7,6},{8,9},{9,8},{10,11... | collective-permute-start | bytes 983048 | tf_op jit(solution)/shard_map/ppermute | solution.py:36
  78.2 17.6 %collective-permute-start.14 = (bf16[256,1280]{1,0:T(8,128)(2,1)S(1)}, bf16[256,1280]{1,0:T(8,128)(2,1)S(1)}, u32[]{:S(2)}, u32[]{:S(2)}) collective-permute-start(bf16[256,1280]{1,0:T(8,128)(2,1)S(1)} %get-tuple-element.48), channel_id=1, source_target_pairs={{0,24},{1,7},{2,26},{3,1},{4,28},{5,3},{6,30},{7,5},{8,0},{9,15},{... | collective-permute-start | bytes 1966088 | tf_op jit(solution)/shard_map/ppermute | solution.py:36
  80.6 18.8 %collective-permute-start.15 = (bf16[256,1280]{1,0:T(8,128)(2,1)S(1)}, bf16[256,1280]{1,0:T(8,128)(2,1)S(1)}, u32[]{:S(2)}, u32[]{:S(2)}) collective-permute-start(bf16[256,1280]{1,0:T(8,128)(2,1)S(1)} %get-tuple-element.49), channel_id=1, source_target_pairs={{0,8},{1,3},{2,10},{3,5},{4,12},{5,7},{6,14},{7,1},{8,16},{9,11},{... | collective-permute-start | bytes 1966088 | tf_op jit(solution)/shard_map/ppermute | solution.py:36
  80.9 18.6 %collective-permute-start.16 = (bf16[256,1280]{1,0:T(8,128)(2,1)S(1)}, bf16[256,1280]{1,0:T(8,128)(2,1)S(1)}, u32[]{:S(2)}, u32[]{:S(2)}) collective-permute-start(bf16[256,1280]{1,0:T(8,128)(2,1)S(1)} %get-tuple-element.50), channel_id=1, source_target_pairs={{0,16},{1,5},{2,18},{3,7},{4,20},{5,1},{6,22},{7,3},{8,24},{9,13},... | collective-permute-start | bytes 1966088 | tf_op jit(solution)/shard_map/ppermute | solution.py:36
  90.1 14.9 %collective-permute-start.25 = (bf16[128,1280]{1,0:T(8,128)(2,1)S(1)}, bf16[128,1280]{1,0:T(8,128)(2,1)S(1)}, u32[]{:S(2)}, u32[]{:S(2)}) collective-permute-start(bf16[128,1280]{1,0:T(8,128)(2,1)S(1)} %get-tuple-element.61), channel_id=1, source_target_pairs={{0,32},{1,225},{2,34},{3,227},{4,36},{5,229},{6,38},{7,231},{8,40}... | collective-permute-start | bytes 983048 | tf_op jit(solution)/shard_map/ppermute | solution.py:36
  90.2 14.8 %collective-permute-start.26 = (bf16[128,1280]{1,0:T(8,128)(2,1)S(1)}, bf16[128,1280]{1,0:T(8,128)(2,1)S(1)}, u32[]{:S(2)}, u32[]{:S(2)}) collective-permute-start(bf16[128,1280]{1,0:T(8,128)(2,1)S(1)} %get-tuple-element.62), channel_id=1, source_target_pairs={{0,64},{1,193},{2,66},{3,195},{4,68},{5,197},{6,70},{7,199},{8,72}... | collective-permute-start | bytes 983048 | tf_op jit(solution)/shard_map/ppermute | solution.py:36
  99.7 5.9 %collective-permute-start.17 = (bf16[64,1280]{1,0:T(8,128)(2,1)S(1)}, bf16[64,1280]{1,0:T(8,128)(2,1)S(1)}, u32[]{:S(2)}, u32[]{:S(2)}) collective-permute-start(bf16[64,1280]{1,0:T(8,128)(2,1)S(1)} %get-tuple-element.52), channel_id=1, source_target_pairs={{0,6},{1,25},{2,0},{3,27},{4,2},{5,29},{6,4},{7,31},{8,14},{9,1},{... | collective-permute-start | bytes 491528 | tf_op jit(solution)/shard_map/ppermute | solution.py:36
  102.8 8.3 %collective-permute-start.18 = (bf16[64,1280]{1,0:T(8,128)(2,1)S(1)}, bf16[64,1280]{1,0:T(8,128)(2,1)S(1)}, u32[]{:S(2)}, u32[]{:S(2)}) collective-permute-start(bf16[64,1280]{1,0:T(8,128)(2,1)S(1)} %get-tuple-element.53), channel_id=1, source_target_pairs={{0,2},{1,9},{2,4},{3,11},{4,6},{5,13},{6,0},{7,15},{8,10},{9,17},{... | collective-permute-start | bytes 491528 | tf_op jit(solution)/shard_map/ppermute | solution.py:36
  102.8 8.3 %collective-permute-start.19 = (bf16[64,1280]{1,0:T(8,128)(2,1)S(1)}, bf16[64,1280]{1,0:T(8,128)(2,1)S(1)}, u32[]{:S(2)}, u32[]{:S(2)}) collective-permute-start(bf16[64,1280]{1,0:T(8,128)(2,1)S(1)} %get-tuple-element.54), channel_id=1, source_target_pairs={{0,4},{1,17},{2,6},{3,19},{4,0},{5,21},{6,2},{7,23},{8,12},{9,25},... | collective-permute-start | bytes 491528 | tf_op jit(solution)/shard_map/ppermute | solution.py:36
  105.1 6.7 %collective-permute-start.27 = (f32[64,1280]{1,0:T(8,128)S(1)}, f32[64,1280]{1,0:T(8,128)S(1)}, u32[]{:S(2)}, u32[]{:S(2)}) collective-permute-start(f32[64,1280]{1,0:T(8,128)S(1)} %get-tuple-element.65), channel_id=1, source_target_pairs={{0,1},{1,0},{2,3},{3,2},{4,5},{5,4},{6,7},{7,6},{8,9},{9,8},{10,11... | collective-permute-start | bytes 983048 | tf_op jit(solution)/shard_map/ppermute | solution.py:36
  (6 other events, 50.7 us)

commit v4 on v3

--- a/solution.py
+++ b/solution.py
@@ -113,15 +113,20 @@
         col_top, col_sum = new, total
 
     col = col_top + jnp.log(col_sum)
-    cols_out[...] = jnp.zeros(cols_out.shape, f32)
     for chunk in range(len(steps)):
         z, turned = chunk_place(place, chunk)
         tile = jnp.broadcast_to(col[:, chunk * lanes : (chunk + 1) * lanes], (8, lanes))
         tile = jnp.where(turned, pltpu.roll(tile, half, 1), tile)
         cols_out[pl.ds(z, 1), :] = tile[:1]
     first = place[0] == 0
-    kept[...] = jnp.where(first, cols_out[...], rows_out[...])
-    sent[...] = jnp.where(first, rows_out[...], cols_out[...])
+    lane = lax.broadcasted_iota(jnp.int32, (8, lanes), 1)
+    for i in range(kept.shape[0]):
+        low = jnp.broadcast_to(rows_out[2 * i : 2 * i + 1, :], (8, lanes))
+        high = jnp.broadcast_to(rows_out[2 * i + 1 : 2 * i + 2, :], (8, lanes))
+        row = jnp.where(lane < half, low, pltpu.roll(high, half, 1))[:1]
+        col = cols_out[i : i + 1, :]
+        kept[i : i + 1, :] = jnp.where(first, col, row)
+        sent[i : i + 1, :] = jnp.where(first, row, col)
     for copy in copies:
         copy.wait()
 
@@ -130,7 +135,7 @@
     width = groups[0].shape[1]
     rows = 4 * groups[0].shape[0]
     cols = 16 * pieces[0].shape[0]
-    tile = (16, lanes)
+    tile = (8, lanes)
     return pl.pallas_call(
         scores_kernel,
         in_specs=[in_smem] + [in_vmem] * 10,
@@ -144,7 +149,7 @@
         scratch_shapes=[
             pltpu.VMEM((rows, cols), f32),
             pltpu.VMEM((cols, width), bf16),
-            pltpu.VMEM(tile, f32),
+            pltpu.VMEM((16, lanes), f32),
             pltpu.VMEM(tile, f32),
             pltpu.SemaphoreType.DMA((5,)),
         ],
@@ -218,7 +223,7 @@
 
 
 def dscores_kernel(
-    place, scores_in, kept, received, labels, g0, g1, g2, g3, dscores, mine, theirs, scores, targets, sems
+    place, scores_in, kept, received, labels, g0, g1, g2, g3, dscores, mine, theirs, scores, targets, rows, sems
 ):
     core, z, spot = place[0], place[3], place[5]
     first = core == 0
@@ -249,8 +254,13 @@
         both = jnp.where(lane_row < half, low, high)
         return jnp.broadcast_to(both[:1], (lanes, lanes)).T
 
+    for i in range(kept.shape[0]):
+        tile = jnp.where(first, received[i : i + 1, :], kept[i : i + 1, :])
+        rows[2 * i : 2 * i + 1, :] = tile
+        rows[2 * i + 1 : 2 * i + 2, :] = pltpu.roll(jnp.broadcast_to(tile, (8, lanes)), half, 1)[:1]
+
     def row_lse(k):
-        return jnp.where(first, received[pl.ds(k, 1), :], kept[pl.ds(k, 1), :])
+        return rows[pl.ds(k, 1), :]
 
     def target_of(k):
         return targets[pl.ds(k, 1), :]
@@ -298,6 +308,7 @@
         scratch_shapes=[
             pltpu.VMEM((rows, cols), f32),
             pltpu.VMEM(labels.shape, f32),
+            pltpu.VMEM(labels.shape, f32),
             pltpu.SemaphoreType.DMA((4,)),
         ],
         compiler_params=pltpu.CompilerParams(vmem_limit_bytes=vmem_bytes),

time: 113 us -> 112 us (level)
  no operation moved by 1% of the time
where the time goes in v4:
time: 112 us; the launch traced here: 111 us
  waiting for transfers between devices  43.7 us (39%)
  starting transfers between devices  33.3 us (30%)
  Pallas kernels  18.4 us (16%)
  blocking collectives  13.7 us (12%)
  other arithmetic  1.46 us (1%)
    ppermute x28, waiting for transfers between devices, send(): return lax.ppermute(value, every, pairs)  43.7 us
    ppermute x28, starting transfers between devices, send(): return lax.ppermute(value, every, pairs)  33.3 us
    all_to_all x1, blocking collectives, shards(): lax.all_to_all(parts.reshape(-1, lanes), every, 0, 0, axis_index_groups=s...  13.7 us
    pallas_call x1, Pallas kernels, local_scores(): pl.pallas_call(scores_kernel, in_specs=[in_smem] + [in_vmem] * 10, out_sp...  5.32 us
    pallas_call x1, Pallas kernels, local_dscores(): pl.pallas_call(dscores_kernel, in_specs=[in_smem, in_hbm] + [in_vmem] * 7...  5.31 us
    pallas_call x1, Pallas kernels, product(): pl.pallas_call(product_kernel, in_specs=[in_vmem] * 2, out_specs=[in_vmem...  2.92 us
  transfers between devices with their start and end apart: 28, of which 13 were waited for; matrix products, arithmetic and copies ran while one was open for 1% of the time, Pallas kernels for 6%

profile of v4, /device:TPU:32, one launch (start us, length us, event | category | flops | bytes accessed | tf_op | source)
XLA Modules:
  0.0 111.5 jit_solution(2485492356455809293)
XLA Ops:
  2.4 3.3 %collective-permute-start.8 = (bf16[128,1280]{1,0:T(8,128)(2,1)S(1)}, bf16[128,1280]{1,0:T(8,128)(2,1)S(1)}, u32[]{:S(2)}, u32[]{:S(2)}) collective-permute-start(bf16[128,1280]{1,0:T(8,128)(2,1)S(1)} %join.5), channel_id=1, source_target_pairs={{0,64},{1,193},{2,66},{3,195},{4,68},{5,197},{6,70},{7,199},{8,72}... | collective-permute-start | bytes 983048 | tf_op jit(solution)/shard_map/ppermute | solution.py:36
  5.7 3.1 %collective-permute-start.7 = (bf16[128,1280]{1,0:T(8,128)(2,1)S(1)}, bf16[128,1280]{1,0:T(8,128)(2,1)S(1)}, u32[]{:S(2)}, u32[]{:S(2)}) collective-permute-start(bf16[128,1280]{1,0:T(8,128)(2,1)S(1)} %join.5), channel_id=1, source_target_pairs={{0,32},{1,225},{2,34},{3,227},{4,36},{5,229},{6,38},{7,231},{8,40}... | collective-permute-start | bytes 983048 | tf_op jit(solution)/shard_map/ppermute | solution.py:36
  8.9 3.2 %collective-permute-start.2 = (bf16[64,1280]{1,0:T(8,128)(2,1)}, bf16[64,1280]{1,0:T(8,128)(2,1)S(1)}, u32[]{:S(2)}, u32[]{:S(2)}) collective-permute-start(bf16[64,1280]{1,0:T(8,128)(2,1)} %a), channel_id=1, source_target_pairs={{0,4},{1,17},{2,6},{3,19},{4,0},{5,21},{6,2},{7,23},{8,12},{9,25},... | collective-permute-start | bytes 491528 | tf_op jit(solution)/shard_map/ppermute | solution.py:36
  14.1 1.8 %collective-permute-done.2.refs_3_ = bf16[64,1280]{1,0:T(8,128)(2,1)S(1)} collective-permute-done((bf16[64,1280]{1,0:T(8,128)(2,1)}, bf16[64,1280]{1,0:T(8,128)(2,1)S(1)}, u32[]{:S(2)}, u32[]{:S(2)}) %collective-permute-start.2) | collective-permute-done | bytes 163872 | tf_op jit(solution)/shard_map/ppermute | solution.py:36
  15.9 2.1 %collective-permute-done.1.refs_2_ = bf16[64,1280]{1,0:T(8,128)(2,1)S(1)} collective-permute-done((bf16[64,1280]{1,0:T(8,128)(2,1)}, bf16[64,1280]{1,0:T(8,128)(2,1)S(1)}, u32[]{:S(2)}, u32[]{:S(2)}) %collective-permute-start.1) | collective-permute-done | bytes 163872 | tf_op jit(solution)/shard_map/ppermute | solution.py:36
  18.0 1.9 %collective-permute-done.refs_1_ = bf16[64,1280]{1,0:T(8,128)(2,1)S(1)} collective-permute-done((bf16[64,1280]{1,0:T(8,128)(2,1)}, bf16[64,1280]{1,0:T(8,128)(2,1)S(1)}, u32[]{:S(2)}, u32[]{:S(2)}) %collective-permute-start) | collective-permute-done | bytes 163872 | tf_op jit(solution)/shard_map/ppermute | solution.py:36
  20.0 2.5 %collective-permute-start.9 = (bf16[192,1280]{1,0:T(8,128)(2,1)S(1)}, bf16[192,1280]{1,0:T(8,128)(2,1)S(1)}, u32[]{:S(2)}, u32[]{:S(2)}) collective-permute-start(bf16[192,1280]{1,0:T(8,128)(2,1)S(1)} %join.7), channel_id=1, source_target_pairs={{0,64},{1,193},{2,66},{3,195},{4,68},{5,197},{6,70},{7,199},{8,72}... | collective-permute-start | bytes 1474568 | tf_op jit(solution)/shard_map/ppermute | solution.py:36
  22.5 3.0 %collective-permute-start.5 = (bf16[256,1280]{1,0:T(8,128)(2,1)S(1)}, bf16[256,1280]{1,0:T(8,128)(2,1)S(1)}, u32[]{:S(2)}, u32[]{:S(2)}) collective-permute-start(bf16[256,1280]{1,0:T(8,128)(2,1)S(1)} %join.4.refs_2_.refs_0_.g0), channel_id=1, source_target_pairs={{0,16},{1,5},{2,18},{3,7},{4,20},{5,1},{6,22},{7,3},{8,24},{9,13},... | collective-permute-start | bytes 1966088 | tf_op jit(solution)/shard_map/ppermute | solution.py:36
  27.7 8.6 %collective-permute-done.9.refs_7_ = bf16[192,1280]{1,0:T(8,128)(2,1)S(1)} collective-permute-done((bf16[192,1280]{1,0:T(8,128)(2,1)S(1)}, bf16[192,1280]{1,0:T(8,128)(2,1)S(1)}, u32[]{:S(2)}, u32[]{:S(2)}) %collective-permute-start.9) | collective-permute-done | bytes 491552 | tf_op jit(solution)/shard_map/ppermute | solution.py:36
  36.3 5.4 %collective-permute-done.4.refs_2_.g2 = bf16[256,1280]{1,0:T(8,128)(2,1)S(1)} collective-permute-done((bf16[256,1280]{1,0:T(8,128)(2,1)S(1)}, bf16[256,1280]{1,0:T(8,128)(2,1)S(1)}, u32[]{:S(2)}, u32[]{:S(2)}) %collective-permute-start.4) | collective-permute-done | bytes 655392 | tf_op jit(solution)/shard_map/ppermute | solution.py:36
  41.7 5.3 %scores.1 = (f32[1024,1024]{1,0:T(8,128)}, bf16[1024,1280]{1,0:T(8,128)(2,1)}, f32[8,128]{1,0:T(8,128)S(1)}, f32[8,128]{1,0:T(8,128)S(1)}) custom-call(s32[6]{0:T(128)S(1)} %stack.27.place, bf16[256,1280]{1,0:T(8,128)(2,1)S(1)} %join.4.refs_2_.refs_0_.g0, bf16[256,1280]{1,0:T(8,128)(2,1)S(1)} %collective-permute-done.3.refs_1_.g1, ...), custom_call_target="tpu_custom_call" | custom-call | flops 2684354560 | bytes 6000000 | tf_op jit(solution)/shard_map/scores/pallas_call | solution.py:139
  49.0 13.7 %all_to_all.9 = f32[16,16,128]{2,1,0:T(8,128)S(1)} all-to-all(f32[16,16,128]{2,1,0:T(8,128)S(1)} %bitcast.10), channel_id=1, replica_groups={{0,32,64,96,128,160,192,224,8,40,72,104,136,168,200,232},{2,34,66,98,13..., dimensions={0} | all-to-all | bytes 262144 | tf_op jit(solution)/shard_map/all_to_all | solution.py:532
  64.6 5.3 %dscores.1 = (bf16[1024,1024]{1,0:T(8,128)(2,1)S(1)}, f32[192,1280]{1,0:T(8,128)S(1)}, bf16[192,1280]{1,0:T(8,128)(2,1)S(1)}) custom-call(s32[6]{0:T(128)S(1)} %stack.27.place, f32[1024,1024]{1,0:T(8,128)} %get-tuple-element.39.scores_in, f32[8,128]{1,0:T(8,128)S(1)} %get-tuple-element.42.kept, f32[8,128]{1,0:T(8,128)S(1)} %collective-permute-done.13.received, ...), custom_call_target="tpu_custom_call" | custom-call | flops 1342177280 | bytes 6000000 | tf_op jit(solution)/shard_map/dscores/pallas_call | solution.py:299
  70.2 2.9 %image_product.1 = (f32[256,1280]{1,0:T(8,128)S(1)}, bf16[256,1280]{1,0:T(8,128)(2,1)S(1)}, bf16[256,1280]{1,0:T(8,128)(2,1)S(1)}, bf16[256,1280]{1,0:T(8,128)(2,1)S(1)}) custom-call(bf16[1024,1024]{1,0:T(8,128)(2,1)S(1)} %get-tuple-element.45.dscores, bf16[1024,1280]{1,0:T(8,128)(2,1)S(1)} %copy-done.1), custom_call_target="tpu_custom_call" | custom-call | flops 2684354560 | bytes 6000000 | tf_op jit(solution)/shard_map/image_product/pallas_call | solution.py:362
  73.2 1.3 %collective-permute-start.24 = (bf16[192,1280]{1,0:T(8,128)(2,1)S(1)}, bf16[192,1280]{1,0:T(8,128)(2,1)S(1)}, u32[]{:S(2)}, u32[]{:S(2)}) collective-permute-start(bf16[192,1280]{1,0:T(8,128)(2,1)S(1)} %text_far.1), channel_id=1, source_target_pairs={{0,64},{1,193},{2,66},{3,195},{4,68},{5,197},{6,70},{7,199},{8,72}... | collective-permute-start | bytes 1474568 | tf_op jit(solution)/shard_map/ppermute | solution.py:36
  74.5 1.9 %near_texts.1 = (f32[320,1280]{1,0:T(8,128)S(1)}, bf16[128,1280]{1,0:T(8,128)(2,1)S(1)}, bf16[128,1280]{1,0:T(8,128)(2,1)S(1)}, bf16[64,1280]{1,0:T(8,128)(2,1)S(1)}) custom-call(bf16[1024,1024]{1,0:T(8,128)(2,1)S(1)} %get-tuple-element.45.dscores, bf16[256,1280]{1,0:T(8,128)(2,1)S(1)} %join.4.refs_2_.refs_0_.g0, ...), custom_call_target="tpu_custom_call" | custom-call | flops 2684354560 | bytes 6000000 | tf_op jit(solution)/shard_map/near_texts/pallas_call | solution.py:337
  77.4 2.1 %collective-permute-start.14 = (bf16[256,1280]{1,0:T(8,128)(2,1)S(1)}, bf16[256,1280]{1,0:T(8,128)(2,1)S(1)}, u32[]{:S(2)}, u32[]{:S(2)}) collective-permute-start(bf16[256,1280]{1,0:T(8,128)(2,1)S(1)} %get-tuple-element.48), channel_id=1, source_target_pairs={{0,24},{1,7},{2,26},{3,1},{4,28},{5,3},{6,30},{7,5},{8,0},{9,15},{... | collective-permute-start | bytes 1966088 | tf_op jit(solution)/shard_map/ppermute | solution.py:36
  79.8 2.7 %collective-permute-start.16 = (bf16[256,1280]{1,0:T(8,128)(2,1)S(1)}, bf16[256,1280]{1,0:T(8,128)(2,1)S(1)}, u32[]{:S(2)}, u32[]{:S(2)}) collective-permute-start(bf16[256,1280]{1,0:T(8,128)(2,1)S(1)} %get-tuple-element.50), channel_id=1, source_target_pairs={{0,16},{1,5},{2,18},{3,7},{4,20},{5,1},{6,22},{7,3},{8,24},{9,13},... | collective-permute-start | bytes 1966088 | tf_op jit(solution)/shard_map/ppermute | solution.py:36
  82.4 7.0 %collective-permute-done.24.far = bf16[192,1280]{1,0:T(8,128)(2,1)S(1)} collective-permute-done((bf16[192,1280]{1,0:T(8,128)(2,1)S(1)}, bf16[192,1280]{1,0:T(8,128)(2,1)S(1)}, u32[]{:S(2)}, u32[]{:S(2)}) %collective-permute-start.24) | collective-permute-done | bytes 491552 | tf_op jit(solution)/shard_map/ppermute | solution.py:36
  90.2 4.5 %collective-permute-done.14.p1 = bf16[256,1280]{1,0:T(8,128)(2,1)S(1)} collective-permute-done((bf16[256,1280]{1,0:T(8,128)(2,1)S(1)}, bf16[256,1280]{1,0:T(8,128)(2,1)S(1)}, u32[]{:S(2)}, u32[]{:S(2)}) %collective-permute-start.14) | collective-permute-done | bytes 655392 | tf_op jit(solution)/shard_map/ppermute | solution.py:36
  94.7 3.7 %collective-permute-done.15.p2 = bf16[256,1280]{1,0:T(8,128)(2,1)S(1)} collective-permute-done((bf16[256,1280]{1,0:T(8,128)(2,1)S(1)}, bf16[256,1280]{1,0:T(8,128)(2,1)S(1)}, u32[]{:S(2)}, u32[]{:S(2)}) %collective-permute-start.15) | collective-permute-done | bytes 655392 | tf_op jit(solution)/shard_map/ppermute | solution.py:36
  98.6 3.1 %collective-permute-start.17 = (bf16[64,1280]{1,0:T(8,128)(2,1)S(1)}, bf16[64,1280]{1,0:T(8,128)(2,1)S(1)}, u32[]{:S(2)}, u32[]{:S(2)}) collective-permute-start(bf16[64,1280]{1,0:T(8,128)(2,1)S(1)} %get-tuple-element.52), channel_id=1, source_target_pairs={{0,6},{1,25},{2,0},{3,27},{4,2},{5,29},{6,4},{7,31},{8,14},{9,1},{... | collective-permute-start | bytes 491528 | tf_op jit(solution)/shard_map/ppermute | solution.py:36
  101.7 2.2 %collective-permute-start.19 = (bf16[64,1280]{1,0:T(8,128)(2,1)S(1)}, bf16[64,1280]{1,0:T(8,128)(2,1)S(1)}, u32[]{:S(2)}, u32[]{:S(2)}) collective-permute-start(bf16[64,1280]{1,0:T(8,128)(2,1)S(1)} %get-tuple-element.54), channel_id=1, source_target_pairs={{0,4},{1,17},{2,6},{3,19},{4,0},{5,21},{6,2},{7,23},{8,12},{9,25},... | collective-permute-start | bytes 491528 | tf_op jit(solution)/shard_map/ppermute | solution.py:36
  105.3 4.7 %collective-permute-done.18 = bf16[64,1280]{1,0:T(8,128)(2,1)S(1)} collective-permute-done((bf16[64,1280]{1,0:T(8,128)(2,1)S(1)}, bf16[64,1280]{1,0:T(8,128)(2,1)S(1)}, u32[]{:S(2)}, u32[]{:S(2)}) %collective-permute-start.18) | collective-permute-done | bytes 163872 | tf_op jit(solution)/shard_map/ppermute | solution.py:36
  (55 shorter events, 15.2 us)
Async XLA Ops:
  2.4 17.5 %collective-permute-start.8 = (bf16[128,1280]{1,0:T(8,128)(2,1)S(1)}, bf16[128,1280]{1,0:T(8,128)(2,1)S(1)}, u32[]{:S(2)}, u32[]{:S(2)}) collective-permute-start(bf16[128,1280]{1,0:T(8,128)(2,1)S(1)} %join.5), channel_id=1, source_target_pairs={{0,64},{1,193},{2,66},{3,195},{4,68},{5,197},{6,70},{7,199},{8,72}... | collective-permute-start | bytes 983048 | tf_op jit(solution)/shard_map/ppermute | solution.py:36
  5.7 14.2 %collective-permute-start.7 = (bf16[128,1280]{1,0:T(8,128)(2,1)S(1)}, bf16[128,1280]{1,0:T(8,128)(2,1)S(1)}, u32[]{:S(2)}, u32[]{:S(2)}) collective-permute-start(bf16[128,1280]{1,0:T(8,128)(2,1)S(1)} %join.5), channel_id=1, source_target_pairs={{0,32},{1,225},{2,34},{3,227},{4,36},{5,229},{6,38},{7,231},{8,40}... | collective-permute-start | bytes 983048 | tf_op jit(solution)/shard_map/ppermute | solution.py:36
  8.9 7.0 %collective-permute-start.2 = (bf16[64,1280]{1,0:T(8,128)(2,1)}, bf16[64,1280]{1,0:T(8,128)(2,1)S(1)}, u32[]{:S(2)}, u32[]{:S(2)}) collective-permute-start(bf16[64,1280]{1,0:T(8,128)(2,1)} %a), channel_id=1, source_target_pairs={{0,4},{1,17},{2,6},{3,19},{4,0},{5,21},{6,2},{7,23},{8,12},{9,25},... | collective-permute-start | bytes 491528 | tf_op jit(solution)/shard_map/ppermute | solution.py:36
  12.1 5.9 %collective-permute-start.1 = (bf16[64,1280]{1,0:T(8,128)(2,1)}, bf16[64,1280]{1,0:T(8,128)(2,1)S(1)}, u32[]{:S(2)}, u32[]{:S(2)}) collective-permute-start(bf16[64,1280]{1,0:T(8,128)(2,1)} %a), channel_id=1, source_target_pairs={{0,6},{1,25},{2,0},{3,27},{4,2},{5,29},{6,4},{7,31},{8,14},{9,1},{... | collective-permute-start | bytes 491528 | tf_op jit(solution)/shard_map/ppermute | solution.py:36
  13.1 6.7 %collective-permute-start = (bf16[64,1280]{1,0:T(8,128)(2,1)}, bf16[64,1280]{1,0:T(8,128)(2,1)S(1)}, u32[]{:S(2)}, u32[]{:S(2)}) collective-permute-start(bf16[64,1280]{1,0:T(8,128)(2,1)} %a), channel_id=1, source_target_pairs={{0,2},{1,9},{2,4},{3,11},{4,6},{5,13},{6,0},{7,15},{8,10},{9,17},{... | collective-permute-start | bytes 491528 | tf_op jit(solution)/shard_map/ppermute | solution.py:36
  20.0 16.3 %collective-permute-start.9 = (bf16[192,1280]{1,0:T(8,128)(2,1)S(1)}, bf16[192,1280]{1,0:T(8,128)(2,1)S(1)}, u32[]{:S(2)}, u32[]{:S(2)}) collective-permute-start(bf16[192,1280]{1,0:T(8,128)(2,1)S(1)} %join.7), channel_id=1, source_target_pairs={{0,64},{1,193},{2,66},{3,195},{4,68},{5,197},{6,70},{7,199},{8,72}... | collective-permute-start | bytes 1474568 | tf_op jit(solution)/shard_map/ppermute | solution.py:36
  22.5 13.8 %collective-permute-start.5 = (bf16[256,1280]{1,0:T(8,128)(2,1)S(1)}, bf16[256,1280]{1,0:T(8,128)(2,1)S(1)}, u32[]{:S(2)}, u32[]{:S(2)}) collective-permute-start(bf16[256,1280]{1,0:T(8,128)(2,1)S(1)} %join.4.refs_2_.refs_0_.g0), channel_id=1, source_target_pairs={{0,16},{1,5},{2,18},{3,7},{4,20},{5,1},{6,22},{7,3},{8,24},{9,13},... | collective-permute-start | bytes 1966088 | tf_op jit(solution)/shard_map/ppermute | solution.py:36
  25.5 16.2 %collective-permute-start.4 = (bf16[256,1280]{1,0:T(8,128)(2,1)S(1)}, bf16[256,1280]{1,0:T(8,128)(2,1)S(1)}, u32[]{:S(2)}, u32[]{:S(2)}) collective-permute-start(bf16[256,1280]{1,0:T(8,128)(2,1)S(1)} %join.4.refs_2_.refs_0_.g0), channel_id=1, source_target_pairs={{0,24},{1,7},{2,26},{3,1},{4,28},{5,3},{6,30},{7,5},{8,0},{9,15},{... | collective-permute-start | bytes 1966088 | tf_op jit(solution)/shard_map/ppermute | solution.py:36
  26.6 15.1 %collective-permute-start.3 = (bf16[256,1280]{1,0:T(8,128)(2,1)S(1)}, bf16[256,1280]{1,0:T(8,128)(2,1)S(1)}, u32[]{:S(2)}, u32[]{:S(2)}) collective-permute-start(bf16[256,1280]{1,0:T(8,128)(2,1)S(1)} %join.4.refs_2_.refs_0_.g0), channel_id=1, source_target_pairs={{0,8},{1,3},{2,10},{3,5},{4,12},{5,7},{6,14},{7,1},{8,16},{9,11},{... | collective-permute-start | bytes 1966088 | tf_op jit(solution)/shard_map/ppermute | solution.py:36
  27.6 14.1 %collective-permute-start.10 = (bf16[256,1280]{1,0:T(8,128)(2,1)S(1)}, bf16[256,1280]{1,0:T(8,128)(2,1)S(1)}, u32[]{:S(2)}, u32[]{:S(2)}) collective-permute-start(bf16[256,1280]{1,0:T(8,128)(2,1)S(1)} %join.6.refs_6_), channel_id=1, source_target_pairs={{0,1},{1,0},{2,3},{3,2},{4,5},{5,4},{6,7},{7,6},{8,9},{9,8},{10,11... | collective-permute-start | bytes 1966088 | tf_op jit(solution)/shard_map/ppermute | solution.py:36
  36.2 5.5 %collective-permute-start.11 = (bf16[192,1280]{1,0:T(8,128)(2,1)S(1)}, bf16[192,1280]{1,0:T(8,128)(2,1)S(1)}, u32[]{:S(2)}, u32[]{:S(2)}) collective-permute-start(bf16[192,1280]{1,0:T(8,128)(2,1)S(1)} %collective-permute-done.9.refs_7_), channel_id=1, source_target_pairs={{0,1},{1,0},{2,3},{3,2},{4,5},{5,4},{6,7},{7,6},{8,9},{9,8},{10,11... | collective-permute-start | bytes 1474568 | tf_op jit(solution)/shard_map/ppermute | solution.py:36
  69.9 3.2 %collective-permute-start.23 = (bf16[192,1280]{1,0:T(8,128)(2,1)S(1)}, bf16[192,1280]{1,0:T(8,128)(2,1)S(1)}, u32[]{:S(2)}, u32[]{:S(2)}) collective-permute-start(bf16[192,1280]{1,0:T(8,128)(2,1)S(1)} %get-tuple-element.60), channel_id=1, source_target_pairs={{0,1},{1,0},{2,3},{3,2},{4,5},{5,4},{6,7},{7,6},{8,9},{9,8},{10,11... | collective-permute-start | bytes 1474568 | tf_op jit(solution)/shard_map/ppermute | solution.py:36
  73.2 16.2 %collective-permute-start.24 = (bf16[192,1280]{1,0:T(8,128)(2,1)S(1)}, bf16[192,1280]{1,0:T(8,128)(2,1)S(1)}, u32[]{:S(2)}, u32[]{:S(2)}) collective-permute-start(bf16[192,1280]{1,0:T(8,128)(2,1)S(1)} %text_far.1), channel_id=1, source_target_pairs={{0,64},{1,193},{2,66},{3,195},{4,68},{5,197},{6,70},{7,199},{8,72}... | collective-permute-start | bytes 1474568 | tf_op jit(solution)/shard_map/ppermute | solution.py:36
  76.4 3.3 %collective-permute-start.20 = (bf16[128,1280]{1,0:T(8,128)(2,1)S(1)}, bf16[128,1280]{1,0:T(8,128)(2,1)S(1)}, u32[]{:S(2)}, u32[]{:S(2)}) collective-permute-start(bf16[128,1280]{1,0:T(8,128)(2,1)S(1)} %get-tuple-element.56), channel_id=1, source_target_pairs={{0,1},{1,0},{2,3},{3,2},{4,5},{5,4},{6,7},{7,6},{8,9},{9,8},{10,11... | collective-permute-start | bytes 983048 | tf_op jit(solution)/shard_map/ppermute | solution.py:36
  76.9 5.5 %collective-permute-start.21 = (bf16[128,1280]{1,0:T(8,128)(2,1)S(1)}, bf16[128,1280]{1,0:T(8,128)(2,1)S(1)}, u32[]{:S(2)}, u32[]{:S(2)}) collective-permute-start(bf16[128,1280]{1,0:T(8,128)(2,1)S(1)} %get-tuple-element.57), channel_id=1, source_target_pairs={{0,1},{1,0},{2,3},{3,2},{4,5},{5,4},{6,7},{7,6},{8,9},{9,8},{10,11... | collective-permute-start | bytes 983048 | tf_op jit(solution)/shard_map/ppermute | solution.py:36
  77.4 17.3 %collective-permute-start.14 = (bf16[256,1280]{1,0:T(8,128)(2,1)S(1)}, bf16[256,1280]{1,0:T(8,128)(2,1)S(1)}, u32[]{:S(2)}, u32[]{:S(2)}) collective-permute-start(bf16[256,1280]{1,0:T(8,128)(2,1)S(1)} %get-tuple-element.48), channel_id=1, source_target_pairs={{0,24},{1,7},{2,26},{3,1},{4,28},{5,3},{6,30},{7,5},{8,0},{9,15},{... | collective-permute-start | bytes 1966088 | tf_op jit(solution)/shard_map/ppermute | solution.py:36
  79.5 18.8 %collective-permute-start.15 = (bf16[256,1280]{1,0:T(8,128)(2,1)S(1)}, bf16[256,1280]{1,0:T(8,128)(2,1)S(1)}, u32[]{:S(2)}, u32[]{:S(2)}) collective-permute-start(bf16[256,1280]{1,0:T(8,128)(2,1)S(1)} %get-tuple-element.49), channel_id=1, source_target_pairs={{0,8},{1,3},{2,10},{3,5},{4,12},{5,7},{6,14},{7,1},{8,16},{9,11},{... | collective-permute-start | bytes 1966088 | tf_op jit(solution)/shard_map/ppermute | solution.py:36
  79.8 18.6 %collective-permute-start.16 = (bf16[256,1280]{1,0:T(8,128)(2,1)S(1)}, bf16[256,1280]{1,0:T(8,128)(2,1)S(1)}, u32[]{:S(2)}, u32[]{:S(2)}) collective-permute-start(bf16[256,1280]{1,0:T(8,128)(2,1)S(1)} %get-tuple-element.50), channel_id=1, source_target_pairs={{0,16},{1,5},{2,18},{3,7},{4,20},{5,1},{6,22},{7,3},{8,24},{9,13},... | collective-permute-start | bytes 1966088 | tf_op jit(solution)/shard_map/ppermute | solution.py:36
  89.6 14.3 %collective-permute-start.25 = (bf16[128,1280]{1,0:T(8,128)(2,1)S(1)}, bf16[128,1280]{1,0:T(8,128)(2,1)S(1)}, u32[]{:S(2)}, u32[]{:S(2)}) collective-permute-start(bf16[128,1280]{1,0:T(8,128)(2,1)S(1)} %get-tuple-element.61), channel_id=1, source_target_pairs={{0,32},{1,225},{2,34},{3,227},{4,36},{5,229},{6,38},{7,231},{8,40}... | collective-permute-start | bytes 983048 | tf_op jit(solution)/shard_map/ppermute | solution.py:36
  89.7 15.4 %collective-permute-start.26 = (bf16[128,1280]{1,0:T(8,128)(2,1)S(1)}, bf16[128,1280]{1,0:T(8,128)(2,1)S(1)}, u32[]{:S(2)}, u32[]{:S(2)}) collective-permute-start(bf16[128,1280]{1,0:T(8,128)(2,1)S(1)} %get-tuple-element.62), channel_id=1, source_target_pairs={{0,64},{1,193},{2,66},{3,195},{4,68},{5,197},{6,70},{7,199},{8,72}... | collective-permute-start | bytes 983048 | tf_op jit(solution)/shard_map/ppermute | solution.py:36
  98.6 6.6 %collective-permute-start.17 = (bf16[64,1280]{1,0:T(8,128)(2,1)S(1)}, bf16[64,1280]{1,0:T(8,128)(2,1)S(1)}, u32[]{:S(2)}, u32[]{:S(2)}) collective-permute-start(bf16[64,1280]{1,0:T(8,128)(2,1)S(1)} %get-tuple-element.52), channel_id=1, source_target_pairs={{0,6},{1,25},{2,0},{3,27},{4,2},{5,29},{6,4},{7,31},{8,14},{9,1},{... | collective-permute-start | bytes 491528 | tf_op jit(solution)/shard_map/ppermute | solution.py:36
  101.7 8.3 %collective-permute-start.18 = (bf16[64,1280]{1,0:T(8,128)(2,1)S(1)}, bf16[64,1280]{1,0:T(8,128)(2,1)S(1)}, u32[]{:S(2)}, u32[]{:S(2)}) collective-permute-start(bf16[64,1280]{1,0:T(8,128)(2,1)S(1)} %get-tuple-element.53), channel_id=1, source_target_pairs={{0,2},{1,9},{2,4},{3,11},{4,6},{5,13},{6,0},{7,15},{8,10},{9,17},{... | collective-permute-start | bytes 491528 | tf_op jit(solution)/shard_map/ppermute | solution.py:36
  101.7 8.3 %collective-permute-start.19 = (bf16[64,1280]{1,0:T(8,128)(2,1)S(1)}, bf16[64,1280]{1,0:T(8,128)(2,1)S(1)}, u32[]{:S(2)}, u32[]{:S(2)}) collective-permute-start(bf16[64,1280]{1,0:T(8,128)(2,1)S(1)} %get-tuple-element.54), channel_id=1, source_target_pairs={{0,4},{1,17},{2,6},{3,19},{4,0},{5,21},{6,2},{7,23},{8,12},{9,25},... | collective-permute-start | bytes 491528 | tf_op jit(solution)/shard_map/ppermute | solution.py:36
  105.1 5.6 %collective-permute-start.27 = (f32[64,1280]{1,0:T(8,128)S(1)}, f32[64,1280]{1,0:T(8,128)S(1)}, u32[]{:S(2)}, u32[]{:S(2)}) collective-permute-start(f32[64,1280]{1,0:T(8,128)S(1)} %get-tuple-element.65), channel_id=1, source_target_pairs={{0,1},{1,0},{2,3},{3,2},{4,5},{5,4},{6,7},{7,6},{8,9},{9,8},{10,11... | collective-permute-start | bytes 983048 | tf_op jit(solution)/shard_map/ppermute | solution.py:36
  (6 other events, 49.4 us)

commit v5 on v4

--- a/solution.py
+++ b/solution.py
@@ -541,12 +541,14 @@
     theirs = swap_cores(theirs)
     terms = product(dscores, texts)
     far = send_z(add_far(mine, theirs), 2)
-    parts = [send_second(t, k) for t, k in zip(terms[1:], offsets[1:])]
+    last = send_second(terms[3], offsets[3])
+    parts = [send_second(t, k) for t, k in zip(terms[1:3], offsets[1:3])] + [last]
     mine, *theirs = near_texts(dscores, groups, terms[0])
     one, two, own = relay_text(mine, [swap_cores(t) for t in theirs], far)
     terms = add_image([terms[0]] + parts)
     two, one = send_z(two, 2), send_z(one, 1)
-    image_parts = [terms[0]] + [send_first(t, k) for t, k in zip(terms[1:], offsets[1:])]
+    last = send_first(terms[3], offsets[3])
+    image_parts = [terms[0]] + [send_first(t, k) for t, k in zip(terms[1:3], offsets[1:3])] + [last]
     here, there = split_text(one, two, own)
     text_grad = (score_scale * (here + swap_cores(there))).astype(bf16)
     image_total = sum(part.astype(f32) for part in image_parts)

time: 112 us -> 112 us (level)
  no operation moved by 1% of the time
where the time goes in v5:
time: 112 us; the launch traced here: 111 us
  waiting for transfers between devices  43.7 us (39%)
  starting transfers between devices  33.3 us (30%)
  Pallas kernels  18.4 us (16%)
  blocking collectives  13.7 us (12%)
  other arithmetic  1.46 us (1%)
    ppermute x28, waiting for transfers between devices, send(): return lax.ppermute(value, every, pairs)  43.7 us
    ppermute x28, starting transfers between devices, send(): return lax.ppermute(value, every, pairs)  33.3 us
    all_to_all x1, blocking collectives, shards(): lax.all_to_all(parts.reshape(-1, lanes), every, 0, 0, axis_index_groups=s...  13.7 us
    pallas_call x1, Pallas kernels, local_scores(): pl.pallas_call(scores_kernel, in_specs=[in_smem] + [in_vmem] * 10, out_sp...  5.32 us
    pallas_call x1, Pallas kernels, local_dscores(): pl.pallas_call(dscores_kernel, in_specs=[in_smem, in_hbm] + [in_vmem] * 7...  5.31 us
    pallas_call x1, Pallas kernels, product(): pl.pallas_call(product_kernel, in_specs=[in_vmem] * 2, out_specs=[in_vmem...  2.92 us
  transfers between devices with their start and end apart: 28, of which 13 were waited for; matrix products, arithmetic and copies ran while one was open for 1% of the time, Pallas kernels for 6%

profile of v5, /device:TPU:32, one launch (start us, length us, event | category | flops | bytes accessed | tf_op | source)
XLA Modules:
  0.0 111.5 jit_solution(2485492356455809293)
XLA Ops:
  2.4 3.3 %collective-permute-start.8 = (bf16[128,1280]{1,0:T(8,128)(2,1)S(1)}, bf16[128,1280]{1,0:T(8,128)(2,1)S(1)}, u32[]{:S(2)}, u32[]{:S(2)}) collective-permute-start(bf16[128,1280]{1,0:T(8,128)(2,1)S(1)} %join.5), channel_id=1, source_target_pairs={{0,64},{1,193},{2,66},{3,195},{4,68},{5,197},{6,70},{7,199},{8,72}... | collective-permute-start | bytes 983048 | tf_op jit(solution)/shard_map/ppermute | solution.py:36
  5.7 3.1 %collective-permute-start.7 = (bf16[128,1280]{1,0:T(8,128)(2,1)S(1)}, bf16[128,1280]{1,0:T(8,128)(2,1)S(1)}, u32[]{:S(2)}, u32[]{:S(2)}) collective-permute-start(bf16[128,1280]{1,0:T(8,128)(2,1)S(1)} %join.5), channel_id=1, source_target_pairs={{0,32},{1,225},{2,34},{3,227},{4,36},{5,229},{6,38},{7,231},{8,40}... | collective-permute-start | bytes 983048 | tf_op jit(solution)/shard_map/ppermute | solution.py:36
  8.9 3.2 %collective-permute-start.2 = (bf16[64,1280]{1,0:T(8,128)(2,1)}, bf16[64,1280]{1,0:T(8,128)(2,1)S(1)}, u32[]{:S(2)}, u32[]{:S(2)}) collective-permute-start(bf16[64,1280]{1,0:T(8,128)(2,1)} %a), channel_id=1, source_target_pairs={{0,4},{1,17},{2,6},{3,19},{4,0},{5,21},{6,2},{7,23},{8,12},{9,25},... | collective-permute-start | bytes 491528 | tf_op jit(solution)/shard_map/ppermute | solution.py:36
  14.1 1.8 %collective-permute-done.2.refs_3_ = bf16[64,1280]{1,0:T(8,128)(2,1)S(1)} collective-permute-done((bf16[64,1280]{1,0:T(8,128)(2,1)}, bf16[64,1280]{1,0:T(8,128)(2,1)S(1)}, u32[]{:S(2)}, u32[]{:S(2)}) %collective-permute-start.2) | collective-permute-done | bytes 163872 | tf_op jit(solution)/shard_map/ppermute | solution.py:36
  15.9 2.1 %collective-permute-done.1.refs_2_ = bf16[64,1280]{1,0:T(8,128)(2,1)S(1)} collective-permute-done((bf16[64,1280]{1,0:T(8,128)(2,1)}, bf16[64,1280]{1,0:T(8,128)(2,1)S(1)}, u32[]{:S(2)}, u32[]{:S(2)}) %collective-permute-start.1) | collective-permute-done | bytes 163872 | tf_op jit(solution)/shard_map/ppermute | solution.py:36
  18.0 1.9 %collective-permute-done.refs_1_ = bf16[64,1280]{1,0:T(8,128)(2,1)S(1)} collective-permute-done((bf16[64,1280]{1,0:T(8,128)(2,1)}, bf16[64,1280]{1,0:T(8,128)(2,1)S(1)}, u32[]{:S(2)}, u32[]{:S(2)}) %collective-permute-start) | collective-permute-done | bytes 163872 | tf_op jit(solution)/shard_map/ppermute | solution.py:36
  20.0 2.5 %collective-permute-start.9 = (bf16[192,1280]{1,0:T(8,128)(2,1)S(1)}, bf16[192,1280]{1,0:T(8,128)(2,1)S(1)}, u32[]{:S(2)}, u32[]{:S(2)}) collective-permute-start(bf16[192,1280]{1,0:T(8,128)(2,1)S(1)} %join.7), channel_id=1, source_target_pairs={{0,64},{1,193},{2,66},{3,195},{4,68},{5,197},{6,70},{7,199},{8,72}... | collective-permute-start | bytes 1474568 | tf_op jit(solution)/shard_map/ppermute | solution.py:36
  22.5 3.0 %collective-permute-start.5 = (bf16[256,1280]{1,0:T(8,128)(2,1)S(1)}, bf16[256,1280]{1,0:T(8,128)(2,1)S(1)}, u32[]{:S(2)}, u32[]{:S(2)}) collective-permute-start(bf16[256,1280]{1,0:T(8,128)(2,1)S(1)} %join.4.refs_2_.refs_0_.g0), channel_id=1, source_target_pairs={{0,16},{1,5},{2,18},{3,7},{4,20},{5,1},{6,22},{7,3},{8,24},{9,13},... | collective-permute-start | bytes 1966088 | tf_op jit(solution)/shard_map/ppermute | solution.py:36
  27.7 8.6 %collective-permute-done.9.refs_7_ = bf16[192,1280]{1,0:T(8,128)(2,1)S(1)} collective-permute-done((bf16[192,1280]{1,0:T(8,128)(2,1)S(1)}, bf16[192,1280]{1,0:T(8,128)(2,1)S(1)}, u32[]{:S(2)}, u32[]{:S(2)}) %collective-permute-start.9) | collective-permute-done | bytes 491552 | tf_op jit(solution)/shard_map/ppermute | solution.py:36
  36.3 5.4 %collective-permute-done.4.refs_2_.g2 = bf16[256,1280]{1,0:T(8,128)(2,1)S(1)} collective-permute-done((bf16[256,1280]{1,0:T(8,128)(2,1)S(1)}, bf16[256,1280]{1,0:T(8,128)(2,1)S(1)}, u32[]{:S(2)}, u32[]{:S(2)}) %collective-permute-start.4) | collective-permute-done | bytes 655392 | tf_op jit(solution)/shard_map/ppermute | solution.py:36
  41.7 5.3 %scores.1 = (f32[1024,1024]{1,0:T(8,128)}, bf16[1024,1280]{1,0:T(8,128)(2,1)}, f32[8,128]{1,0:T(8,128)S(1)}, f32[8,128]{1,0:T(8,128)S(1)}) custom-call(s32[6]{0:T(128)S(1)} %stack.27.place, bf16[256,1280]{1,0:T(8,128)(2,1)S(1)} %join.4.refs_2_.refs_0_.g0, bf16[256,1280]{1,0:T(8,128)(2,1)S(1)} %collective-permute-done.3.refs_1_.g1, ...), custom_call_target="tpu_custom_call" | custom-call | flops 2684354560 | bytes 6000000 | tf_op jit(solution)/shard_map/scores/pallas_call | solution.py:139
  49.0 13.7 %all_to_all.9 = f32[16,16,128]{2,1,0:T(8,128)S(1)} all-to-all(f32[16,16,128]{2,1,0:T(8,128)S(1)} %bitcast.10), channel_id=1, replica_groups={{0,32,64,96,128,160,192,224,8,40,72,104,136,168,200,232},{2,34,66,98,13..., dimensions={0} | all-to-all | bytes 262144 | tf_op jit(solution)/shard_map/all_to_all | solution.py:532
  64.6 5.3 %dscores.1 = (bf16[1024,1024]{1,0:T(8,128)(2,1)S(1)}, f32[192,1280]{1,0:T(8,128)S(1)}, bf16[192,1280]{1,0:T(8,128)(2,1)S(1)}) custom-call(s32[6]{0:T(128)S(1)} %stack.27.place, f32[1024,1024]{1,0:T(8,128)} %get-tuple-element.39.scores_in, f32[8,128]{1,0:T(8,128)S(1)} %get-tuple-element.42.kept, f32[8,128]{1,0:T(8,128)S(1)} %collective-permute-done.13.received, ...), custom_call_target="tpu_custom_call" | custom-call | flops 1342177280 | bytes 6000000 | tf_op jit(solution)/shard_map/dscores/pallas_call | solution.py:299
  70.2 2.9 %image_product.1 = (f32[256,1280]{1,0:T(8,128)S(1)}, bf16[256,1280]{1,0:T(8,128)(2,1)S(1)}, bf16[256,1280]{1,0:T(8,128)(2,1)S(1)}, bf16[256,1280]{1,0:T(8,128)(2,1)S(1)}) custom-call(bf16[1024,1024]{1,0:T(8,128)(2,1)S(1)} %get-tuple-element.45.dscores, bf16[1024,1280]{1,0:T(8,128)(2,1)S(1)} %copy-done.1), custom_call_target="tpu_custom_call" | custom-call | flops 2684354560 | bytes 6000000 | tf_op jit(solution)/shard_map/image_product/pallas_call | solution.py:362
  73.2 1.3 %collective-permute-start.24 = (bf16[192,1280]{1,0:T(8,128)(2,1)S(1)}, bf16[192,1280]{1,0:T(8,128)(2,1)S(1)}, u32[]{:S(2)}, u32[]{:S(2)}) collective-permute-start(bf16[192,1280]{1,0:T(8,128)(2,1)S(1)} %text_far.1), channel_id=1, source_target_pairs={{0,64},{1,193},{2,66},{3,195},{4,68},{5,197},{6,70},{7,199},{8,72}... | collective-permute-start | bytes 1474568 | tf_op jit(solution)/shard_map/ppermute | solution.py:36
  74.5 1.9 %near_texts.1 = (f32[320,1280]{1,0:T(8,128)S(1)}, bf16[128,1280]{1,0:T(8,128)(2,1)S(1)}, bf16[128,1280]{1,0:T(8,128)(2,1)S(1)}, bf16[64,1280]{1,0:T(8,128)(2,1)S(1)}) custom-call(bf16[1024,1024]{1,0:T(8,128)(2,1)S(1)} %get-tuple-element.45.dscores, bf16[256,1280]{1,0:T(8,128)(2,1)S(1)} %join.4.refs_2_.refs_0_.g0, ...), custom_call_target="tpu_custom_call" | custom-call | flops 2684354560 | bytes 6000000 | tf_op jit(solution)/shard_map/near_texts/pallas_call | solution.py:337
  77.4 2.1 %collective-permute-start.14 = (bf16[256,1280]{1,0:T(8,128)(2,1)S(1)}, bf16[256,1280]{1,0:T(8,128)(2,1)S(1)}, u32[]{:S(2)}, u32[]{:S(2)}) collective-permute-start(bf16[256,1280]{1,0:T(8,128)(2,1)S(1)} %get-tuple-element.48), channel_id=1, source_target_pairs={{0,24},{1,7},{2,26},{3,1},{4,28},{5,3},{6,30},{7,5},{8,0},{9,15},{... | collective-permute-start | bytes 1966088 | tf_op jit(solution)/shard_map/ppermute | solution.py:36
  79.8 2.7 %collective-permute-start.16 = (bf16[256,1280]{1,0:T(8,128)(2,1)S(1)}, bf16[256,1280]{1,0:T(8,128)(2,1)S(1)}, u32[]{:S(2)}, u32[]{:S(2)}) collective-permute-start(bf16[256,1280]{1,0:T(8,128)(2,1)S(1)} %get-tuple-element.50), channel_id=1, source_target_pairs={{0,16},{1,5},{2,18},{3,7},{4,20},{5,1},{6,22},{7,3},{8,24},{9,13},... | collective-permute-start | bytes 1966088 | tf_op jit(solution)/shard_map/ppermute | solution.py:36
  82.4 7.0 %collective-permute-done.24.far = bf16[192,1280]{1,0:T(8,128)(2,1)S(1)} collective-permute-done((bf16[192,1280]{1,0:T(8,128)(2,1)S(1)}, bf16[192,1280]{1,0:T(8,128)(2,1)S(1)}, u32[]{:S(2)}, u32[]{:S(2)}) %collective-permute-start.24) | collective-permute-done | bytes 491552 | tf_op jit(solution)/shard_map/ppermute | solution.py:36
  90.2 4.5 %collective-permute-done.14.p1 = bf16[256,1280]{1,0:T(8,128)(2,1)S(1)} collective-permute-done((bf16[256,1280]{1,0:T(8,128)(2,1)S(1)}, bf16[256,1280]{1,0:T(8,128)(2,1)S(1)}, u32[]{:S(2)}, u32[]{:S(2)}) %collective-permute-start.14) | collective-permute-done | bytes 655392 | tf_op jit(solution)/shard_map/ppermute | solution.py:36
  94.7 3.7 %collective-permute-done.15.p2 = bf16[256,1280]{1,0:T(8,128)(2,1)S(1)} collective-permute-done((bf16[256,1280]{1,0:T(8,128)(2,1)S(1)}, bf16[256,1280]{1,0:T(8,128)(2,1)S(1)}, u32[]{:S(2)}, u32[]{:S(2)}) %collective-permute-start.15) | collective-permute-done | bytes 655392 | tf_op jit(solution)/shard_map/ppermute | solution.py:36
  98.6 3.1 %collective-permute-start.17 = (bf16[64,1280]{1,0:T(8,128)(2,1)S(1)}, bf16[64,1280]{1,0:T(8,128)(2,1)S(1)}, u32[]{:S(2)}, u32[]{:S(2)}) collective-permute-start(bf16[64,1280]{1,0:T(8,128)(2,1)S(1)} %get-tuple-element.52), channel_id=1, source_target_pairs={{0,6},{1,25},{2,0},{3,27},{4,2},{5,29},{6,4},{7,31},{8,14},{9,1},{... | collective-permute-start | bytes 491528 | tf_op jit(solution)/shard_map/ppermute | solution.py:36
  101.7 2.2 %collective-permute-start.19 = (bf16[64,1280]{1,0:T(8,128)(2,1)S(1)}, bf16[64,1280]{1,0:T(8,128)(2,1)S(1)}, u32[]{:S(2)}, u32[]{:S(2)}) collective-permute-start(bf16[64,1280]{1,0:T(8,128)(2,1)S(1)} %get-tuple-element.54), channel_id=1, source_target_pairs={{0,4},{1,17},{2,6},{3,19},{4,0},{5,21},{6,2},{7,23},{8,12},{9,25},... | collective-permute-start | bytes 491528 | tf_op jit(solution)/shard_map/ppermute | solution.py:36
  105.3 4.7 %collective-permute-done.18 = bf16[64,1280]{1,0:T(8,128)(2,1)S(1)} collective-permute-done((bf16[64,1280]{1,0:T(8,128)(2,1)S(1)}, bf16[64,1280]{1,0:T(8,128)(2,1)S(1)}, u32[]{:S(2)}, u32[]{:S(2)}) %collective-permute-start.18) | collective-permute-done | bytes 163872 | tf_op jit(solution)/shard_map/ppermute | solution.py:36
  (55 shorter events, 15.2 us)
Async XLA Ops:
  2.4 17.5 %collective-permute-start.8 = (bf16[128,1280]{1,0:T(8,128)(2,1)S(1)}, bf16[128,1280]{1,0:T(8,128)(2,1)S(1)}, u32[]{:S(2)}, u32[]{:S(2)}) collective-permute-start(bf16[128,1280]{1,0:T(8,128)(2,1)S(1)} %join.5), channel_id=1, source_target_pairs={{0,64},{1,193},{2,66},{3,195},{4,68},{5,197},{6,70},{7,199},{8,72}... | collective-permute-start | bytes 983048 | tf_op jit(solution)/shard_map/ppermute | solution.py:36
  5.7 14.2 %collective-permute-start.7 = (bf16[128,1280]{1,0:T(8,128)(2,1)S(1)}, bf16[128,1280]{1,0:T(8,128)(2,1)S(1)}, u32[]{:S(2)}, u32[]{:S(2)}) collective-permute-start(bf16[128,1280]{1,0:T(8,128)(2,1)S(1)} %join.5), channel_id=1, source_target_pairs={{0,32},{1,225},{2,34},{3,227},{4,36},{5,229},{6,38},{7,231},{8,40}... | collective-permute-start | bytes 983048 | tf_op jit(solution)/shard_map/ppermute | solution.py:36
  8.9 7.0 %collective-permute-start.2 = (bf16[64,1280]{1,0:T(8,128)(2,1)}, bf16[64,1280]{1,0:T(8,128)(2,1)S(1)}, u32[]{:S(2)}, u32[]{:S(2)}) collective-permute-start(bf16[64,1280]{1,0:T(8,128)(2,1)} %a), channel_id=1, source_target_pairs={{0,4},{1,17},{2,6},{3,19},{4,0},{5,21},{6,2},{7,23},{8,12},{9,25},... | collective-permute-start | bytes 491528 | tf_op jit(solution)/shard_map/ppermute | solution.py:36
  12.1 5.9 %collective-permute-start.1 = (bf16[64,1280]{1,0:T(8,128)(2,1)}, bf16[64,1280]{1,0:T(8,128)(2,1)S(1)}, u32[]{:S(2)}, u32[]{:S(2)}) collective-permute-start(bf16[64,1280]{1,0:T(8,128)(2,1)} %a), channel_id=1, source_target_pairs={{0,6},{1,25},{2,0},{3,27},{4,2},{5,29},{6,4},{7,31},{8,14},{9,1},{... | collective-permute-start | bytes 491528 | tf_op jit(solution)/shard_map/ppermute | solution.py:36
  13.1 6.7 %collective-permute-start = (bf16[64,1280]{1,0:T(8,128)(2,1)}, bf16[64,1280]{1,0:T(8,128)(2,1)S(1)}, u32[]{:S(2)}, u32[]{:S(2)}) collective-permute-start(bf16[64,1280]{1,0:T(8,128)(2,1)} %a), channel_id=1, source_target_pairs={{0,2},{1,9},{2,4},{3,11},{4,6},{5,13},{6,0},{7,15},{8,10},{9,17},{... | collective-permute-start | bytes 491528 | tf_op jit(solution)/shard_map/ppermute | solution.py:36
  20.0 16.3 %collective-permute-start.9 = (bf16[192,1280]{1,0:T(8,128)(2,1)S(1)}, bf16[192,1280]{1,0:T(8,128)(2,1)S(1)}, u32[]{:S(2)}, u32[]{:S(2)}) collective-permute-start(bf16[192,1280]{1,0:T(8,128)(2,1)S(1)} %join.7), channel_id=1, source_target_pairs={{0,64},{1,193},{2,66},{3,195},{4,68},{5,197},{6,70},{7,199},{8,72}... | collective-permute-start | bytes 1474568 | tf_op jit(solution)/shard_map/ppermute | solution.py:36
  22.5 13.8 %collective-permute-start.5 = (bf16[256,1280]{1,0:T(8,128)(2,1)S(1)}, bf16[256,1280]{1,0:T(8,128)(2,1)S(1)}, u32[]{:S(2)}, u32[]{:S(2)}) collective-permute-start(bf16[256,1280]{1,0:T(8,128)(2,1)S(1)} %join.4.refs_2_.refs_0_.g0), channel_id=1, source_target_pairs={{0,16},{1,5},{2,18},{3,7},{4,20},{5,1},{6,22},{7,3},{8,24},{9,13},... | collective-permute-start | bytes 1966088 | tf_op jit(solution)/shard_map/ppermute | solution.py:36
  25.5 16.2 %collective-permute-start.4 = (bf16[256,1280]{1,0:T(8,128)(2,1)S(1)}, bf16[256,1280]{1,0:T(8,128)(2,1)S(1)}, u32[]{:S(2)}, u32[]{:S(2)}) collective-permute-start(bf16[256,1280]{1,0:T(8,128)(2,1)S(1)} %join.4.refs_2_.refs_0_.g0), channel_id=1, source_target_pairs={{0,24},{1,7},{2,26},{3,1},{4,28},{5,3},{6,30},{7,5},{8,0},{9,15},{... | collective-permute-start | bytes 1966088 | tf_op jit(solution)/shard_map/ppermute | solution.py:36
  26.6 15.1 %collective-permute-start.3 = (bf16[256,1280]{1,0:T(8,128)(2,1)S(1)}, bf16[256,1280]{1,0:T(8,128)(2,1)S(1)}, u32[]{:S(2)}, u32[]{:S(2)}) collective-permute-start(bf16[256,1280]{1,0:T(8,128)(2,1)S(1)} %join.4.refs_2_.refs_0_.g0), channel_id=1, source_target_pairs={{0,8},{1,3},{2,10},{3,5},{4,12},{5,7},{6,14},{7,1},{8,16},{9,11},{... | collective-permute-start | bytes 1966088 | tf_op jit(solution)/shard_map/ppermute | solution.py:36
  27.6 14.1 %collective-permute-start.10 = (bf16[256,1280]{1,0:T(8,128)(2,1)S(1)}, bf16[256,1280]{1,0:T(8,128)(2,1)S(1)}, u32[]{:S(2)}, u32[]{:S(2)}) collective-permute-start(bf16[256,1280]{1,0:T(8,128)(2,1)S(1)} %join.6.refs_6_), channel_id=1, source_target_pairs={{0,1},{1,0},{2,3},{3,2},{4,5},{5,4},{6,7},{7,6},{8,9},{9,8},{10,11... | collective-permute-start | bytes 1966088 | tf_op jit(solution)/shard_map/ppermute | solution.py:36
  36.2 5.5 %collective-permute-start.11 = (bf16[192,1280]{1,0:T(8,128)(2,1)S(1)}, bf16[192,1280]{1,0:T(8,128)(2,1)S(1)}, u32[]{:S(2)}, u32[]{:S(2)}) collective-permute-start(bf16[192,1280]{1,0:T(8,128)(2,1)S(1)} %collective-permute-done.9.refs_7_), channel_id=1, source_target_pairs={{0,1},{1,0},{2,3},{3,2},{4,5},{5,4},{6,7},{7,6},{8,9},{9,8},{10,11... | collective-permute-start | bytes 1474568 | tf_op jit(solution)/shard_map/ppermute | solution.py:36
  69.9 3.2 %collective-permute-start.23 = (bf16[192,1280]{1,0:T(8,128)(2,1)S(1)}, bf16[192,1280]{1,0:T(8,128)(2,1)S(1)}, u32[]{:S(2)}, u32[]{:S(2)}) collective-permute-start(bf16[192,1280]{1,0:T(8,128)(2,1)S(1)} %get-tuple-element.60), channel_id=1, source_target_pairs={{0,1},{1,0},{2,3},{3,2},{4,5},{5,4},{6,7},{7,6},{8,9},{9,8},{10,11... | collective-permute-start | bytes 1474568 | tf_op jit(solution)/shard_map/ppermute | solution.py:36
  73.2 16.2 %collective-permute-start.24 = (bf16[192,1280]{1,0:T(8,128)(2,1)S(1)}, bf16[192,1280]{1,0:T(8,128)(2,1)S(1)}, u32[]{:S(2)}, u32[]{:S(2)}) collective-permute-start(bf16[192,1280]{1,0:T(8,128)(2,1)S(1)} %text_far.1), channel_id=1, source_target_pairs={{0,64},{1,193},{2,66},{3,195},{4,68},{5,197},{6,70},{7,199},{8,72}... | collective-permute-start | bytes 1474568 | tf_op jit(solution)/shard_map/ppermute | solution.py:36
  76.4 3.3 %collective-permute-start.20 = (bf16[128,1280]{1,0:T(8,128)(2,1)S(1)}, bf16[128,1280]{1,0:T(8,128)(2,1)S(1)}, u32[]{:S(2)}, u32[]{:S(2)}) collective-permute-start(bf16[128,1280]{1,0:T(8,128)(2,1)S(1)} %get-tuple-element.56), channel_id=1, source_target_pairs={{0,1},{1,0},{2,3},{3,2},{4,5},{5,4},{6,7},{7,6},{8,9},{9,8},{10,11... | collective-permute-start | bytes 983048 | tf_op jit(solution)/shard_map/ppermute | solution.py:36
  76.9 5.5 %collective-permute-start.21 = (bf16[128,1280]{1,0:T(8,128)(2,1)S(1)}, bf16[128,1280]{1,0:T(8,128)(2,1)S(1)}, u32[]{:S(2)}, u32[]{:S(2)}) collective-permute-start(bf16[128,1280]{1,0:T(8,128)(2,1)S(1)} %get-tuple-element.57), channel_id=1, source_target_pairs={{0,1},{1,0},{2,3},{3,2},{4,5},{5,4},{6,7},{7,6},{8,9},{9,8},{10,11... | collective-permute-start | bytes 983048 | tf_op jit(solution)/shard_map/ppermute | solution.py:36
  77.4 17.3 %collective-permute-start.14 = (bf16[256,1280]{1,0:T(8,128)(2,1)S(1)}, bf16[256,1280]{1,0:T(8,128)(2,1)S(1)}, u32[]{:S(2)}, u32[]{:S(2)}) collective-permute-start(bf16[256,1280]{1,0:T(8,128)(2,1)S(1)} %get-tuple-element.48), channel_id=1, source_target_pairs={{0,24},{1,7},{2,26},{3,1},{4,28},{5,3},{6,30},{7,5},{8,0},{9,15},{... | collective-permute-start | bytes 1966088 | tf_op jit(solution)/shard_map/ppermute | solution.py:36
  79.5 18.8 %collective-permute-start.15 = (bf16[256,1280]{1,0:T(8,128)(2,1)S(1)}, bf16[256,1280]{1,0:T(8,128)(2,1)S(1)}, u32[]{:S(2)}, u32[]{:S(2)}) collective-permute-start(bf16[256,1280]{1,0:T(8,128)(2,1)S(1)} %get-tuple-element.49), channel_id=1, source_target_pairs={{0,8},{1,3},{2,10},{3,5},{4,12},{5,7},{6,14},{7,1},{8,16},{9,11},{... | collective-permute-start | bytes 1966088 | tf_op jit(solution)/shard_map/ppermute | solution.py:36
  79.8 18.6 %collective-permute-start.16 = (bf16[256,1280]{1,0:T(8,128)(2,1)S(1)}, bf16[256,1280]{1,0:T(8,128)(2,1)S(1)}, u32[]{:S(2)}, u32[]{:S(2)}) collective-permute-start(bf16[256,1280]{1,0:T(8,128)(2,1)S(1)} %get-tuple-element.50), channel_id=1, source_target_pairs={{0,16},{1,5},{2,18},{3,7},{4,20},{5,1},{6,22},{7,3},{8,24},{9,13},... | collective-permute-start | bytes 1966088 | tf_op jit(solution)/shard_map/ppermute | solution.py:36
  89.6 14.3 %collective-permute-start.25 = (bf16[128,1280]{1,0:T(8,128)(2,1)S(1)}, bf16[128,1280]{1,0:T(8,128)(2,1)S(1)}, u32[]{:S(2)}, u32[]{:S(2)}) collective-permute-start(bf16[128,1280]{1,0:T(8,128)(2,1)S(1)} %get-tuple-element.61), channel_id=1, source_target_pairs={{0,32},{1,225},{2,34},{3,227},{4,36},{5,229},{6,38},{7,231},{8,40}... | collective-permute-start | bytes 983048 | tf_op jit(solution)/shard_map/ppermute | solution.py:36
  89.7 15.4 %collective-permute-start.26 = (bf16[128,1280]{1,0:T(8,128)(2,1)S(1)}, bf16[128,1280]{1,0:T(8,128)(2,1)S(1)}, u32[]{:S(2)}, u32[]{:S(2)}) collective-permute-start(bf16[128,1280]{1,0:T(8,128)(2,1)S(1)} %get-tuple-element.62), channel_id=1, source_target_pairs={{0,64},{1,193},{2,66},{3,195},{4,68},{5,197},{6,70},{7,199},{8,72}... | collective-permute-start | bytes 983048 | tf_op jit(solution)/shard_map/ppermute | solution.py:36
  98.6 6.6 %collective-permute-start.17 = (bf16[64,1280]{1,0:T(8,128)(2,1)S(1)}, bf16[64,1280]{1,0:T(8,128)(2,1)S(1)}, u32[]{:S(2)}, u32[]{:S(2)}) collective-permute-start(bf16[64,1280]{1,0:T(8,128)(2,1)S(1)} %get-tuple-element.52), channel_id=1, source_target_pairs={{0,6},{1,25},{2,0},{3,27},{4,2},{5,29},{6,4},{7,31},{8,14},{9,1},{... | collective-permute-start | bytes 491528 | tf_op jit(solution)/shard_map/ppermute | solution.py:36
  101.7 8.3 %collective-permute-start.18 = (bf16[64,1280]{1,0:T(8,128)(2,1)S(1)}, bf16[64,1280]{1,0:T(8,128)(2,1)S(1)}, u32[]{:S(2)}, u32[]{:S(2)}) collective-permute-start(bf16[64,1280]{1,0:T(8,128)(2,1)S(1)} %get-tuple-element.53), channel_id=1, source_target_pairs={{0,2},{1,9},{2,4},{3,11},{4,6},{5,13},{6,0},{7,15},{8,10},{9,17},{... | collective-permute-start | bytes 491528 | tf_op jit(solution)/shard_map/ppermute | solution.py:36
  101.7 8.3 %collective-permute-start.19 = (bf16[64,1280]{1,0:T(8,128)(2,1)S(1)}, bf16[64,1280]{1,0:T(8,128)(2,1)S(1)}, u32[]{:S(2)}, u32[]{:S(2)}) collective-permute-start(bf16[64,1280]{1,0:T(8,128)(2,1)S(1)} %get-tuple-element.54), channel_id=1, source_target_pairs={{0,4},{1,17},{2,6},{3,19},{4,0},{5,21},{6,2},{7,23},{8,12},{9,25},... | collective-permute-start | bytes 491528 | tf_op jit(solution)/shard_map/ppermute | solution.py:36
  105.1 5.6 %collective-permute-start.27 = (f32[64,1280]{1,0:T(8,128)S(1)}, f32[64,1280]{1,0:T(8,128)S(1)}, u32[]{:S(2)}, u32[]{:S(2)}) collective-permute-start(f32[64,1280]{1,0:T(8,128)S(1)} %get-tuple-element.65), channel_id=1, source_target_pairs={{0,1},{1,0},{2,3},{3,2},{4,5},{5,4},{6,7},{7,6},{8,9},{9,8},{10,11... | collective-permute-start | bytes 983048 | tf_op jit(solution)/shard_map/ppermute | solution.py:36
  (6 other events, 49.4 us)
